TPU v7x, 256 devices: a whole 4x4x8 slice. The times are simulated.
256 devices in a mesh: grp: 8 (over z), seq: 16 (over y_hi, x, core), tp: 2 (over y_lo).
Axes of the slice: x: 4, y: 4 (y_hi: 2, y_lo: 2; y = y_hi * 2 + y_lo), z: 8, core: 2. Of those that a mesh axis runs over, the one named last changes fastest.
Arguments:
- token_ids: int32 [8, 128], replicated, may hold values from 0 to 32127
- text_lengths: int32 [8], P('grp'), may hold values from 32 to 128, as said below
- embed_table: bfloat16 [32128, 4096], P(('seq', 'tp'), 'grp'), may hold values from -36 to 36
- ff_gain: float32 [4096], P('grp'), may hold values from 0.5 to 1.5
- wi_gate: bfloat16 [4096, 10240], P('grp', ('seq', 'tp')), may hold values from -0.09375 to 0.09375
- wi_up: bfloat16 [4096, 10240], P('grp', ('seq', 'tp')), may hold values from -0.09375 to 0.09375
- wo_down: bfloat16 [10240, 4096], P(('seq', 'tp')), may hold values from -0.0625 to 0.0625
- final_gain: float32 [4096], P(('seq', 'tp')), may hold values from 0.5 to 1.5
- cap_weight: bfloat16 [4096, 1152], P(('seq', 'tp')), may hold values from -0.09375 to 0.09375
- cap_bias: float32 [1152], replicated, may hold values from -8 to 8
- image: bfloat16 [8, 6144, 1152], P('grp', ('seq', 'tp')), may hold values from -6 to 6
- modulation: float32 [8, 3, 1152], P('grp'), may hold values from -2 to 7
- w_qkv: bfloat16 [1152, 3456], P(None, 'seq'), may hold values from -0.1875 to 0.1875
- w_out: bfloat16 [1152, 1152], P(('seq', 'tp')), may hold values from -0.1875 to 0.1875
- w_cq: bfloat16 [1152, 1152], P(('seq', 'tp')), may hold values from -0.1875 to 0.1875
- w_ckv: bfloat16 [1152, 2304], P(None, ('seq', 'tp')), may hold values from -0.1875 to 0.1875
- w_co: bfloat16 [1152, 1152], P(('seq', 'tp')), may hold values from -0.1875 to 0.1875
Outputs:
- result: bfloat16 [8, 6144, 1152], P('grp', ('seq', 'tp'))
Inputs may be any that keep to these rules, and one draw needn't show every extreme that they name: `text_lengths`: one prompt in every draw is unpadded.
All inputs are finite; a program needn't handle non-finite values.
Results may differ from a plain program's by a relative error of at most 0.014.
The roundings to bfloat16 on the way count: a program that leaves them out, or rounds other values in their place, can miss the bound.
Values may be sent and summed in bfloat16 or wider, within the bound.
No kernel may reach another device: no remote copies, remote signals or barrier semaphores. Data moves between devices by JAX's collectives and lax.ppermute only.
A program may use at most 128 MiB of HBM per device.

v0:
```python
import math

import jax
import jax.numpy as jnp
from jax import lax
from jax.experimental import pallas as pl
from jax.experimental.pallas import tpu as pltpu
from jax.sharding import Mesh
from jax.sharding import PartitionSpec as P

W = 1152
HEADS = 16
DT = 4096
HEAD = 72
SLOT = 80
LT = 128
EPSILON = 1e-06
PLANE = ("yhi", "x", "core", "tp")
SEQ = ("yhi", "x", "core")
SIDE = ("yhi", "core")
SCORE_SCALE = 1.0 / math.sqrt(HEAD)
EXP2_SCALE = SCORE_SCALE * math.log2(math.e)
LIFT = 64.0
F32 = jnp.float32
BF16 = jnp.bfloat16

VMEM = pl.BlockSpec(memory_space=pltpu.VMEM)
SMEM = pl.BlockSpec(memory_space=pltpu.SMEM)


def grant(mib):
    return pltpu.CompilerParams(vmem_limit_bytes=mib * 1024 * 1024)


def gelu_tanh(values):
    return jax.nn.gelu(values, approximate=True)


def exchange(blocks, axes):
    return lax.all_to_all(blocks, axes, 0, 0, tiled=True)


def shifted(value, axis, shift):
    size = lax.axis_size(axis)
    return lax.ppermute(value, axis, [(i, (i + shift) % size) for i in range(size)])


def crossed(value, axis, mask):
    size = lax.axis_size(axis)
    return lax.ppermute(value, axis, [(i, i ^ mask) for i in range(size)])


def nt_dot(a, b):
    return lax.dot_general(a, b, (((1,), (1,)), ((), ())), preferred_element_type=F32)


def thirds(values):
    high = values.astype(BF16).astype(F32)
    mid = (values - high).astype(BF16).astype(F32)
    return high, mid, values - high - mid


TICK = (8, 128)


def call(
    kernel,
    name,
    out_shape,
    args,
    scratch=(),
    in_specs=None,
    flops=0,
    moved=1 << 20,
    exps=0,
    after=(),
    tick=False,
    mib=16,
):
    outs = list(out_shape) if isinstance(out_shape, list) else [out_shape]
    many = tick or isinstance(out_shape, list)
    if tick:
        outs.append(shape(TICK, F32))
    first, waits = len(args), len(after)
    last = first + waits + len(outs)

    def body(*refs):
        if tick:
            refs[last - 1][...] = jnp.zeros(TICK, F32)
        kernel(*refs[:first], *refs[first + waits : last - tick], *refs[last:])

    return pl.pallas_call(
        body,
        out_shape=outs if many else outs[0],
        in_specs=(in_specs or [VMEM] * len(args)) + [VMEM] * waits,
        out_specs=[VMEM] * len(outs) if many else VMEM,
        scratch_shapes=list(scratch),
        compiler_params=grant(mib),
        cost_estimate=pl.CostEstimate(flops=flops, bytes_accessed=moved, transcendentals=exps),
        name=name,
    )(*args, *after)


def tie(*arrays):
    total = jnp.zeros(TICK, F32)
    for array in arrays:
        total = total + array[: TICK[0], : TICK[1]].astype(F32)
    return total


def shape(dims, dtype=BF16):
    return jax.ShapeDtypeStruct(dims, dtype)


def embed_kernel(in_ref, out_ref):
    total = in_ref[0].astype(F32)
    for j in range(1, in_ref.shape[0]):
        total += in_ref[j].astype(F32)
    total = total.astype(BF16)
    for j in range(out_ref.shape[0]):
        out_ref[j] = total


def row_of(column):
    return jnp.broadcast_to(column, (column.shape[0], 128)).T[:1]


def column_of(row):
    return jnp.broadcast_to(row, (128, row.shape[1])).T[:, :1]


def gate_up_kernel(at_ref, in_ref, gain_ref, gate_ref, up_ref, out_ref, weight, rows32):
    prompts, _, both = out_ref.shape
    plane, group, feats = in_ref.shape
    tokens = plane * group // prompts
    share = tokens // plane
    weight[...] = (
        jnp.concatenate([gate_ref[...].astype(F32), up_ref[...].astype(F32)], axis=0)
        .T.astype(BF16)
    )
    per = plane // prompts
    at = at_ref[3] * share
    base = pl.multiple_of(at // 8 * 8, 8)
    upper = lax.rem(at, 8) == 0
    for p in range(prompts):
        rows = in_ref[p * per : (p + 1) * per].reshape(tokens, feats).astype(F32)
        rows32[...] = rows
        scaled = (rows * gain_ref[...]).astype(BF16)
        out_ref[p, :tokens, :] = jnp.dot(
            scaled, weight[...], preferred_element_type=F32
        ).astype(BF16)
        near = rows32[pl.ds(base, 8), :]
        own = jnp.where(upper, near[:share], near[share:])
        square = row_of(jnp.sum(rows * rows, axis=-1, keepdims=True))
        squares = jnp.concatenate(list(thirds(square)) + [jnp.zeros_like(square)], axis=0)
        out_ref[p, tokens:, :] = jnp.concatenate(
            [
                jnp.concatenate([own, jnp.zeros((share, both - feats), F32)], axis=1),
                jnp.concatenate([squares, jnp.zeros((4, both - tokens), F32)], axis=1),
            ],
            axis=0,
        ).astype(BF16)


def down_kernel(in_ref, down_ref, out_ref):
    groups, rows, both = in_ref.shape
    plane, _, width = out_ref.shape
    tokens = 128
    share = tokens // plane
    units = down_ref.shape[0]
    feats = DT // groups
    total = in_ref[0, :tokens, :].astype(F32)
    square = None
    for g in range(groups):
        if g:
            total += in_ref[g, :tokens, :].astype(F32)
        extra = in_ref[g, tokens:, :].astype(F32)
        for i in range(3):
            part = extra[share + i : share + i + 1, :tokens]
            square = part if square is None else square + part
        for k in range(feats // width):
            piece = extra[:share, k * width : (k + 1) * width]
            out_ref[g * (feats // width) + k, tokens:, :] = jnp.concatenate(
                [piece, jnp.zeros_like(piece)], axis=0
            ).astype(BF16)
    inverse = column_of(lax.rsqrt(square / DT + EPSILON))
    total = total * inverse
    hidden = (gelu_tanh(total[:, :units]) * total[:, units:]).astype(BF16)
    step = 4
    for j in range(0, plane, step):
        part = jnp.dot(
            hidden, down_ref[:, j * width : (j + step) * width], preferred_element_type=F32
        ).astype(BF16)
        for k in range(step):
            out_ref[j + k, :tokens, :] = part[:, k * width : (k + 1) * width]


def cap_kernel(in_ref, gain_ref, weight_ref, out_ref, rest, wide):
    plane, share, _ = out_ref.shape
    tokens = plane * share
    total = in_ref[0, :tokens, :].astype(F32)
    for j in range(1, plane):
        total += in_ref[j, :tokens, :].astype(F32)
    for j in range(plane):
        rest[j * share : (j + 1) * share, :] = in_ref[j, tokens:, :].astype(F32)[:share]
    state = total + rest[...]
    high, mid, low = thirds(jnp.sum(state * state, axis=-1, keepdims=True))
    lane = lax.broadcasted_iota(jnp.int32, (tokens, wide.shape[1] - W), 1)
    wide[:, W:] = jnp.where(
        lane == 0, high, jnp.where(lane == 1, mid, jnp.where(lane == 2, low, 0.0))
    )
    gained = (state * gain_ref[...]).astype(BF16)
    wide[:, :W] = jnp.dot(gained, weight_ref[...], preferred_element_type=F32)
    for j in range(plane):
        out_ref[j] = wide[j * share : (j + 1) * share, :].astype(BF16)


def caption_kernel(in_ref, bias_ref, out_ref):
    total = in_ref[0].astype(F32)
    for j in range(1, in_ref.shape[0]):
        total += in_ref[j].astype(F32)
    square = total[:, W : W + 1] + total[:, W + 1 : W + 2] + total[:, W + 2 : W + 3]
    inverse = lax.rsqrt(square / DT + EPSILON)
    caption = gelu_tanh(total[:, :W] * inverse + bias_ref[...]).astype(BF16)
    for j in range(out_ref.shape[0]):
        out_ref[j] = caption


def kv_kernel(in_ref, weight_ref, out_ref, rows):
    plane, share, _ = in_ref.shape
    for j in range(plane):
        rows[j * share : (j + 1) * share, :] = in_ref[j].astype(F32)
    kv = nt_dot(weight_ref[...], rows[...].astype(BF16)).astype(BF16)
    for j in range(plane):
        out_ref[j] = kv


def modulate_kernel(image_ref, mod_ref, out_ref):
    pixels = image_ref[...].astype(F32)
    center = jnp.mean(pixels, axis=-1, keepdims=True)
    spread = jnp.mean((pixels - center) ** 2, axis=-1, keepdims=True)
    out_ref[...] = (
        (pixels - center) * lax.rsqrt(spread + EPSILON) * (1.0 + mod_ref[1:2]) + mod_ref[0:1]
    ).astype(BF16)


def side_kernel(*refs):
    out_ref = refs[-1]
    for k, ref in enumerate(refs[:-1]):
        out_ref[:, k * W : (k + 1) * W] = ref[...]


def pair_kernel(at_ref, own_ref, other_ref, out_ref):
    own, other = own_ref[...].astype(F32), other_ref[...].astype(F32)
    first = at_ref[2] == 0
    out_ref[...] = jnp.concatenate(
        [jnp.where(first, own, other), jnp.where(first, other, own)], axis=0
    ).astype(BF16)


def qkv_kernel(at_ref, *refs):
    tokens, weights = refs[:4], refs[4:8]
    fulls, pairs = refs[8:12], refs[12:16]
    x_rows = refs[16]
    rows = tokens[0].shape[0]
    for m, block in enumerate(tokens):
        at = lax.rem(at_ref[1] - m + 4, 4)
        x_rows[pl.ds(pl.multiple_of(at * rows, rows), rows), :] = block[...]
    span = x_rows.shape[0]
    zeros = jnp.zeros((SLOT - HEAD, span), F32)
    ones = (lax.broadcasted_iota(jnp.int32, zeros.shape, 0) == 0).astype(F32)
    for s in range(4):
        out = nt_dot(weights[s][...], x_rows[...])
        slots = [
            jnp.concatenate([out[i * HEAD : (i + 1) * HEAD], tail], axis=0).astype(BF16)
            for i, tail in enumerate((zeros, ones, zeros))
        ]
        for i in range(3):
            fulls[s][i * SLOT : (i + 1) * SLOT, :] = slots[i]
        for i in range(2):
            pairs[s][i * SLOT : (i + 1) * SLOT, :] = slots[i + 1]


ROWS = 192
TILE = 256


def attention_kernel(at_ref, *refs):
    fulls, others = refs[:4], refs[4:8]
    outs = refs[8:12]
    keys, vals, qry, terms_a, terms_b, found = refs[12:18]
    span = fulls[0].shape[1]
    count = 8 * span
    largest = None
    for c, (ref, first) in enumerate([(r, SLOT) for r in fulls] + [(r, 0) for r in others]):
        block = ref[first : first + SLOT, :]
        cols = slice(c * span, (c + 1) * span)
        keys[:SLOT, cols] = block
        keys[SLOT:, cols] = block
        vals[cols, :] = ref[first + SLOT : first + 2 * SLOT, :].astype(F32).T.astype(BF16)
        wide = block.astype(F32)
        row = lax.broadcasted_iota(jnp.int32, wide.shape, 0)
        norm = jnp.sum(jnp.where(row < HEAD, wide * wide, 0.0), axis=0, keepdims=True)
        largest = norm if largest is None else jnp.maximum(largest, norm)
    largest = jnp.max(largest, axis=-1, keepdims=True)
    for s in range(4):
        q = fulls[s][0:SLOT, :].astype(F32) * SCORE_SCALE
        high = q.astype(BF16).astype(F32)
        row = lax.broadcasted_iota(jnp.int32, q.shape, 0)
        bound = jnp.sqrt(jnp.sum(q * q, axis=0, keepdims=True) * largest) * (1.0 + 2.0**-6)
        high = jnp.where(row == HEAD, LIFT * math.log(2.0) - bound, high)
        low = jnp.where(row == HEAD, 0.0, q - high)
        both = jnp.concatenate([high, low], axis=0).T
        for a in range(4):
            away = lax.rem(a - at_ref[1] + 4, 4)
            qry[s * 4 + away] = both[a * ROWS : (a + 1) * ROWS].astype(BF16)

    def tile(t):
        return slice(t * TILE, (t + 1) * TILE)

    def fill(q, t, terms, total, shift=None):
        s = jnp.dot(q, keys[:, tile(t)], preferred_element_type=F32)
        e = jnp.exp(s if shift is None else s - shift)
        terms[:, tile(t)] = e
        return total + (e[:, :128] + e[:, 128:])

    def weigh(t, terms, inverse, acc):
        p = (terms[:, tile(t)] * inverse).astype(BF16)
        return acc + jnp.dot(p, vals[tile(t), :], preferred_element_type=F32)

    def put(i, acc):
        found[i] = acc.T[:HEAD].astype(BF16)

    tiles = count // TILE
    none = jnp.zeros((ROWS, 128), F32)
    empty = jnp.zeros((ROWS, SLOT), F32)

    def step(i, seen):
        one, two = qry[2 * i], qry[2 * i + 1]
        total_a, total_b, acc_a, acc_b = none, none, empty, empty
        for t in range(tiles):
            total_a = fill(one, t, terms_a, total_a)
        total_a = jnp.sum(total_a, axis=-1, keepdims=True)
        inverse = 1.0 / total_a
        for t in range(tiles):
            total_b = fill(two, t, terms_b, total_b)
            acc_a = weigh(t, terms_a, inverse, acc_a)
        put(2 * i, acc_a)
        total_b = jnp.sum(total_b, axis=-1, keepdims=True)
        inverse = 1.0 / total_b
        for t in range(tiles):
            acc_b = weigh(t, terms_b, inverse, acc_b)
        put(2 * i + 1, acc_b)
        least, most = seen
        return (
            jnp.minimum(least, jnp.min(jnp.minimum(total_a, total_b))),
            jnp.maximum(most, jnp.max(jnp.maximum(total_a, total_b))),
        )

    least, most = lax.fori_loop(0, 8, step, (jnp.float32(1.0), jnp.float32(1.0)))
    safe = jnp.logical_and(least > 2.0**-76, most < 2.0**100)

    @pl.when(jnp.logical_not(safe))
    def _():
        def again(i, _):
            q = qry[i].astype(F32)
            lane = lax.broadcasted_iota(jnp.int32, q.shape, 1)
            q = jnp.where(lane == HEAD, 0.0, q).astype(BF16)
            top = None
            for t in range(tiles):
                s = jnp.dot(q, keys[:, tile(t)], preferred_element_type=F32)
                here = jnp.max(s, axis=-1, keepdims=True)
                top = here if top is None else jnp.maximum(top, here)
            total = none
            for t in range(tiles):
                total = fill(q, t, terms_a, total, top)
            inverse = 1.0 / jnp.sum(total, axis=-1, keepdims=True)
            acc = empty
            for t in range(tiles):
                acc = weigh(t, terms_a, inverse, acc)
            put(i, acc)
            return 0

        lax.fori_loop(0, 16, again, 0)

    for s, out in enumerate(outs):
        out[...] = found[4 * s : 4 * s + 4]


def regroup_kernel(*refs):
    for m, out in enumerate(refs[4:]):
        for s, part in enumerate(refs[:4]):
            out[s] = part[m]


def project_kernel(at_ref, *refs):
    parts = refs[:4]
    wout_ref, wcq_ref, img_ref, gate_ref, after_ref, cq_ref, wide = refs[4:]
    for d, part in enumerate(parts):
        x = lax.rem(at_ref[1] - d + 4, 4)
        for m in range(4):
            side = lax.bitwise_xor(at_ref[0], m)
            head = (side // 2) * 8 + x * 2 + lax.rem(side, 2)
            wide[pl.ds(pl.multiple_of(head * HEAD, 8), HEAD), :] = part[m].astype(F32)
    projected = jnp.dot(wide[...].T.astype(BF16), wout_ref[...], preferred_element_type=F32)
    after = (img_ref[...].astype(F32) + gate_ref[...] * projected).astype(BF16)
    after_ref[...] = after
    cq_ref[...] = jnp.dot(after, wcq_ref[...], preferred_element_type=F32).astype(BF16)


def cross_kernel(len_ref, cq_ref, after_ref, kv_ref, wco_ref, out_ref, wide):
    length = len_ref[0]
    rows = cq_ref.shape[0]
    visible = lax.broadcasted_iota(jnp.int32, (rows, LT), 1) < length
    for h in range(HEADS):
        qry = cq_ref[:, h * HEAD : (h + 1) * HEAD]
        s = jnp.dot(qry, kv_ref[h], preferred_element_type=F32) * SCORE_SCALE
        s = jnp.where(visible, s, -1e30)
        e = jnp.exp(s - jnp.max(s, axis=-1, keepdims=True))
        p = (e / jnp.sum(e, axis=-1, keepdims=True)).astype(BF16)
        wide[h * HEAD : (h + 1) * HEAD, :] = nt_dot(kv_ref[HEADS + h], p)
    final = jnp.dot(wide[...].T.astype(BF16), wco_ref[...], preferred_element_type=F32)
    out_ref[...] = (after_ref[...].astype(F32) + final).astype(BF16)


def whole(dims):
    return pl.BlockSpec(dims, lambda i: (0,) * len(dims))


def third(k):
    return pl.BlockSpec((W, W), lambda i: (0, k))


def project(at, parts, side, img, gate):
    rows = img.shape[0]
    return pl.pallas_call(
        project_kernel,
        grid=(1,),
        out_shape=[shape((rows, W))] * 2,
        in_specs=[SMEM]
        + [whole(part.shape) for part in parts]
        + [third(0), third(1), whole(img.shape), whole(gate.shape)],
        out_specs=[whole((rows, W))] * 2,
        scratch_shapes=[pltpu.VMEM((W, rows), F32)],
        compiler_params=grant(56),
        cost_estimate=pl.CostEstimate(
            flops=4 * rows * W * W, bytes_accessed=8 << 20, transcendentals=0
        ),
        name="project_out_and_query",
    )(at, *parts, side, side, img, gate)


def cross(length, cq, after, kv, side):
    rows = cq.shape[0]
    return pl.pallas_call(
        cross_kernel,
        grid=(1,),
        out_shape=shape((rows, W)),
        in_specs=[SMEM, whole(cq.shape), whole(after.shape), whole(kv.shape), third(2)],
        out_specs=whole((rows, W)),
        scratch_shapes=[pltpu.VMEM((W, rows), F32)],
        compiler_params=grant(56),
        cost_estimate=pl.CostEstimate(
            flops=4 * rows * W * W, bytes_accessed=5 << 20, transcendentals=rows * LT * HEADS
        ),
        name="cross_attention",
    )(length, cq, after, kv, side)


def local(
    token_ids,
    text_lengths,
    embed_table,
    ff_gain,
    wi_gate,
    wi_up,
    wo_down,
    final_gain,
    cap_weight,
    cap_bias,
    image,
    modulation,
    w_qkv,
    w_out,
    w_cq,
    w_ckv,
    w_co,
):
    plane = lax.axis_size(PLANE)
    place = lax.axis_index(PLANE)
    prompts, tokens = token_ids.shape
    share = tokens // plane
    vocab_rows, feats = embed_table.shape
    units = wi_gate.shape[1]
    width = DT // plane

    local_ids = token_ids.reshape(-1) - place * vocab_rows
    one_hot = (local_ids[:, None] == jnp.arange(vocab_rows, dtype=jnp.int32)[None]).astype(BF16)
    picked = jnp.dot(one_hot, embed_table, preferred_element_type=F32).astype(BF16)
    picked = exchange(picked.reshape(plane, -1, feats), PLANE)

    pixels = image[0]
    rows = pixels.shape[0]
    modulate = modulation[0]
    modulated = call(modulate_kernel, "modulate", shape((rows, W)), (pixels, modulate))
    token_blocks = [modulated] + [shifted(modulated, "x", s) for s in range(1, 4)]
    weight_blocks = [w_qkv.T, crossed(w_qkv.T, "core", 1), crossed(w_qkv.T, "yhi", 1)]
    weight_blocks.append(crossed(weight_blocks[2], "core", 1))
    at = jnp.stack([lax.axis_index(a) for a in (SIDE, "x", "tp", PLANE)]).astype(jnp.int32)
    span = 4 * rows
    made = call(
        qkv_kernel,
        "query_key_value",
        [shape((3 * SLOT, span))] * 4 + [shape((2 * SLOT, span))] * 4,
        (at, *token_blocks, *weight_blocks),
        scratch=[pltpu.VMEM((span, W), BF16)],
        in_specs=[SMEM] + [VMEM] * 8,
        flops=2 * span * W * 12 * HEAD,
        moved=8 << 20,
        mib=56,
        tick=True,
    )
    fulls = [made[0]] + [crossed(made[m], SIDE, m) for m in range(1, 4)]
    others = [crossed(made[4 + m], SIDE + ("tp",), 2 * m + 1) for m in range(4)]

    embedded = call(
        embed_kernel,
        "embed_sum",
        shape(picked.shape),
        (picked,),
        after=(tie(*token_blocks[1:], *weight_blocks[1:]),),
    )
    gate_up, tick = call(
        gate_up_kernel,
        "text_gate_up",
        [shape((prompts, tokens + 2 * share, 2 * units))],
        (at, exchange(embedded, PLANE), ff_gain.reshape(1, feats), wi_gate.T, wi_up.T),
        scratch=[pltpu.VMEM((feats, 2 * units), BF16), pltpu.VMEM((tokens, feats), F32)],
        in_specs=[SMEM] + [VMEM] * 4,
        flops=4 * prompts * tokens * feats * units,
        moved=4 << 20,
        after=(tie(*fulls[1:], *others),),
        tick=True,
    )
    side = call(side_kernel, "side_weights", shape((w_out.shape[0], 3 * W)), (w_out, w_cq, w_co))
    pair = call(
        pair_kernel,
        "side_pair",
        shape((HEAD, 3 * W)),
        (at, side, crossed(side, "tp", 1)),
        in_specs=[SMEM, VMEM, VMEM],
        after=(tick,),
    )
    side = lax.all_gather(pair, SEQ, axis=0, tiled=True)
    *found, attended = call(
        attention_kernel,
        "self_attention",
        [shape((4, HEAD, rows))] * 4,
        (at, *fulls, *others),
        scratch=[
            pltpu.VMEM((2 * SLOT, 8 * span), BF16),
            pltpu.VMEM((8 * span, SLOT), BF16),
            pltpu.VMEM((16, ROWS, 2 * SLOT), BF16),
            pltpu.VMEM((ROWS, 8 * span), F32),
            pltpu.VMEM((ROWS, 8 * span), F32),
            pltpu.VMEM((16, HEAD, ROWS), BF16),
        ],
        in_specs=[SMEM] + [VMEM] * 8,
        flops=16 * span * 2 * span * 256 * 2,
        moved=8 << 20,
        exps=4 * span * 8 * span,
        after=(tick,),
        tick=True,
        mib=56,
    )
    found = [found[0]] + [crossed(found[m], SIDE, m) for m in range(1, 4)]
    down = call(
        down_kernel,
        "text_down",
        shape((plane, tokens + 2 * share, width)),
        (exchange(gate_up, "grp"), wo_down),
        flops=2 * tokens * DT * units,
        moved=5 << 20,
        exps=tokens * units,
        after=(attended,),
    )
    cap_part = call(
        cap_kernel,
        "caption_partial",
        shape((plane, share, W + 128)),
        (exchange(down, PLANE), final_gain.reshape(1, width), cap_weight),
        scratch=[pltpu.VMEM((tokens, width), F32), pltpu.VMEM((tokens, W + 128), F32)],
    )
    *grouped, tick = call(
        regroup_kernel, "regroup", [shape((4, HEAD, rows))] * 4, tuple(found), tick=True
    )
    caption = call(
        caption_kernel,
        "caption",
        shape((plane, share, W)),
        (exchange(cap_part, PLANE), cap_bias.reshape(1, W)),
        after=(tick,),
    )
    parts = [grouped[0]] + [shifted(grouped[d], "x", d) for d in range(1, 4)]
    after_self, cross_query = project(at, parts, side, pixels, modulate[2:3])
    kv_part = call(
        kv_kernel,
        "text_kv",
        shape((plane, w_ckv.shape[1], tokens)),
        (exchange(caption, PLANE), w_ckv.T),
        scratch=[pltpu.VMEM((tokens, W), F32)],
        after=(tie(*(part[0] for part in parts[1:])),),
    )
    text_kv = exchange(kv_part, PLANE)
    result = cross(text_lengths, cross_query, after_self, text_kv, side)
    return result[None]


def solution(mesh):
    grp, seq, tp = mesh.devices.shape
    fine = Mesh(mesh.devices.reshape(grp, 2, seq // 4, 2, tp), ("grp",) + PLANE)
    placed = (
        P(),
        P("grp"),
        P(PLANE, "grp"),
        P("grp"),
        P("grp", PLANE),
        P("grp", PLANE),
        P(PLANE, None),
        P(PLANE),
        P(PLANE, None),
        P(),
        P("grp", PLANE, None),
        P("grp", None, None),
        P(None, SEQ),
        P(PLANE, None),
        P(PLANE, None),
        P(None, PLANE),
        P(PLANE, None),
    )
    return jax.shard_map(
        local, mesh=fine, in_specs=placed, out_specs=P("grp", PLANE, None), check_vma=False
    )
```

profile of v0, /device:TPU:32, one launch (start us, length us, event | category | flops | bytes accessed | tf_op | source)
XLA Modules:
  0.0 297.2 jit_solution(2291330243744657140)
XLA Ops:
  6.5 3.2 %collective-permute-start.4 = (bf16[216,1152]{1,0:T(8,128)(2,1)}, bf16[216,1152]{1,0:T(8,128)(2,1)}, u32[]{:S(2)}, u32[]{:S(2)}) collective-permute-start(bf16[216,1152]{1,0:T(8,128)(2,1)} %bitcast.5.refs_5_), channel_id=1, source_target_pairs={{0,16},{16,0},{1,17},{17,1},{2,18},{18,2},{3,19},{19,3},{4,20},{20... | collective-permute-start | bytes 1493000 | tf_op jit(solution)/shard_map/ppermute | solution.py:50
  10.4 2.3 fusion.2
  12.7 5.3 %all-to-all-start = ((bf16[32,32,512]{2,1,0:T(8,128)(2,1)}), bf16[32,32,512]{2,1,0:T(8,128)(2,1)S(1)}, u32[]{:S(2)}, u32[]{:S(2)}) async-start(bf16[32,32,512]{2,1,0:T(8,128)(2,1)} %bitcast.35), calls=%async_computation | async-start | bytes 2097152 | tf_op jit(solution)/shard_map/all_to_all | solution.py:40
  18.4 6.1 %collective-permute-done.4.refs_7_ = bf16[216,1152]{1,0:T(8,128)(2,1)} collective-permute-done((bf16[216,1152]{1,0:T(8,128)(2,1)}, bf16[216,1152]{1,0:T(8,128)(2,1)}, u32[]{:S(2)}, u32[]{:S(2)}) %collective-permute-start.4) | collective-permute-done | bytes 497696 | tf_op jit(solution)/shard_map/ppermute | solution.py:50
  24.9 2.6 collective-permute-start
  27.5 7.3 %collective-permute-start.1 = (bf16[192,1152]{1,0:T(8,128)(2,1)S(1)}, bf16[192,1152]{1,0:T(8,128)(2,1)S(1)}, u32[]{:S(2)}, u32[]{:S(2)}) collective-permute-start(bf16[192,1152]{1,0:T(8,128)(2,1)S(1)} %modulate.1.refs_1_), channel_id=1, source_target_pairs={{0,8},{4,12},{8,0},{12,4},{1,9},{5,13},{9,1},{13,5},{2,10},{6,14},... | collective-permute-start | bytes 1327112 | tf_op jit(solution)/shard_map/ppermute | solution.py:45
  34.8 1.3 collective-permute-start.2
  36.1 8.1 %collective-permute-done.refs_2_ = bf16[192,1152]{1,0:T(8,128)(2,1)S(1)} collective-permute-done((bf16[192,1152]{1,0:T(8,128)(2,1)S(1)}, bf16[192,1152]{1,0:T(8,128)(2,1)S(1)}, u32[]{:S(2)}, u32[]{:S(2)}) %collective-permute-start) | collective-permute-done | bytes 442400 | tf_op jit(solution)/shard_map/ppermute | solution.py:45
  44.2 10.7 %collective-permute-done.1.refs_3_ = bf16[192,1152]{1,0:T(8,128)(2,1)S(1)} collective-permute-done((bf16[192,1152]{1,0:T(8,128)(2,1)S(1)}, bf16[192,1152]{1,0:T(8,128)(2,1)S(1)}, u32[]{:S(2)}, u32[]{:S(2)}) %collective-permute-start.1) | collective-permute-done | bytes 442400 | tf_op jit(solution)/shard_map/ppermute | solution.py:45
  57.4 1.2 embed_sum.1
  58.7 7.8 %all-to-all-start.1 = ((bf16[32,32,512]{2,1,0:T(8,128)(2,1)}), bf16[32,32,512]{2,1,0:T(8,128)(2,1)S(1)}, u32[]{:S(2)}, u32[]{:S(2)}) async-start(bf16[32,32,512]{2,1,0:T(8,128)(2,1)} %embed_sum.1), calls=%async_computation.1 | async-start | bytes 2097152 | tf_op jit(solution)/shard_map/all_to_all | solution.py:40
  67.2 5.9 %query_key_value.1 = (bf16[240,768]{1,0:T(8,128)(2,1)}, bf16[240,768]{1,0:T(8,128)(2,1)}, bf16[240,768]{1,0:T(8,128)(2,1)}, bf16[240,768]{1,0:T(8,128)(2,1)}, bf...) custom-call(s32[4]{0:T(128)} %pad_add_fusion.refs_0_.at_ref, ...), custom_call_target="tpu_custom_call" | custom-call | flops 1528823808 | bytes 8388608 | tf_op jit(solution)/shard_map/query_key_value/pallas_call | solution.py:92
  73.1 1.5 collective-permute-start.10
  74.6 2.1 collective-permute-start.11
  77.7 2.4 collective-permute-start.8
  80.1 5.3 %collective-permute-done.10.refs_6_ = bf16[160,768]{1,0:T(8,128)(2,1)S(1)} collective-permute-done((bf16[160,768]{1,0:T(8,128)(2,1)}, bf16[160,768]{1,0:T(8,128)(2,1)S(1)}, u32[]{:S(2)}, u32[]{:S(2)}) %collective-permute-start.10) | collective-permute-done | bytes 245792 | tf_op jit(solution)/shard_map/ppermute | solution.py:50
  85.4 2.7 collective-permute-start.12
  88.1 13.3 %collective-permute-done.11.refs_7_ = bf16[160,768]{1,0:T(8,128)(2,1)S(1)} collective-permute-done((bf16[160,768]{1,0:T(8,128)(2,1)}, bf16[160,768]{1,0:T(8,128)(2,1)S(1)}, u32[]{:S(2)}, u32[]{:S(2)}) %collective-permute-start.11) | collective-permute-done | bytes 245792 | tf_op jit(solution)/shard_map/ppermute | solution.py:50
  101.4 3.1 %collective-permute-start.9 = (bf16[160,768]{1,0:T(8,128)(2,1)}, bf16[160,768]{1,0:T(8,128)(2,1)S(1)}, u32[]{:S(2)}, u32[]{:S(2)}) collective-permute-start(bf16[160,768]{1,0:T(8,128)(2,1)} %get-tuple-element.31), channel_id=1, source_target_pairs={{0,1},{1,0},{2,3},{3,2},{16,17},{17,16},{18,19},{19,18},{4,5},{5,4... | collective-permute-start | bytes 737288 | tf_op jit(solution)/shard_map/ppermute | solution.py:50
  104.5 4.2 %collective-permute-done.12.refs_8_ = bf16[160,768]{1,0:T(8,128)(2,1)S(1)} collective-permute-done((bf16[160,768]{1,0:T(8,128)(2,1)}, bf16[160,768]{1,0:T(8,128)(2,1)S(1)}, u32[]{:S(2)}, u32[]{:S(2)}) %collective-permute-start.12) | collective-permute-done | bytes 245792 | tf_op jit(solution)/shard_map/ppermute | solution.py:50
  108.7 1.0 collective-permute-start.19
  109.8 1.2 collective-permute-done.9.refs_5_
  112.7 1.8 text_gate_up.1
  114.4 1.1 copy-done.3
  115.5 1.9 collective-permute-done.19.refs_2_
  117.4 1.5 side_pair.1
  118.9 8.6 %all-to-all-start.2 = ((bf16[8,136,640]{2,1,0:T(8,128)(2,1)}), bf16[8,136,640]{2,1,0:T(8,128)(2,1)S(1)}, u32[]{:S(2)}, u32[]{:S(2)}) async-start(bf16[8,136,640]{2,1,0:T(8,128)(2,1)} %copy-done.3), calls=%async_computation.2 | async-start | bytes 2785280 | tf_op jit(solution)/shard_map/all_to_all | solution.py:40
  127.5 69.2 %self_attention.1 = (bf16[4,72,192]{2,1,0:T(8,128)(2,1)}, bf16[4,72,192]{2,1,0:T(8,128)(2,1)}, bf16[4,72,192]{2,1,0:T(8,128)(2,1)}, bf16[4,72,192]{2,1,0:T(8,128)(2,1)}, f32[8,128]{1,0:T(8,128)}) custom-call(s32[4]{0:T(128)} %pad_add_fusion.refs_0_.at_ref, bf16[240,768]{1,0:T(8,128)(2,1)} %get-tuple-element.27.refs_1_, bf16[240,768]{1,0:T(8,128)(2,1)} %copy-done.29, ...), custom_call_target="tpu_custom_call" | custom-call | flops 9663676416 | bytes 8388608 | tf_op jit(solution)/shard_map/self_attention/pallas_call | solution.py:92
  196.7 1.7 copy-done.1
  199.1 2.0 text_down.1
  201.2 5.0 %all-to-all-start.3 = ((bf16[32,136,128]{2,1,0:T(8,128)(2,1)}), bf16[32,136,128]{2,1,0:T(8,128)(2,1)S(1)}, u32[]{:S(2)}, u32[]{:S(2)}) async-start(bf16[32,136,128]{2,1,0:T(8,128)(2,1)} %text_down.1), calls=%async_computation.3 | async-start | bytes 2228224 | tf_op jit(solution)/shard_map/all_to_all | solution.py:40
  206.5 3.2 %collective-permute-start.14 = (bf16[4,72,192]{2,1,0:T(8,128)(2,1)S(1)}, bf16[4,72,192]{2,1,0:T(8,128)(2,1)S(1)}, u32[]{:S(2)}, u32[]{:S(2)}) collective-permute-start(bf16[4,72,192]{2,1,0:T(8,128)(2,1)S(1)} %copy-done.38), channel_id=1, source_target_pairs={{0,16},{2,18},{16,0},{18,2},{1,17},{3,19},{17,1},{19,3},{4,20},{6,... | collective-permute-start | bytes 331784 | tf_op jit(solution)/shard_map/ppermute | solution.py:50
  210.0 16.4 %collective-permute-done.14.refs_2_ = bf16[4,72,192]{2,1,0:T(8,128)(2,1)S(1)} collective-permute-done((bf16[4,72,192]{2,1,0:T(8,128)(2,1)S(1)}, bf16[4,72,192]{2,1,0:T(8,128)(2,1)S(1)}, u32[]{:S(2)}, u32[]{:S(2)}) %collective-permute-start.14) | collective-permute-done | bytes 110624 | tf_op jit(solution)/shard_map/ppermute | solution.py:50
  226.4 2.2 collective-permute-done.15.refs_3_
  229.3 3.1 %collective-permute-start.18 = (bf16[4,72,192]{2,1,0:T(8,128)(2,1)S(1)}, bf16[4,72,192]{2,1,0:T(8,128)(2,1)S(1)}, u32[]{:S(2)}, u32[]{:S(2)}) collective-permute-start(bf16[4,72,192]{2,1,0:T(8,128)(2,1)S(1)} %get-tuple-element.43), channel_id=1, source_target_pairs={{0,12},{4,0},{8,4},{12,8},{1,13},{5,1},{9,5},{13,9},{2,14},{6,2},{... | collective-permute-start | bytes 331784 | tf_op jit(solution)/shard_map/ppermute | solution.py:45
  232.7 1.0 collective-permute-start.16
  233.7 1.1 caption_partial.1
  234.8 4.7 %all-to-all-start.4 = ((bf16[32,4,1280]{2,1,0:T(4,128)(2,1)}), bf16[32,4,1280]{2,1,0:T(4,128)(2,1)S(1)}, u32[]{:S(2)}, u32[]{:S(2)}) async-start(bf16[32,4,1280]{2,1,0:T(4,128)(2,1)} %caption_partial.1), calls=%async_computation.4 | async-start | bytes 655360 | tf_op jit(solution)/shard_map/all_to_all | solution.py:40
  239.5 1.1 collective-permute-done.17.refs_2_
  240.6 9.1 %all-to-all-done.4.refs_0_ = bf16[32,4,1280]{2,1,0:T(4,128)(2,1)S(1)} async-done(((bf16[32,4,1280]{2,1,0:T(4,128)(2,1)}), bf16[32,4,1280]{2,1,0:T(4,128)(2,1)S(1)}, u32[]{:S(2)}, u32[]{:S(2)}) %all-to-all-start.4) | async-done | bytes 327712 | tf_op jit(solution)/shard_map/all_to_all | solution.py:40
  249.7 0.9 caption.1
  250.7 3.9 %all-to-all-start.5 = ((bf16[32,4,1152]{2,1,0:T(4,128)(2,1)}), bf16[32,4,1152]{2,1,0:T(4,128)(2,1)S(1)}, u32[]{:S(2)}, u32[]{:S(2)}) async-start(bf16[32,4,1152]{2,1,0:T(4,128)(2,1)} %caption.1), calls=%async_computation.5 | async-start | bytes 589824 | tf_op jit(solution)/shard_map/all_to_all | solution.py:40
  254.6 9.8 %all-to-all-done.5.refs_0_ = bf16[32,4,1152]{2,1,0:T(4,128)(2,1)S(1)} async-done(((bf16[32,4,1152]{2,1,0:T(4,128)(2,1)}), bf16[32,4,1152]{2,1,0:T(4,128)(2,1)S(1)}, u32[]{:S(2)}, u32[]{:S(2)}) %all-to-all-start.5) | async-done | bytes 294944 | tf_op jit(solution)/shard_map/all_to_all | solution.py:40
  264.5 1.1 text_kv.1
  265.6 3.9 %all-to-all-start.6 = ((bf16[32,72,128]{2,1,0:T(8,128)(2,1)}), bf16[32,72,128]{2,1,0:T(8,128)(2,1)S(1)}, u32[]{:S(2)}, u32[]{:S(2)}) async-start(bf16[32,72,128]{2,1,0:T(8,128)(2,1)} %text_kv.1), calls=%async_computation.6 | async-start | bytes 1179648 | tf_op jit(solution)/shard_map/all_to_all | solution.py:40
  270.8 5.2 %project_out_and_query.1 = (bf16[192,1152]{1,0:T(8,128)(2,1)}, bf16[192,1152]{1,0:T(8,128)(2,1)}) custom-call(s32[4]{0:T(128)} %pad_add_fusion.refs_0_.at_ref, bf16[4,72,192]{2,1,0:T(8,128)(2,1)} %copy-done.8, bf16[4,72,192]{2,1,0:T(8,128)(2,1)} %copy-done.22, bf16[4,72,192]{2,1,0:T(8,128)(2,1)} %copy-done.21, bf16[4,72,192]{2,1,0:T(8,128)(2,1)} %copy-done.20, ...), custom_call_target="tpu_custom_call" | custom-call | flops 1019215872 | bytes 8388608 | tf_op jit(solution)/shard_map/project_out_and_query/pallas_call | solution.py:436
  276.0 6.5 %all-to-all-done.6.kv_ref = bf16[32,72,128]{2,1,0:T(8,128)(2,1)S(1)} async-done(((bf16[32,72,128]{2,1,0:T(8,128)(2,1)}), bf16[32,72,128]{2,1,0:T(8,128)(2,1)S(1)}, u32[]{:S(2)}, u32[]{:S(2)}) %all-to-all-start.6) | async-done | bytes 589856 | tf_op jit(solution)/shard_map/all_to_all | solution.py:40
  283.3 7.0 %cross_attention.1 = bf16[192,1152]{1,0:T(8,128)(2,1)} custom-call(s32[1]{0:T(128)S(6)} %copy.21.len_ref, bf16[192,1152]{1,0:T(8,128)(2,1)} %get-tuple-element.44.cq_ref, bf16[192,1152]{1,0:T(8,128)(2,1)} %get-tuple-element.45.after_ref, bf16[32,72,128]{2,1,0:T(8,128)(2,1)} %copy-done.19, bf16[1152,3456]{1,0:T(8,128)(2,1)} %all-gather.2.cloned.1.call-done.refs_4_.refs_5_.wco_ref), custom_call_target="tpu_custom_call" | custom-call | flops 1019215872 | bytes 5242880 | tf_op jit(solution)/shard_map/cross_attention/pallas_call | solution.py:455
  (115 shorter events, 11.2 us)
Async XLA Ops:
  6.5 18.0 %collective-permute-start.4 = (bf16[216,1152]{1,0:T(8,128)(2,1)}, bf16[216,1152]{1,0:T(8,128)(2,1)}, u32[]{:S(2)}, u32[]{:S(2)}) collective-permute-start(bf16[216,1152]{1,0:T(8,128)(2,1)} %bitcast.5.refs_5_), channel_id=1, source_target_pairs={{0,16},{16,0},{1,17},{17,1},{2,18},{18,2},{3,19},{19,3},{4,20},{20... | collective-permute-start | bytes 1493000 | tf_op jit(solution)/shard_map/ppermute | solution.py:50
  12.7 11.8 %copy-start.23 = (f32[1,3,1152]{2,0,1:T(1,128)S(1)}, f32[1,3,1152]{2,0,1:T(1,128)}, u32[]{:S(2)}) copy-start(f32[1,3,1152]{2,0,1:T(1,128)} %param.28) | copy-start | bytes 41476
  12.7 11.8 %copy-start.2 = (bf16[1,192,1152]{2,1,0:T(8,128)(2,1)S(1)}, bf16[1,192,1152]{2,1,0:T(8,128)(2,1)}, u32[]{:S(2)}) copy-start(bf16[1,192,1152]{2,1,0:T(8,128)(2,1)} %param.27) | copy-start | bytes 1327108
  12.7 44.7 %all-to-all-start = ((bf16[32,32,512]{2,1,0:T(8,128)(2,1)}), bf16[32,32,512]{2,1,0:T(8,128)(2,1)S(1)}, u32[]{:S(2)}, u32[]{:S(2)}) async-start(bf16[32,32,512]{2,1,0:T(8,128)(2,1)} %bitcast.35), calls=%async_computation | async-start | bytes 2097152 | tf_op jit(solution)/shard_map/all_to_all | solution.py:40
  18.0 36.8 %collective-permute-start.3 = (bf16[216,1152]{1,0:T(8,128)(2,1)}, bf16[216,1152]{1,0:T(8,128)(2,1)S(1)}, u32[]{:S(2)}, u32[]{:S(2)}) collective-permute-start(bf16[216,1152]{1,0:T(8,128)(2,1)} %bitcast.5.refs_5_), channel_id=1, source_target_pairs={{0,2},{2,0},{1,3},{3,1},{4,6},{6,4},{5,7},{7,5},{8,10},{10,8},{9,1... | collective-permute-start | bytes 1493000 | tf_op jit(solution)/shard_map/ppermute | solution.py:50
  24.5 30.4 %collective-permute-start.5 = (bf16[216,1152]{1,0:T(8,128)(2,1)}, bf16[216,1152]{1,0:T(8,128)(2,1)S(1)}, u32[]{:S(2)}, u32[]{:S(2)}) collective-permute-start(bf16[216,1152]{1,0:T(8,128)(2,1)} %collective-permute-done.4.refs_7_), channel_id=1, source_target_pairs={{0,2},{2,0},{1,3},{3,1},{4,6},{6,4},{5,7},{7,5},{8,10},{10,8},{9,1... | collective-permute-start | bytes 1493000 | tf_op jit(solution)/shard_map/ppermute | solution.py:50
  24.9 33.8 %copy-start.4 = (bf16[192,1152]{1,0:T(8,128)(2,1)}, bf16[192,1152]{1,0:T(8,128)(2,1)S(1)}, u32[]{:S(2)}) copy-start(bf16[192,1152]{1,0:T(8,128)(2,1)S(1)} %modulate.1.refs_1_) | copy-start | bytes 1327108
  24.9 19.3 %collective-permute-start = (bf16[192,1152]{1,0:T(8,128)(2,1)S(1)}, bf16[192,1152]{1,0:T(8,128)(2,1)S(1)}, u32[]{:S(2)}, u32[]{:S(2)}) collective-permute-start(bf16[192,1152]{1,0:T(8,128)(2,1)S(1)} %modulate.1.refs_1_), channel_id=1, source_target_pairs={{0,4},{4,8},{8,12},{12,0},{1,5},{5,9},{9,13},{13,1},{2,6},{6,10},{... | collective-permute-start | bytes 1327112 | tf_op jit(solution)/shard_map/ppermute | solution.py:45
  27.5 27.3 %collective-permute-start.1 = (bf16[192,1152]{1,0:T(8,128)(2,1)S(1)}, bf16[192,1152]{1,0:T(8,128)(2,1)S(1)}, u32[]{:S(2)}, u32[]{:S(2)}) collective-permute-start(bf16[192,1152]{1,0:T(8,128)(2,1)S(1)} %modulate.1.refs_1_), channel_id=1, source_target_pairs={{0,8},{4,12},{8,0},{12,4},{1,9},{5,13},{9,1},{13,5},{2,10},{6,14},... | collective-permute-start | bytes 1327112 | tf_op jit(solution)/shard_map/ppermute | solution.py:45
  34.8 20.0 %collective-permute-start.2 = (bf16[192,1152]{1,0:T(8,128)(2,1)S(1)}, bf16[192,1152]{1,0:T(8,128)(2,1)S(1)}, u32[]{:S(2)}, u32[]{:S(2)}) collective-permute-start(bf16[192,1152]{1,0:T(8,128)(2,1)S(1)} %modulate.1.refs_1_), channel_id=1, source_target_pairs={{0,12},{4,0},{8,4},{12,8},{1,13},{5,1},{9,5},{13,9},{2,14},{6,2},{... | collective-permute-start | bytes 1327112 | tf_op jit(solution)/shard_map/ppermute | solution.py:45
  44.2 14.5 %copy-start.32 = (bf16[192,1152]{1,0:T(8,128)(2,1)}, bf16[192,1152]{1,0:T(8,128)(2,1)S(1)}, u32[]{:S(2)}) copy-start(bf16[192,1152]{1,0:T(8,128)(2,1)S(1)} %collective-permute-done.refs_2_) | copy-start | bytes 1327108
  58.7 54.0 %all-to-all-start.1 = ((bf16[32,32,512]{2,1,0:T(8,128)(2,1)}), bf16[32,32,512]{2,1,0:T(8,128)(2,1)S(1)}, u32[]{:S(2)}, u32[]{:S(2)}) async-start(bf16[32,32,512]{2,1,0:T(8,128)(2,1)} %embed_sum.1), calls=%async_computation.1 | async-start | bytes 2097152 | tf_op jit(solution)/shard_map/all_to_all | solution.py:40
  66.5 204.3 %all-gather.2.cloned.1.call-start = ((), (), s32[]{:S(2)}) async-start(), calls=%async_computation.7 | async-start | bytes 8460288 | tf_op jit(solution)/shard_map/all_gather | solution.py:554
  67.2 37.3 %copy-start.9 = (bf16[36,1152]{1,0:T(8,128)(2,1)S(1)}, bf16[36,1152]{1,0:T(8,128)(2,1)}, u32[]{:S(2)}) copy-start(bf16[36,1152]{1,0:T(8,128)(2,1)} %refs_0_.1) | copy-start | bytes 248836
  67.2 37.3 %copy-start.10 = (bf16[36,1152]{1,0:T(8,128)(2,1)S(1)}, bf16[36,1152]{1,0:T(8,128)(2,1)}, u32[]{:S(2)}) copy-start(bf16[36,1152]{1,0:T(8,128)(2,1)} %refs_1_.2) | copy-start | bytes 248836
  67.2 37.3 %copy-start.11 = (bf16[36,1152]{1,0:T(8,128)(2,1)S(1)}, bf16[36,1152]{1,0:T(8,128)(2,1)}, u32[]{:S(2)}) copy-start(bf16[36,1152]{1,0:T(8,128)(2,1)} %refs_2_.2) | copy-start | bytes 248836
  67.2 45.4 %copy-start.12 = (s32[4]{0:T(128)S(1)}, s32[4]{0:T(128)}, u32[]{:S(2)}) copy-start(s32[4]{0:T(128)} %pad_add_fusion.refs_0_.at_ref) | copy-start | bytes 52
  67.2 45.4 %copy-start.16 = (bf16[512,320]{0,1:T(8,128)(2,1)S(1)}, bf16[512,320]{0,1:T(8,128)(2,1)}, u32[]{:S(2)}) copy-start(bf16[512,320]{0,1:T(8,128)(2,1)} %param.21) | copy-start | bytes 983044
  67.2 45.4 %copy-start.17 = (bf16[512,320]{0,1:T(8,128)(2,1)S(1)}, bf16[512,320]{0,1:T(8,128)(2,1)}, u32[]{:S(2)}) copy-start(bf16[512,320]{0,1:T(8,128)(2,1)} %param.22) | copy-start | bytes 983044
  67.2 45.4 %copy-start.18 = (f32[512]{0:T(512)S(1)}, f32[512]{0:T(512)}, u32[]{:S(2)}) copy-start(f32[512]{0:T(512)} %param.20) | copy-start | bytes 6148
  73.1 12.3 %collective-permute-start.10 = (bf16[160,768]{1,0:T(8,128)(2,1)}, bf16[160,768]{1,0:T(8,128)(2,1)S(1)}, u32[]{:S(2)}, u32[]{:S(2)}) collective-permute-start(bf16[160,768]{1,0:T(8,128)(2,1)} %get-tuple-element.32), channel_id=1, source_target_pairs={{0,3},{1,2},{2,1},{3,0},{16,19},{17,18},{18,17},{19,16},{4,7},{5,6... | collective-permute-start | bytes 737288 | tf_op jit(solution)/shard_map/ppermute | solution.py:50
  74.6 26.7 %collective-permute-start.11 = (bf16[160,768]{1,0:T(8,128)(2,1)}, bf16[160,768]{1,0:T(8,128)(2,1)S(1)}, u32[]{:S(2)}, u32[]{:S(2)}) collective-permute-start(bf16[160,768]{1,0:T(8,128)(2,1)} %get-tuple-element.33), channel_id=1, source_target_pairs={{0,17},{1,16},{2,19},{3,18},{16,1},{17,0},{18,3},{19,2},{4,21},{5,... | collective-permute-start | bytes 737288 | tf_op jit(solution)/shard_map/ppermute | solution.py:50
  76.7 34.2 %collective-permute-start.6 = (bf16[240,768]{1,0:T(8,128)(2,1)}, bf16[240,768]{1,0:T(8,128)(2,1)S(1)}, u32[]{:S(2)}, u32[]{:S(2)}) collective-permute-start(bf16[240,768]{1,0:T(8,128)(2,1)} %get-tuple-element.28), channel_id=1, source_target_pairs={{0,2},{2,0},{16,18},{18,16},{1,3},{3,1},{17,19},{19,17},{4,6},{6,4... | collective-permute-start | bytes 1105928 | tf_op jit(solution)/shard_map/ppermute | solution.py:50
  76.8 34.1 %collective-permute-start.7 = (bf16[240,768]{1,0:T(8,128)(2,1)}, bf16[240,768]{1,0:T(8,128)(2,1)S(1)}, u32[]{:S(2)}, u32[]{:S(2)}) collective-permute-start(bf16[240,768]{1,0:T(8,128)(2,1)} %get-tuple-element.29), channel_id=1, source_target_pairs={{0,16},{2,18},{16,0},{18,2},{1,17},{3,19},{17,1},{19,3},{4,20},{6,... | collective-permute-start | bytes 1105928 | tf_op jit(solution)/shard_map/ppermute | solution.py:50
  77.7 33.3 %collective-permute-start.8 = (bf16[240,768]{1,0:T(8,128)(2,1)}, bf16[240,768]{1,0:T(8,128)(2,1)S(1)}, u32[]{:S(2)}, u32[]{:S(2)}) collective-permute-start(bf16[240,768]{1,0:T(8,128)(2,1)} %get-tuple-element.30), channel_id=1, source_target_pairs={{0,18},{2,16},{16,2},{18,0},{1,19},{3,17},{17,3},{19,1},{4,22},{6,... | collective-permute-start | bytes 1105928 | tf_op jit(solution)/shard_map/ppermute | solution.py:50
  85.4 25.6 %copy-start.25 = (bf16[160,768]{1,0:T(8,128)(2,1)}, bf16[160,768]{1,0:T(8,128)(2,1)S(1)}, u32[]{:S(2)}) copy-start(bf16[160,768]{1,0:T(8,128)(2,1)S(1)} %collective-permute-done.10.refs_6_) | copy-start | bytes 737284
  85.4 23.4 %collective-permute-start.12 = (bf16[160,768]{1,0:T(8,128)(2,1)}, bf16[160,768]{1,0:T(8,128)(2,1)S(1)}, u32[]{:S(2)}, u32[]{:S(2)}) collective-permute-start(bf16[160,768]{1,0:T(8,128)(2,1)} %get-tuple-element.34), channel_id=1, source_target_pairs={{0,19},{1,18},{2,17},{3,16},{16,3},{17,2},{18,1},{19,0},{4,23},{5,... | collective-permute-start | bytes 737288 | tf_op jit(solution)/shard_map/ppermute | solution.py:50
  101.4 9.5 %collective-permute-start.9 = (bf16[160,768]{1,0:T(8,128)(2,1)}, bf16[160,768]{1,0:T(8,128)(2,1)S(1)}, u32[]{:S(2)}, u32[]{:S(2)}) collective-permute-start(bf16[160,768]{1,0:T(8,128)(2,1)} %get-tuple-element.31), channel_id=1, source_target_pairs={{0,1},{1,0},{2,3},{3,2},{16,17},{17,16},{18,19},{19,18},{4,5},{5,4... | collective-permute-start | bytes 737288 | tf_op jit(solution)/shard_map/ppermute | solution.py:50
  108.7 8.6 %collective-permute-start.19 = (bf16[36,3456]{1,0:T(8,128)(2,1)S(1)}, bf16[36,3456]{1,0:T(8,128)(2,1)S(1)}, u32[]{:S(2)}, u32[]{:S(2)}) collective-permute-start(bf16[36,3456]{1,0:T(8,128)(2,1)S(1)} %side_weights.1.refs_1_), channel_id=1, source_target_pairs={{0,1},{1,0},{2,3},{3,2},{4,5},{5,4},{6,7},{7,6},{8,9},{9,8},{10,11... | collective-permute-start | bytes 746504 | tf_op jit(solution)/shard_map/ppermute | solution.py:50
  118.9 77.8 %all-to-all-start.2 = ((bf16[8,136,640]{2,1,0:T(8,128)(2,1)}), bf16[8,136,640]{2,1,0:T(8,128)(2,1)S(1)}, u32[]{:S(2)}, u32[]{:S(2)}) async-start(bf16[8,136,640]{2,1,0:T(8,128)(2,1)} %copy-done.3), calls=%async_computation.2 | async-start | bytes 2785280 | tf_op jit(solution)/shard_map/all_to_all | solution.py:40
  201.1 27.5 %copy-start.7 = (bf16[4,72,192]{2,1,0:T(8,128)(2,1)S(1)}, bf16[4,72,192]{2,1,0:T(8,128)(2,1)}, u32[]{:S(2)}) copy-start(bf16[4,72,192]{2,1,0:T(8,128)(2,1)} %get-tuple-element.36.refs_0_) | copy-start | bytes 331780
  201.1 31.3 %copy-start.24 = (f32[1152]{0:T(1024)S(1)}, f32[1152]{0:T(1024)}, u32[]{:S(2)}) copy-start(f32[1152]{0:T(1024)} %param.26) | copy-start | bytes 13828
  201.1 32.6 %copy-start.5 = (bf16[128,1152]{1,0:T(8,128)(2,1)S(1)}, bf16[128,1152]{1,0:T(8,128)(2,1)}, u32[]{:S(2)}) copy-start(bf16[128,1152]{1,0:T(8,128)(2,1)} %refs_2_.3) | copy-start | bytes 884740
  201.1 32.5 %copy-start.15 = (f32[128]{0:T(128)S(1)}, f32[128]{0:T(128)}, u32[]{:S(2)}) copy-start(f32[128]{0:T(128)} %param.24) | copy-start | bytes 1540
  201.2 32.5 %all-to-all-start.3 = ((bf16[32,136,128]{2,1,0:T(8,128)(2,1)}), bf16[32,136,128]{2,1,0:T(8,128)(2,1)S(1)}, u32[]{:S(2)}, u32[]{:S(2)}) async-start(bf16[32,136,128]{2,1,0:T(8,128)(2,1)} %text_down.1), calls=%async_computation.3 | async-start | bytes 2228224 | tf_op jit(solution)/shard_map/all_to_all | solution.py:40
  206.1 3.8 %collective-permute-start.13 = (bf16[4,72,192]{2,1,0:T(8,128)(2,1)S(1)}, bf16[4,72,192]{2,1,0:T(8,128)(2,1)S(1)}, u32[]{:S(2)}, u32[]{:S(2)}) collective-permute-start(bf16[4,72,192]{2,1,0:T(8,128)(2,1)S(1)} %copy-done.39), channel_id=1, source_target_pairs={{0,2},{2,0},{16,18},{18,16},{1,3},{3,1},{17,19},{19,17},{4,6},{6,4... | collective-permute-start | bytes 331784 | tf_op jit(solution)/shard_map/ppermute | solution.py:50
  206.5 19.9 %collective-permute-start.14 = (bf16[4,72,192]{2,1,0:T(8,128)(2,1)S(1)}, bf16[4,72,192]{2,1,0:T(8,128)(2,1)S(1)}, u32[]{:S(2)}, u32[]{:S(2)}) collective-permute-start(bf16[4,72,192]{2,1,0:T(8,128)(2,1)S(1)} %copy-done.38), channel_id=1, source_target_pairs={{0,16},{2,18},{16,0},{18,2},{1,17},{3,19},{17,1},{19,3},{4,20},{6,... | collective-permute-start | bytes 331784 | tf_op jit(solution)/shard_map/ppermute | solution.py:50
  209.7 18.9 %collective-permute-start.15 = (bf16[4,72,192]{2,1,0:T(8,128)(2,1)S(1)}, bf16[4,72,192]{2,1,0:T(8,128)(2,1)S(1)}, u32[]{:S(2)}, u32[]{:S(2)}) collective-permute-start(bf16[4,72,192]{2,1,0:T(8,128)(2,1)S(1)} %copy-done.37), channel_id=1, source_target_pairs={{0,18},{2,16},{16,2},{18,0},{1,19},{3,17},{17,3},{19,1},{4,22},{6,... | collective-permute-start | bytes 331784 | tf_op jit(solution)/shard_map/ppermute | solution.py:50
  228.6 35.9 %copy-start.6 = (bf16[1152,72]{0,1:T(8,128)(2,1)S(1)}, bf16[1152,72]{0,1:T(8,128)(2,1)}, u32[]{:S(2)}) copy-start(bf16[1152,72]{0,1:T(8,128)(2,1)} %param.32) | copy-start | bytes 497668
  229.3 10.2 %collective-permute-start.18 = (bf16[4,72,192]{2,1,0:T(8,128)(2,1)S(1)}, bf16[4,72,192]{2,1,0:T(8,128)(2,1)S(1)}, u32[]{:S(2)}, u32[]{:S(2)}) collective-permute-start(bf16[4,72,192]{2,1,0:T(8,128)(2,1)S(1)} %get-tuple-element.43), channel_id=1, source_target_pairs={{0,12},{4,0},{8,4},{12,8},{1,13},{5,1},{9,5},{13,9},{2,14},{6,2},{... | collective-permute-start | bytes 331784 | tf_op jit(solution)/shard_map/ppermute | solution.py:45
  232.4 8.2 %collective-permute-start.17 = (bf16[4,72,192]{2,1,0:T(8,128)(2,1)S(1)}, bf16[4,72,192]{2,1,0:T(8,128)(2,1)S(1)}, u32[]{:S(2)}, u32[]{:S(2)}) collective-permute-start(bf16[4,72,192]{2,1,0:T(8,128)(2,1)S(1)} %get-tuple-element.42), channel_id=1, source_target_pairs={{0,8},{4,12},{8,0},{12,4},{1,9},{5,13},{9,1},{13,5},{2,10},{6,14},... | collective-permute-start | bytes 331784 | tf_op jit(solution)/shard_map/ppermute | solution.py:45
  232.7 21.9 %collective-permute-start.16 = (bf16[4,72,192]{2,1,0:T(8,128)(2,1)S(1)}, bf16[4,72,192]{2,1,0:T(8,128)(2,1)S(1)}, u32[]{:S(2)}, u32[]{:S(2)}) collective-permute-start(bf16[4,72,192]{2,1,0:T(8,128)(2,1)S(1)} %get-tuple-element.41), channel_id=1, source_target_pairs={{0,4},{4,8},{8,12},{12,0},{1,5},{5,9},{9,13},{13,1},{2,6},{6,10},{... | collective-permute-start | bytes 331784 | tf_op jit(solution)/shard_map/ppermute | solution.py:45
  234.8 14.9 %all-to-all-start.4 = ((bf16[32,4,1280]{2,1,0:T(4,128)(2,1)}), bf16[32,4,1280]{2,1,0:T(4,128)(2,1)S(1)}, u32[]{:S(2)}, u32[]{:S(2)}) async-start(bf16[32,4,1280]{2,1,0:T(4,128)(2,1)} %caption_partial.1), calls=%async_computation.4 | async-start | bytes 655360 | tf_op jit(solution)/shard_map/all_to_all | solution.py:40
  239.5 31.2 %copy-start.20 = (bf16[4,72,192]{2,1,0:T(8,128)(2,1)}, bf16[4,72,192]{2,1,0:T(8,128)(2,1)S(1)}, u32[]{:S(2)}) copy-start(bf16[4,72,192]{2,1,0:T(8,128)(2,1)S(1)} %collective-permute-done.18.refs_3_) | copy-start | bytes 331780
  240.6 30.1 %copy-start.21 = (bf16[4,72,192]{2,1,0:T(8,128)(2,1)}, bf16[4,72,192]{2,1,0:T(8,128)(2,1)S(1)}, u32[]{:S(2)}) copy-start(bf16[4,72,192]{2,1,0:T(8,128)(2,1)S(1)} %collective-permute-done.17.refs_2_) | copy-start | bytes 331780
  250.7 13.8 %all-to-all-start.5 = ((bf16[32,4,1152]{2,1,0:T(4,128)(2,1)}), bf16[32,4,1152]{2,1,0:T(4,128)(2,1)S(1)}, u32[]{:S(2)}, u32[]{:S(2)}) async-start(bf16[32,4,1152]{2,1,0:T(4,128)(2,1)} %caption.1), calls=%async_computation.5 | async-start | bytes 589824 | tf_op jit(solution)/shard_map/all_to_all | solution.py:40
  254.6 16.2 %copy-start.22 = (bf16[4,72,192]{2,1,0:T(8,128)(2,1)}, bf16[4,72,192]{2,1,0:T(8,128)(2,1)S(1)}, u32[]{:S(2)}) copy-start(bf16[4,72,192]{2,1,0:T(8,128)(2,1)S(1)} %collective-permute-done.16.refs_1_) | copy-start | bytes 331780
  265.6 16.9 %all-to-all-start.6 = ((bf16[32,72,128]{2,1,0:T(8,128)(2,1)}), bf16[32,72,128]{2,1,0:T(8,128)(2,1)S(1)}, u32[]{:S(2)}, u32[]{:S(2)}) async-start(bf16[32,72,128]{2,1,0:T(8,128)(2,1)} %text_kv.1), calls=%async_computation.6 | async-start | bytes 1179648 | tf_op jit(solution)/shard_map/all_to_all | solution.py:40
  (20 other events, 49.9 us)
Sparse Core Ops, SparseCore 0:
  119.0 76.2 all-gather.1
where the time goes:
time: 298 us; the launch traced here: 297 us
  Pallas kernels  97.4 us (33%)
  waiting for transfers between devices  95.8 us (32%)
  starting transfers between devices  76 us (26%)
  between operations  14.5 us (5%)
  local copies, waits for them, and re-layouts  9.21 us (3%)
    pallas_call x12, Pallas kernels, call(): pl.pallas_call(body, out_shape=outs if many else outs[0], in_specs=(in_sp...  85.1 us
    ppermute x14, waiting for transfers between devices, crossed(): return lax.ppermute(value, axis, [(i, i ^ mask) for i in range(size)])  50.5 us
    all_to_all x7, starting transfers between devices, exchange(): return lax.all_to_all(blocks, axes, 0, 0, tiled=True)  39.1 us
    all_to_all x7, waiting for transfers between devices, exchange(): return lax.all_to_all(blocks, axes, 0, 0, tiled=True)  25.4 us
    ppermute x14, starting transfers between devices, crossed(): return lax.ppermute(value, axis, [(i, i ^ mask) for i in range(size)])  21.2 us
    ppermute x6, waiting for transfers between devices, shifted(): lax.ppermute(value, axis, [(i, (i + shift) % size) for i in range(size)])  19.8 us
    ppermute x6, starting transfers between devices, shifted(): lax.ppermute(value, axis, [(i, (i + shift) % size) for i in range(size)])  15.6 us
    unnamed x81, local copies, waits for them, and re-layouts  8.59 us
  transfers between devices with their start and end apart: 28, of which 14 were waited for; matrix products, arithmetic and copies ran while one was open for 2% of the time, Pallas kernels for 29%

commit v1 on v0

--- a/solution.py
+++ b/solution.py
@@ -18,6 +18,7 @@
 PLANE = ("yhi", "x", "core", "tp")
 SEQ = ("yhi", "x", "core")
 SIDE = ("yhi", "core")
+ROW = ("yhi", "tp")
 SCORE_SCALE = 1.0 / math.sqrt(HEAD)
 EXP2_SCALE = SCORE_SCALE * math.log2(math.e)
 LIFT = 64.0
@@ -235,7 +236,8 @@
         out_ref[j] = kv
 
 
-def modulate_kernel(image_ref, mod_ref, out_ref):
+def modulate_kernel(image_ref, mod_ref, weight_ref, out_ref, copy_ref):
+    copy_ref[...] = weight_ref[...]
     pixels = image_ref[...].astype(F32)
     center = jnp.mean(pixels, axis=-1, keepdims=True)
     spread = jnp.mean((pixels - center) ** 2, axis=-1, keepdims=True)
@@ -260,25 +262,23 @@
 
 def qkv_kernel(at_ref, *refs):
     tokens, weights = refs[:4], refs[4:8]
-    fulls, pairs = refs[8:12], refs[12:16]
-    x_rows = refs[16]
+    fulls = refs[8:12]
+    x_rows, by_chip = refs[12:14]
     rows = tokens[0].shape[0]
     for m, block in enumerate(tokens):
         at = lax.rem(at_ref[1] - m + 4, 4)
         x_rows[pl.ds(pl.multiple_of(at * rows, rows), rows), :] = block[...]
+    for m, block in enumerate(weights):
+        by_chip[lax.bitwise_xor(at_ref[4], m)] = block[...]
     span = x_rows.shape[0]
     zeros = jnp.zeros((SLOT - HEAD, span), F32)
     ones = (lax.broadcasted_iota(jnp.int32, zeros.shape, 0) == 0).astype(F32)
     for s in range(4):
-        out = nt_dot(weights[s][...], x_rows[...])
-        slots = [
-            jnp.concatenate([out[i * HEAD : (i + 1) * HEAD], tail], axis=0).astype(BF16)
-            for i, tail in enumerate((zeros, ones, zeros))
-        ]
-        for i in range(3):
-            fulls[s][i * SLOT : (i + 1) * SLOT, :] = slots[i]
-        for i in range(2):
-            pairs[s][i * SLOT : (i + 1) * SLOT, :] = slots[i + 1]
+        out = nt_dot(by_chip[s], x_rows[...])
+        for i, tail in enumerate((zeros, ones, zeros)):
+            fulls[s][i * SLOT : (i + 1) * SLOT, :] = jnp.concatenate(
+                [out[i * HEAD : (i + 1) * HEAD], tail], axis=0
+            ).astype(BF16)
 
 
 ROWS = 192
@@ -292,12 +292,12 @@
     span = fulls[0].shape[1]
     count = 8 * span
     largest = None
-    for c, (ref, first) in enumerate([(r, SLOT) for r in fulls] + [(r, 0) for r in others]):
-        block = ref[first : first + SLOT, :]
+    for c, ref in enumerate(fulls + others):
+        block = ref[SLOT : 2 * SLOT, :]
         cols = slice(c * span, (c + 1) * span)
         keys[:SLOT, cols] = block
         keys[SLOT:, cols] = block
-        vals[cols, :] = ref[first + SLOT : first + 2 * SLOT, :].astype(F32).T.astype(BF16)
+        vals[cols, :] = ref[2 * SLOT : 3 * SLOT, :].astype(F32).T.astype(BF16)
         wide = block.astype(F32)
         row = lax.broadcasted_iota(jnp.int32, wide.shape, 0)
         norm = jnp.sum(jnp.where(row < HEAD, wide * wide, 0.0), axis=0, keepdims=True)
@@ -335,29 +335,43 @@
     none = jnp.zeros((ROWS, 128), F32)
     empty = jnp.zeros((ROWS, SLOT), F32)
 
-    def step(i, seen):
+    def sums(total):
+        total = jnp.sum(total, axis=-1, keepdims=True)
+        return total, 1.0 / total
+
+    blocks = qry.shape[0]
+    terms_b[...] = jnp.zeros(terms_b.shape, F32)
+
+    def step(i, carry):
+        inverse_b, least, most = carry
         one, two = qry[2 * i], qry[2 * i + 1]
         total_a, total_b, acc_a, acc_b = none, none, empty, empty
         for t in range(tiles):
             total_a = fill(one, t, terms_a, total_a)
-        total_a = jnp.sum(total_a, axis=-1, keepdims=True)
-        inverse = 1.0 / total_a
+            acc_b = weigh(t, terms_b, inverse_b, acc_b)
+        put(lax.rem(2 * i + blocks, blocks + 1), acc_b)
+        total_a, inverse_a = sums(total_a)
         for t in range(tiles):
             total_b = fill(two, t, terms_b, total_b)
-            acc_a = weigh(t, terms_a, inverse, acc_a)
+            acc_a = weigh(t, terms_a, inverse_a, acc_a)
         put(2 * i, acc_a)
-        total_b = jnp.sum(total_b, axis=-1, keepdims=True)
-        inverse = 1.0 / total_b
-        for t in range(tiles):
-            acc_b = weigh(t, terms_b, inverse, acc_b)
-        put(2 * i + 1, acc_b)
-        least, most = seen
+        total_b, inverse_b = sums(total_b)
         return (
+            inverse_b,
             jnp.minimum(least, jnp.min(jnp.minimum(total_a, total_b))),
             jnp.maximum(most, jnp.max(jnp.maximum(total_a, total_b))),
         )
 
-    least, most = lax.fori_loop(0, 8, step, (jnp.float32(1.0), jnp.float32(1.0)))
+    inverse, least, most = lax.fori_loop(
+        0,
+        blocks // 2,
+        step,
+        (jnp.zeros((ROWS, 1), F32), jnp.float32(1.0), jnp.float32(1.0)),
+    )
+    acc = empty
+    for t in range(tiles):
+        acc = weigh(t, terms_b, inverse, acc)
+    put(blocks - 1, acc)
     safe = jnp.logical_and(least > 2.0**-76, most < 2.0**100)
 
     @pl.when(jnp.logical_not(safe))
@@ -381,7 +395,7 @@
             put(i, acc)
             return 0
 
-        lax.fori_loop(0, 16, again, 0)
+        lax.fori_loop(0, blocks, again, 0)
 
     for s, out in enumerate(outs):
         out[...] = found[4 * s : 4 * s + 4]
@@ -502,26 +516,33 @@
     pixels = image[0]
     rows = pixels.shape[0]
     modulate = modulation[0]
-    modulated = call(modulate_kernel, "modulate", shape((rows, W)), (pixels, modulate))
+    modulated, head_weight = call(
+        modulate_kernel,
+        "modulate",
+        [shape((rows, W)), shape((3 * HEAD, W))],
+        (pixels, modulate, w_qkv.T),
+    )
     token_blocks = [modulated] + [shifted(modulated, "x", s) for s in range(1, 4)]
-    weight_blocks = [w_qkv.T, crossed(w_qkv.T, "core", 1), crossed(w_qkv.T, "yhi", 1)]
+    weight_blocks = [head_weight, crossed(head_weight, "core", 1), crossed(head_weight, "yhi", 1)]
     weight_blocks.append(crossed(weight_blocks[2], "core", 1))
-    at = jnp.stack([lax.axis_index(a) for a in (SIDE, "x", "tp", PLANE)]).astype(jnp.int32)
+    core, row = lax.axis_index("core"), lax.axis_index("tp")
+    at = jnp.stack(
+        [lax.axis_index(a) for a in (ROW, "x", "tp", PLANE)] + [lax.bitwise_xor(core, row)]
+    ).astype(jnp.int32)
     span = 4 * rows
     made = call(
         qkv_kernel,
         "query_key_value",
-        [shape((3 * SLOT, span))] * 4 + [shape((2 * SLOT, span))] * 4,
+        [shape((3 * SLOT, span))] * 4,
         (at, *token_blocks, *weight_blocks),
-        scratch=[pltpu.VMEM((span, W), BF16)],
+        scratch=[pltpu.VMEM((span, W), BF16), pltpu.VMEM((4, 3 * HEAD, W), BF16)],
         in_specs=[SMEM] + [VMEM] * 8,
         flops=2 * span * W * 12 * HEAD,
         moved=8 << 20,
         mib=56,
-        tick=True,
-    )
-    fulls = [made[0]] + [crossed(made[m], SIDE, m) for m in range(1, 4)]
-    others = [crossed(made[4 + m], SIDE + ("tp",), 2 * m + 1) for m in range(4)]
+    )
+    fulls = [made[0]] + [crossed(made[m], ROW, m) for m in range(1, 4)]
+    others = [crossed(full, "core", 1) for full in fulls]
 
     embedded = call(
         embed_kernel,
@@ -563,7 +584,7 @@
             pltpu.VMEM((16, ROWS, 2 * SLOT), BF16),
             pltpu.VMEM((ROWS, 8 * span), F32),
             pltpu.VMEM((ROWS, 8 * span), F32),
-            pltpu.VMEM((16, HEAD, ROWS), BF16),
+            pltpu.VMEM((17, HEAD, ROWS), BF16),
         ],
         in_specs=[SMEM] + [VMEM] * 8,
         flops=16 * span * 2 * span * 256 * 2,
@@ -573,7 +594,7 @@
         tick=True,
         mib=56,
     )
-    found = [found[0]] + [crossed(found[m], SIDE, m) for m in range(1, 4)]
+    found = [found[0]] + [crossed(found[m], ROW, m) for m in range(1, 4)]
     down = call(
         down_kernel,
         "text_down",
@@ -584,15 +605,21 @@
         exps=tokens * units,
         after=(attended,),
     )
-    cap_part = call(
+    cap_part, tick = call(
         cap_kernel,
         "caption_partial",
-        shape((plane, share, W + 128)),
+        [shape((plane, share, W + 128))],
         (exchange(down, PLANE), final_gain.reshape(1, width), cap_weight),
         scratch=[pltpu.VMEM((tokens, width), F32), pltpu.VMEM((tokens, W + 128), F32)],
+        tick=True,
     )
     *grouped, tick = call(
-        regroup_kernel, "regroup", [shape((4, HEAD, rows))] * 4, tuple(found), tick=True
+        regroup_kernel,
+        "regroup",
+        [shape((4, HEAD, rows))] * 4,
+        tuple(found),
+        after=(tick,),
+        tick=True,
     )
     caption = call(
         caption_kernel,

time: 298 us -> 286 us (0.960)
  starting transfers between devices: 76 us -> 68.6 us
  waiting for transfers between devices: 95.8 us -> 92.8 us
    ppermute x14, waiting for transfers between devices: 50.5 us -> 35.2 us  [crossed(): return lax.ppermute(value, axis, [(i, i ^ mask) for i in range(size)])]
    all_to_all x7, waiting for transfers between devices: 25.4 us -> 37.5 us  [exchange(): return lax.all_to_all(blocks, axes, 0, 0, tiled=True)]
    ppermute x14, starting transfers between devices: 21.2 us -> 13.9 us  [crossed(): return lax.ppermute(value, axis, [(i, i ^ mask) for i in range(size)])]
    unnamed x81 -> x71, local copies, waits for them, and re-layouts: 8.59 us -> 8.74 us
  transfers between devices with their start and end apart: 28 -> 28, of which waited for: 14 -> 15; matrix products, arithmetic and copies ran while one was open for 2% -> 2% of each run, Pallas kernels for 29% -> 30%
where the time goes in v1:
time: 286 us; the launch traced here: 285 us
  Pallas kernels  95.2 us (33%)
  waiting for transfers between devices  92.8 us (32%)
  starting transfers between devices  68.6 us (24%)
  between operations  14.4 us (5%)
  local copies, waits for them, and re-layouts  10.7 us (4%)
    pallas_call x12, Pallas kernels, call(): pl.pallas_call(body, out_shape=outs if many else outs[0], in_specs=(in_sp...  82.9 us
    all_to_all x7, starting transfers between devices, exchange(): return lax.all_to_all(blocks, axes, 0, 0, tiled=True)  39.2 us
    all_to_all x7, waiting for transfers between devices, exchange(): return lax.all_to_all(blocks, axes, 0, 0, tiled=True)  37.5 us
    ppermute x14, waiting for transfers between devices, crossed(): return lax.ppermute(value, axis, [(i, i ^ mask) for i in range(size)])  35.2 us
    ppermute x6, waiting for transfers between devices, shifted(): lax.ppermute(value, axis, [(i, (i + shift) % size) for i in range(size)])  20.1 us
    ppermute x6, starting transfers between devices, shifted(): lax.ppermute(value, axis, [(i, (i + shift) % size) for i in range(size)])  15.5 us
    ppermute x14, starting transfers between devices, crossed(): return lax.ppermute(value, axis, [(i, i ^ mask) for i in range(size)])  13.9 us
    unnamed x71, local copies, waits for them, and re-layouts  8.74 us
  transfers between devices with their start and end apart: 28, of which 15 were waited for; matrix products, arithmetic and copies ran while one was open for 2% of the time, Pallas kernels for 30%

profile of v1, /device:TPU:32, one launch (start us, length us, event | category | flops | bytes accessed | tf_op | source)
XLA Modules:
  0.0 285.5 jit_solution(14457052302751171639)
XLA Ops:
  6.5 0.8 copy.20
  7.3 1.0 copy-done.2
  8.4 1.0 copy-done.4
  9.8 3.3 %collective-permute-start.4 = (bf16[216,1152]{1,0:T(8,128)(2,1)S(1)}, bf16[216,1152]{1,0:T(8,128)(2,1)}, u32[]{:S(2)}, u32[]{:S(2)}) collective-permute-start(bf16[216,1152]{1,0:T(8,128)(2,1)S(1)} %get-tuple-element.28.refs_5_), channel_id=1, source_target_pairs={{0,16},{16,0},{1,17},{17,1},{2,18},{18,2},{3,19},{19,3},{4,20},{20... | collective-permute-start | bytes 1493000 | tf_op jit(solution)/shard_map/ppermute | solution.py:51
  13.8 2.3 fusion.2
  16.0 5.2 %all-to-all-start = ((bf16[32,32,512]{2,1,0:T(8,128)(2,1)}), bf16[32,32,512]{2,1,0:T(8,128)(2,1)S(1)}, u32[]{:S(2)}, u32[]{:S(2)}) async-start(bf16[32,32,512]{2,1,0:T(8,128)(2,1)} %bitcast.37), calls=%async_computation | async-start | bytes 2097152 | tf_op jit(solution)/shard_map/all_to_all | solution.py:41
  21.6 5.8 %collective-permute-done.4.refs_7_ = bf16[216,1152]{1,0:T(8,128)(2,1)} collective-permute-done((bf16[216,1152]{1,0:T(8,128)(2,1)S(1)}, bf16[216,1152]{1,0:T(8,128)(2,1)}, u32[]{:S(2)}, u32[]{:S(2)}) %collective-permute-start.4) | collective-permute-done | bytes 497696 | tf_op jit(solution)/shard_map/ppermute | solution.py:51
  27.5 2.5 collective-permute-start
  29.9 7.3 %collective-permute-start.1 = (bf16[192,1152]{1,0:T(8,128)(2,1)S(1)}, bf16[192,1152]{1,0:T(8,128)(2,1)}, u32[]{:S(2)}, u32[]{:S(2)}) collective-permute-start(bf16[192,1152]{1,0:T(8,128)(2,1)S(1)} %get-tuple-element.27.refs_1_), channel_id=1, source_target_pairs={{0,8},{4,12},{8,0},{12,4},{1,9},{5,13},{9,1},{13,5},{2,10},{6,14},... | collective-permute-start | bytes 1327112 | tf_op jit(solution)/shard_map/ppermute | solution.py:46
  37.2 1.5 collective-permute-start.2
  39.3 7.3 %collective-permute-done.refs_2_ = bf16[192,1152]{1,0:T(8,128)(2,1)S(1)} collective-permute-done((bf16[192,1152]{1,0:T(8,128)(2,1)S(1)}, bf16[192,1152]{1,0:T(8,128)(2,1)S(1)}, u32[]{:S(2)}, u32[]{:S(2)}) %collective-permute-start) | collective-permute-done | bytes 442400 | tf_op jit(solution)/shard_map/ppermute | solution.py:46
  46.6 10.8 %collective-permute-done.1.refs_3_ = bf16[192,1152]{1,0:T(8,128)(2,1)} collective-permute-done((bf16[192,1152]{1,0:T(8,128)(2,1)S(1)}, bf16[192,1152]{1,0:T(8,128)(2,1)}, u32[]{:S(2)}, u32[]{:S(2)}) %collective-permute-start.1) | collective-permute-done | bytes 442400 | tf_op jit(solution)/shard_map/ppermute | solution.py:46
  58.0 1.2 embed_sum.1
  59.2 8.2 %all-to-all-start.1 = ((bf16[32,32,512]{2,1,0:T(8,128)(2,1)}), bf16[32,32,512]{2,1,0:T(8,128)(2,1)S(1)}, u32[]{:S(2)}, u32[]{:S(2)}) async-start(bf16[32,32,512]{2,1,0:T(8,128)(2,1)} %embed_sum.1), calls=%async_computation.1 | async-start | bytes 2097152 | tf_op jit(solution)/shard_map/all_to_all | solution.py:41
  67.6 5.8 %query_key_value.1 = (bf16[240,768]{1,0:T(8,128)(2,1)}, bf16[240,768]{1,0:T(8,128)(2,1)}, bf16[240,768]{1,0:T(8,128)(2,1)}, bf16[240,768]{1,0:T(8,128)(2,1)}) custom-call(s32[5]{0:T(128)} %stack.23.refs_0_.at_ref, bf16[192,1152]{1,0:T(8,128)(2,1)} %copy-done.17, bf16[192,1152]{1,0:T(8,128)(2,1)} %copy-done.33, ...), custom_call_target="tpu_custom_call" | custom-call | flops 1528823808 | bytes 8388608 | tf_op jit(solution)/shard_map/query_key_value/pallas_call | solution.py:93
  73.4 1.8 collective-permute-start.6
  75.1 2.7 collective-permute-start.7
  78.1 11.9 %collective-permute-done.6.refs_2_ = bf16[240,768]{1,0:T(8,128)(2,1)S(1)} collective-permute-done((bf16[240,768]{1,0:T(8,128)(2,1)}, bf16[240,768]{1,0:T(8,128)(2,1)S(1)}, u32[]{:S(2)}, u32[]{:S(2)}) %collective-permute-start.6) | collective-permute-done | bytes 368672 | tf_op jit(solution)/shard_map/ppermute | solution.py:51
  90.0 9.0 %collective-permute-done.7.refs_3_ = bf16[240,768]{1,0:T(8,128)(2,1)S(1)} collective-permute-done((bf16[240,768]{1,0:T(8,128)(2,1)}, bf16[240,768]{1,0:T(8,128)(2,1)S(1)}, u32[]{:S(2)}, u32[]{:S(2)}) %collective-permute-start.7) | collective-permute-done | bytes 368672 | tf_op jit(solution)/shard_map/ppermute | solution.py:51
  102.4 1.8 text_gate_up.1
  104.2 1.1 copy-done.3
  105.3 3.7 %collective-permute-done.19.refs_2_ = bf16[36,3456]{1,0:T(8,128)(2,1)S(1)} collective-permute-done((bf16[36,3456]{1,0:T(8,128)(2,1)S(1)}, bf16[36,3456]{1,0:T(8,128)(2,1)S(1)}, u32[]{:S(2)}, u32[]{:S(2)}) %collective-permute-start.19) | collective-permute-done | bytes 248864 | tf_op jit(solution)/shard_map/ppermute | solution.py:51
  109.0 1.5 side_pair.1
  110.5 8.6 %all-to-all-start.2 = ((bf16[8,136,640]{2,1,0:T(8,128)(2,1)}), bf16[8,136,640]{2,1,0:T(8,128)(2,1)S(1)}, u32[]{:S(2)}, u32[]{:S(2)}) async-start(bf16[8,136,640]{2,1,0:T(8,128)(2,1)} %copy-done.3), calls=%async_computation.2 | async-start | bytes 2785280 | tf_op jit(solution)/shard_map/all_to_all | solution.py:41
  119.1 67.0 %self_attention.1 = (bf16[4,72,192]{2,1,0:T(8,128)(2,1)}, bf16[4,72,192]{2,1,0:T(8,128)(2,1)}, bf16[4,72,192]{2,1,0:T(8,128)(2,1)}, bf16[4,72,192]{2,1,0:T(8,128)(2,1)}, f32[8,128]{1,0:T(8,128)}) custom-call(s32[5]{0:T(128)} %stack.23.refs_0_.at_ref, bf16[240,768]{1,0:T(8,128)(2,1)} %get-tuple-element.29.refs_1_, bf16[240,768]{1,0:T(8,128)(2,1)} %copy-done.26, ...), custom_call_target="tpu_custom_call" | custom-call | flops 9663676416 | bytes 8388608 | tf_op jit(solution)/shard_map/self_attention/pallas_call | solution.py:93
  186.1 1.7 copy-done.1
  188.6 2.0 text_down.1
  190.6 4.8 %all-to-all-start.3 = ((bf16[32,136,128]{2,1,0:T(8,128)(2,1)}), bf16[32,136,128]{2,1,0:T(8,128)(2,1)S(1)}, u32[]{:S(2)}, u32[]{:S(2)}) async-start(bf16[32,136,128]{2,1,0:T(8,128)(2,1)} %text_down.1), calls=%async_computation.3 | async-start | bytes 2228224 | tf_op jit(solution)/shard_map/all_to_all | solution.py:41
  195.4 1.9 collective-permute-start.13
  197.2 2.7 collective-permute-start.14
  200.2 13.7 %all-to-all-done.3.refs_0_ = bf16[32,136,128]{2,1,0:T(8,128)(2,1)S(1)} async-done(((bf16[32,136,128]{2,1,0:T(8,128)(2,1)}), bf16[32,136,128]{2,1,0:T(8,128)(2,1)S(1)}, u32[]{:S(2)}, u32[]{:S(2)}) %all-to-all-start.3) | async-done | bytes 1114144 | tf_op jit(solution)/shard_map/all_to_all | solution.py:41
  214.0 1.1 caption_partial.1
  215.1 2.9 %collective-permute-done.14.refs_2_ = bf16[4,72,192]{2,1,0:T(8,128)(2,1)S(1)} collective-permute-done((bf16[4,72,192]{2,1,0:T(8,128)(2,1)}, bf16[4,72,192]{2,1,0:T(8,128)(2,1)S(1)}, u32[]{:S(2)}, u32[]{:S(2)}) %collective-permute-start.14) | collective-permute-done | bytes 110624 | tf_op jit(solution)/shard_map/ppermute | solution.py:51
  218.7 2.8 collective-permute-start.18
  221.6 0.8 collective-permute-start.17
  223.1 4.6 %all-to-all-start.4 = ((bf16[32,4,1280]{2,1,0:T(4,128)(2,1)}), bf16[32,4,1280]{2,1,0:T(4,128)(2,1)S(1)}, u32[]{:S(2)}, u32[]{:S(2)}) async-start(bf16[32,4,1280]{2,1,0:T(4,128)(2,1)} %get-tuple-element.47), calls=%async_computation.4 | async-start | bytes 655360 | tf_op jit(solution)/shard_map/all_to_all | solution.py:41
  227.8 2.1 collective-permute-done.17.refs_2_
  229.9 8.1 %all-to-all-done.4.refs_0_ = bf16[32,4,1280]{2,1,0:T(4,128)(2,1)S(1)} async-done(((bf16[32,4,1280]{2,1,0:T(4,128)(2,1)}), bf16[32,4,1280]{2,1,0:T(4,128)(2,1)S(1)}, u32[]{:S(2)}, u32[]{:S(2)}) %all-to-all-start.4) | async-done | bytes 327712 | tf_op jit(solution)/shard_map/all_to_all | solution.py:41
  238.0 0.9 caption.1
  238.9 3.9 %all-to-all-start.5 = ((bf16[32,4,1152]{2,1,0:T(4,128)(2,1)}), bf16[32,4,1152]{2,1,0:T(4,128)(2,1)S(1)}, u32[]{:S(2)}, u32[]{:S(2)}) async-start(bf16[32,4,1152]{2,1,0:T(4,128)(2,1)} %caption.1), calls=%async_computation.5 | async-start | bytes 589824 | tf_op jit(solution)/shard_map/all_to_all | solution.py:41
  242.9 9.8 %all-to-all-done.5.refs_0_ = bf16[32,4,1152]{2,1,0:T(4,128)(2,1)S(1)} async-done(((bf16[32,4,1152]{2,1,0:T(4,128)(2,1)}), bf16[32,4,1152]{2,1,0:T(4,128)(2,1)S(1)}, u32[]{:S(2)}, u32[]{:S(2)}) %all-to-all-start.5) | async-done | bytes 294944 | tf_op jit(solution)/shard_map/all_to_all | solution.py:41
  252.7 1.2 text_kv.1
  253.9 3.9 %all-to-all-start.6 = ((bf16[32,72,128]{2,1,0:T(8,128)(2,1)}), bf16[32,72,128]{2,1,0:T(8,128)(2,1)S(1)}, u32[]{:S(2)}, u32[]{:S(2)}) async-start(bf16[32,72,128]{2,1,0:T(8,128)(2,1)} %text_kv.1), calls=%async_computation.6 | async-start | bytes 1179648 | tf_op jit(solution)/shard_map/all_to_all | solution.py:41
  258.4 1.3 slice_bitcast_fusion.3.refs_7_
  259.7 5.2 %project_out_and_query.1 = (bf16[192,1152]{1,0:T(8,128)(2,1)}, bf16[192,1152]{1,0:T(8,128)(2,1)}) custom-call(s32[5]{0:T(128)} %stack.23.refs_0_.at_ref, bf16[4,72,192]{2,1,0:T(8,128)(2,1)} %copy-done.8, bf16[4,72,192]{2,1,0:T(8,128)(2,1)} %copy-done.24, bf16[4,72,192]{2,1,0:T(8,128)(2,1)} %copy-done.23, bf16[4,72,192]{2,1,0:T(8,128)(2,1)} %copy-done.22, ...), custom_call_target="tpu_custom_call" | custom-call | flops 1019215872 | bytes 8388608 | tf_op jit(solution)/shard_map/project_out_and_query/pallas_call | solution.py:450
  264.9 5.8 %all-to-all-done.6.kv_ref = bf16[32,72,128]{2,1,0:T(8,128)(2,1)S(1)} async-done(((bf16[32,72,128]{2,1,0:T(8,128)(2,1)}), bf16[32,72,128]{2,1,0:T(8,128)(2,1)S(1)}, u32[]{:S(2)}, u32[]{:S(2)}) %all-to-all-start.6) | async-done | bytes 589856 | tf_op jit(solution)/shard_map/all_to_all | solution.py:41
  270.7 0.8 copy-done.21
  271.6 7.0 %cross_attention.1 = bf16[192,1152]{1,0:T(8,128)(2,1)} custom-call(s32[1]{0:T(128)S(6)} %copy.21.len_ref, bf16[192,1152]{1,0:T(8,128)(2,1)} %get-tuple-element.45.cq_ref, bf16[192,1152]{1,0:T(8,128)(2,1)} %get-tuple-element.46.after_ref, bf16[32,72,128]{2,1,0:T(8,128)(2,1)} %copy-done.21, bf16[1152,3456]{1,0:T(8,128)(2,1)} %all-gather.2.cloned.1.call-done.refs_4_.refs_5_.wco_ref), custom_call_target="tpu_custom_call" | custom-call | flops 1019215872 | bytes 5242880 | tf_op jit(solution)/shard_map/cross_attention/pallas_call | solution.py:469
  (105 shorter events, 8.9 us)
Async XLA Ops:
  9.8 11.5 %copy-start.16 = (bf16[216,1152]{1,0:T(8,128)(2,1)}, bf16[216,1152]{1,0:T(8,128)(2,1)S(1)}, u32[]{:S(2)}) copy-start(bf16[216,1152]{1,0:T(8,128)(2,1)S(1)} %get-tuple-element.28.refs_5_) | copy-start | bytes 1492996
  9.8 27.4 %copy-start.17 = (bf16[192,1152]{1,0:T(8,128)(2,1)}, bf16[192,1152]{1,0:T(8,128)(2,1)S(1)}, u32[]{:S(2)}) copy-start(bf16[192,1152]{1,0:T(8,128)(2,1)S(1)} %get-tuple-element.27.refs_1_) | copy-start | bytes 1327108
  9.8 17.7 %collective-permute-start.4 = (bf16[216,1152]{1,0:T(8,128)(2,1)S(1)}, bf16[216,1152]{1,0:T(8,128)(2,1)}, u32[]{:S(2)}, u32[]{:S(2)}) collective-permute-start(bf16[216,1152]{1,0:T(8,128)(2,1)S(1)} %get-tuple-element.28.refs_5_), channel_id=1, source_target_pairs={{0,16},{16,0},{1,17},{17,1},{2,18},{18,2},{3,19},{19,3},{4,20},{20... | collective-permute-start | bytes 1493000 | tf_op jit(solution)/shard_map/ppermute | solution.py:51
  16.0 42.0 %all-to-all-start = ((bf16[32,32,512]{2,1,0:T(8,128)(2,1)}), bf16[32,32,512]{2,1,0:T(8,128)(2,1)S(1)}, u32[]{:S(2)}, u32[]{:S(2)}) async-start(bf16[32,32,512]{2,1,0:T(8,128)(2,1)} %bitcast.37), calls=%async_computation | async-start | bytes 2097152 | tf_op jit(solution)/shard_map/all_to_all | solution.py:41
  21.2 36.1 %collective-permute-start.3 = (bf16[216,1152]{1,0:T(8,128)(2,1)S(1)}, bf16[216,1152]{1,0:T(8,128)(2,1)}, u32[]{:S(2)}, u32[]{:S(2)}) collective-permute-start(bf16[216,1152]{1,0:T(8,128)(2,1)S(1)} %get-tuple-element.28.refs_5_), channel_id=1, source_target_pairs={{0,2},{2,0},{1,3},{3,1},{4,6},{6,4},{5,7},{7,5},{8,10},{10,8},{9,1... | collective-permute-start | bytes 1493000 | tf_op jit(solution)/shard_map/ppermute | solution.py:51
  27.5 29.9 %collective-permute-start.5 = (bf16[216,1152]{1,0:T(8,128)(2,1)}, bf16[216,1152]{1,0:T(8,128)(2,1)}, u32[]{:S(2)}, u32[]{:S(2)}) collective-permute-start(bf16[216,1152]{1,0:T(8,128)(2,1)} %collective-permute-done.4.refs_7_), channel_id=1, source_target_pairs={{0,2},{2,0},{1,3},{3,1},{4,6},{6,4},{5,7},{7,5},{8,10},{10,8},{9,1... | collective-permute-start | bytes 1493000 | tf_op jit(solution)/shard_map/ppermute | solution.py:51
  27.5 19.1 %collective-permute-start = (bf16[192,1152]{1,0:T(8,128)(2,1)S(1)}, bf16[192,1152]{1,0:T(8,128)(2,1)S(1)}, u32[]{:S(2)}, u32[]{:S(2)}) collective-permute-start(bf16[192,1152]{1,0:T(8,128)(2,1)S(1)} %get-tuple-element.27.refs_1_), channel_id=1, source_target_pairs={{0,4},{4,8},{8,12},{12,0},{1,5},{5,9},{9,13},{13,1},{2,6},{6,10},{... | collective-permute-start | bytes 1327112 | tf_op jit(solution)/shard_map/ppermute | solution.py:46
  29.9 27.4 %collective-permute-start.1 = (bf16[192,1152]{1,0:T(8,128)(2,1)S(1)}, bf16[192,1152]{1,0:T(8,128)(2,1)}, u32[]{:S(2)}, u32[]{:S(2)}) collective-permute-start(bf16[192,1152]{1,0:T(8,128)(2,1)S(1)} %get-tuple-element.27.refs_1_), channel_id=1, source_target_pairs={{0,8},{4,12},{8,0},{12,4},{1,9},{5,13},{9,1},{13,5},{2,10},{6,14},... | collective-permute-start | bytes 1327112 | tf_op jit(solution)/shard_map/ppermute | solution.py:46
  37.2 20.1 %collective-permute-start.2 = (bf16[192,1152]{1,0:T(8,128)(2,1)S(1)}, bf16[192,1152]{1,0:T(8,128)(2,1)}, u32[]{:S(2)}, u32[]{:S(2)}) collective-permute-start(bf16[192,1152]{1,0:T(8,128)(2,1)S(1)} %get-tuple-element.27.refs_1_), channel_id=1, source_target_pairs={{0,12},{4,0},{8,4},{12,8},{1,13},{5,1},{9,5},{13,9},{2,14},{6,2},{... | collective-permute-start | bytes 1327112 | tf_op jit(solution)/shard_map/ppermute | solution.py:46
  46.5 12.7 %copy-start.33 = (bf16[192,1152]{1,0:T(8,128)(2,1)}, bf16[192,1152]{1,0:T(8,128)(2,1)S(1)}, u32[]{:S(2)}) copy-start(bf16[192,1152]{1,0:T(8,128)(2,1)S(1)} %collective-permute-done.refs_2_) | copy-start | bytes 1327108
  59.2 43.1 %all-to-all-start.1 = ((bf16[32,32,512]{2,1,0:T(8,128)(2,1)}), bf16[32,32,512]{2,1,0:T(8,128)(2,1)S(1)}, u32[]{:S(2)}, u32[]{:S(2)}) async-start(bf16[32,32,512]{2,1,0:T(8,128)(2,1)} %embed_sum.1), calls=%async_computation.1 | async-start | bytes 2097152 | tf_op jit(solution)/shard_map/all_to_all | solution.py:41
  67.5 32.3 %copy-start.9 = (bf16[36,1152]{1,0:T(8,128)(2,1)S(1)}, bf16[36,1152]{1,0:T(8,128)(2,1)}, u32[]{:S(2)}) copy-start(bf16[36,1152]{1,0:T(8,128)(2,1)} %refs_0_.1) | copy-start | bytes 248836
  67.5 32.3 %copy-start.10 = (bf16[36,1152]{1,0:T(8,128)(2,1)S(1)}, bf16[36,1152]{1,0:T(8,128)(2,1)}, u32[]{:S(2)}) copy-start(bf16[36,1152]{1,0:T(8,128)(2,1)} %refs_1_.3) | copy-start | bytes 248836
  67.5 32.3 %copy-start.11 = (bf16[36,1152]{1,0:T(8,128)(2,1)S(1)}, bf16[36,1152]{1,0:T(8,128)(2,1)}, u32[]{:S(2)}) copy-start(bf16[36,1152]{1,0:T(8,128)(2,1)} %refs_2_.3) | copy-start | bytes 248836
  67.5 34.8 %copy-start.12 = (s32[5]{0:T(128)S(1)}, s32[5]{0:T(128)}, u32[]{:S(2)}) copy-start(s32[5]{0:T(128)} %stack.23.refs_0_.at_ref) | copy-start | bytes 64
  67.5 34.8 %copy-start.18 = (bf16[512,320]{0,1:T(8,128)(2,1)S(1)}, bf16[512,320]{0,1:T(8,128)(2,1)}, u32[]{:S(2)}) copy-start(bf16[512,320]{0,1:T(8,128)(2,1)} %param.21) | copy-start | bytes 983044
  67.5 34.8 %copy-start.19 = (bf16[512,320]{0,1:T(8,128)(2,1)S(1)}, bf16[512,320]{0,1:T(8,128)(2,1)}, u32[]{:S(2)}) copy-start(bf16[512,320]{0,1:T(8,128)(2,1)} %param.22) | copy-start | bytes 983044
  67.5 34.8 %copy-start.20 = (f32[512]{0:T(512)S(1)}, f32[512]{0:T(512)}, u32[]{:S(2)}) copy-start(f32[512]{0:T(512)} %param.20) | copy-start | bytes 6148
  67.6 192.1 %all-gather.2.cloned.1.call-start = ((), (), s32[]{:S(2)}) async-start(), calls=%async_computation.7 | async-start | bytes 8460288 | tf_op jit(solution)/shard_map/all_gather | solution.py:575
  73.4 16.6 %collective-permute-start.6 = (bf16[240,768]{1,0:T(8,128)(2,1)}, bf16[240,768]{1,0:T(8,128)(2,1)S(1)}, u32[]{:S(2)}, u32[]{:S(2)}) collective-permute-start(bf16[240,768]{1,0:T(8,128)(2,1)} %get-tuple-element.30), channel_id=1, source_target_pairs={{0,1},{1,0},{16,17},{17,16},{2,3},{3,2},{18,19},{19,18},{4,5},{5,4... | collective-permute-start | bytes 1105928 | tf_op jit(solution)/shard_map/ppermute | solution.py:51
  75.1 23.9 %collective-permute-start.7 = (bf16[240,768]{1,0:T(8,128)(2,1)}, bf16[240,768]{1,0:T(8,128)(2,1)S(1)}, u32[]{:S(2)}, u32[]{:S(2)}) collective-permute-start(bf16[240,768]{1,0:T(8,128)(2,1)} %get-tuple-element.31), channel_id=1, source_target_pairs={{0,16},{1,17},{16,0},{17,1},{2,18},{3,19},{18,2},{19,3},{4,20},{5,... | collective-permute-start | bytes 1105928 | tf_op jit(solution)/shard_map/ppermute | solution.py:51
  77.8 22.0 %collective-permute-start.8 = (bf16[240,768]{1,0:T(8,128)(2,1)}, bf16[240,768]{1,0:T(8,128)(2,1)S(1)}, u32[]{:S(2)}, u32[]{:S(2)}) collective-permute-start(bf16[240,768]{1,0:T(8,128)(2,1)} %get-tuple-element.32), channel_id=1, source_target_pairs={{0,17},{1,16},{16,1},{17,0},{2,19},{3,18},{18,3},{19,2},{4,21},{5,... | collective-permute-start | bytes 1105928 | tf_op jit(solution)/shard_map/ppermute | solution.py:51
  78.1 22.4 %collective-permute-start.9 = (bf16[240,768]{1,0:T(8,128)(2,1)}, bf16[240,768]{1,0:T(8,128)(2,1)S(1)}, u32[]{:S(2)}, u32[]{:S(2)}) collective-permute-start(bf16[240,768]{1,0:T(8,128)(2,1)} %get-tuple-element.29.refs_1_), channel_id=1, source_target_pairs={{0,2},{2,0},{1,3},{3,1},{4,6},{6,4},{5,7},{7,5},{8,10},{10,8},{9,1... | collective-permute-start | bytes 1105928 | tf_op jit(solution)/shard_map/ppermute | solution.py:51
  90.0 11.5 %copy-start.26 = (bf16[240,768]{1,0:T(8,128)(2,1)}, bf16[240,768]{1,0:T(8,128)(2,1)S(1)}, u32[]{:S(2)}) copy-start(bf16[240,768]{1,0:T(8,128)(2,1)S(1)} %collective-permute-done.6.refs_2_) | copy-start | bytes 1105924
  90.0 10.5 %collective-permute-start.10 = (bf16[240,768]{1,0:T(8,128)(2,1)S(1)}, bf16[240,768]{1,0:T(8,128)(2,1)S(1)}, u32[]{:S(2)}, u32[]{:S(2)}) collective-permute-start(bf16[240,768]{1,0:T(8,128)(2,1)S(1)} %collective-permute-done.6.refs_2_), channel_id=1, source_target_pairs={{0,2},{2,0},{1,3},{3,1},{4,6},{6,4},{5,7},{7,5},{8,10},{10,8},{9,1... | collective-permute-start | bytes 1105928 | tf_op jit(solution)/shard_map/ppermute | solution.py:51
  99.0 1.7 collective-permute-start.11
  99.8 1.7 collective-permute-start.12
  99.9 9.1 %collective-permute-start.19 = (bf16[36,3456]{1,0:T(8,128)(2,1)S(1)}, bf16[36,3456]{1,0:T(8,128)(2,1)S(1)}, u32[]{:S(2)}, u32[]{:S(2)}) collective-permute-start(bf16[36,3456]{1,0:T(8,128)(2,1)S(1)} %side_weights.1.refs_1_), channel_id=1, source_target_pairs={{0,1},{1,0},{2,3},{3,2},{4,5},{5,4},{6,7},{7,6},{8,9},{9,8},{10,11... | collective-permute-start | bytes 746504 | tf_op jit(solution)/shard_map/ppermute | solution.py:51
  110.5 75.6 %all-to-all-start.2 = ((bf16[8,136,640]{2,1,0:T(8,128)(2,1)}), bf16[8,136,640]{2,1,0:T(8,128)(2,1)S(1)}, u32[]{:S(2)}, u32[]{:S(2)}) async-start(bf16[8,136,640]{2,1,0:T(8,128)(2,1)} %copy-done.3), calls=%async_computation.2 | async-start | bytes 2785280 | tf_op jit(solution)/shard_map/all_to_all | solution.py:41
  190.5 9.4 %copy-start.34 = (bf16[4,72,192]{2,1,0:T(8,128)(2,1)S(1)}, bf16[4,72,192]{2,1,0:T(8,128)(2,1)}, u32[]{:S(2)}) copy-start(bf16[4,72,192]{2,1,0:T(8,128)(2,1)} %get-tuple-element.37) | copy-start | bytes 331780
  190.5 23.4 %copy-start.5 = (bf16[128,1152]{1,0:T(8,128)(2,1)S(1)}, bf16[128,1152]{1,0:T(8,128)(2,1)}, u32[]{:S(2)}) copy-start(bf16[128,1152]{1,0:T(8,128)(2,1)} %refs_2_.2) | copy-start | bytes 884740
  190.5 23.4 %copy-start.15 = (f32[128]{0:T(128)S(1)}, f32[128]{0:T(128)}, u32[]{:S(2)}) copy-start(f32[128]{0:T(128)} %param.24) | copy-start | bytes 1540
  190.5 27.5 %copy-start.7 = (bf16[4,72,192]{2,1,0:T(8,128)(2,1)S(1)}, bf16[4,72,192]{2,1,0:T(8,128)(2,1)}, u32[]{:S(2)}) copy-start(bf16[4,72,192]{2,1,0:T(8,128)(2,1)} %get-tuple-element.34.refs_0_) | copy-start | bytes 331780
  190.5 31.0 %copy-start.25 = (f32[1152]{0:T(1024)S(1)}, f32[1152]{0:T(1024)}, u32[]{:S(2)}) copy-start(f32[1152]{0:T(1024)} %param.26) | copy-start | bytes 13828
  190.6 23.4 %all-to-all-start.3 = ((bf16[32,136,128]{2,1,0:T(8,128)(2,1)}), bf16[32,136,128]{2,1,0:T(8,128)(2,1)S(1)}, u32[]{:S(2)}, u32[]{:S(2)}) async-start(bf16[32,136,128]{2,1,0:T(8,128)(2,1)} %text_down.1), calls=%async_computation.3 | async-start | bytes 2228224 | tf_op jit(solution)/shard_map/all_to_all | solution.py:41
  195.3 57.4 %copy-start.6 = (bf16[1152,72]{0,1:T(8,128)(2,1)S(1)}, bf16[1152,72]{0,1:T(8,128)(2,1)}, u32[]{:S(2)}) copy-start(bf16[1152,72]{0,1:T(8,128)(2,1)} %param.32) | copy-start | bytes 497668
  195.4 19.7 %collective-permute-start.13 = (bf16[4,72,192]{2,1,0:T(8,128)(2,1)}, bf16[4,72,192]{2,1,0:T(8,128)(2,1)S(1)}, u32[]{:S(2)}, u32[]{:S(2)}) collective-permute-start(bf16[4,72,192]{2,1,0:T(8,128)(2,1)} %get-tuple-element.35), channel_id=1, source_target_pairs={{0,1},{1,0},{16,17},{17,16},{2,3},{3,2},{18,19},{19,18},{4,5},{5,4... | collective-permute-start | bytes 331784 | tf_op jit(solution)/shard_map/ppermute | solution.py:51
  197.2 20.8 %collective-permute-start.14 = (bf16[4,72,192]{2,1,0:T(8,128)(2,1)}, bf16[4,72,192]{2,1,0:T(8,128)(2,1)S(1)}, u32[]{:S(2)}, u32[]{:S(2)}) collective-permute-start(bf16[4,72,192]{2,1,0:T(8,128)(2,1)} %get-tuple-element.36), channel_id=1, source_target_pairs={{0,16},{1,17},{16,0},{17,1},{2,18},{3,19},{18,2},{19,3},{4,20},{5,... | collective-permute-start | bytes 331784 | tf_op jit(solution)/shard_map/ppermute | solution.py:51
  199.9 18.1 %collective-permute-start.15 = (bf16[4,72,192]{2,1,0:T(8,128)(2,1)S(1)}, bf16[4,72,192]{2,1,0:T(8,128)(2,1)S(1)}, u32[]{:S(2)}, u32[]{:S(2)}) collective-permute-start(bf16[4,72,192]{2,1,0:T(8,128)(2,1)S(1)} %copy-done.34), channel_id=1, source_target_pairs={{0,17},{1,16},{16,1},{17,0},{2,19},{3,18},{18,3},{19,2},{4,21},{5,... | collective-permute-start | bytes 331784 | tf_op jit(solution)/shard_map/ppermute | solution.py:51
  218.7 9.1 %collective-permute-start.18 = (bf16[4,72,192]{2,1,0:T(8,128)(2,1)S(1)}, bf16[4,72,192]{2,1,0:T(8,128)(2,1)S(1)}, u32[]{:S(2)}, u32[]{:S(2)}) collective-permute-start(bf16[4,72,192]{2,1,0:T(8,128)(2,1)S(1)} %get-tuple-element.44), channel_id=1, source_target_pairs={{0,12},{4,0},{8,4},{12,8},{1,13},{5,1},{9,5},{13,9},{2,14},{6,2},{... | collective-permute-start | bytes 331784 | tf_op jit(solution)/shard_map/ppermute | solution.py:46
  221.6 8.3 %collective-permute-start.17 = (bf16[4,72,192]{2,1,0:T(8,128)(2,1)S(1)}, bf16[4,72,192]{2,1,0:T(8,128)(2,1)S(1)}, u32[]{:S(2)}, u32[]{:S(2)}) collective-permute-start(bf16[4,72,192]{2,1,0:T(8,128)(2,1)S(1)} %get-tuple-element.43), channel_id=1, source_target_pairs={{0,8},{4,12},{8,0},{12,4},{1,9},{5,13},{9,1},{13,5},{2,10},{6,14},... | collective-permute-start | bytes 331784 | tf_op jit(solution)/shard_map/ppermute | solution.py:46
  222.4 20.4 %collective-permute-start.16 = (bf16[4,72,192]{2,1,0:T(8,128)(2,1)S(1)}, bf16[4,72,192]{2,1,0:T(8,128)(2,1)S(1)}, u32[]{:S(2)}, u32[]{:S(2)}) collective-permute-start(bf16[4,72,192]{2,1,0:T(8,128)(2,1)S(1)} %get-tuple-element.42), channel_id=1, source_target_pairs={{0,4},{4,8},{8,12},{12,0},{1,5},{5,9},{9,13},{13,1},{2,6},{6,10},{... | collective-permute-start | bytes 331784 | tf_op jit(solution)/shard_map/ppermute | solution.py:46
  223.1 14.9 %all-to-all-start.4 = ((bf16[32,4,1280]{2,1,0:T(4,128)(2,1)}), bf16[32,4,1280]{2,1,0:T(4,128)(2,1)S(1)}, u32[]{:S(2)}, u32[]{:S(2)}) async-start(bf16[32,4,1280]{2,1,0:T(4,128)(2,1)} %get-tuple-element.47), calls=%async_computation.4 | async-start | bytes 655360 | tf_op jit(solution)/shard_map/all_to_all | solution.py:41
  227.8 31.9 %copy-start.22 = (bf16[4,72,192]{2,1,0:T(8,128)(2,1)}, bf16[4,72,192]{2,1,0:T(8,128)(2,1)S(1)}, u32[]{:S(2)}) copy-start(bf16[4,72,192]{2,1,0:T(8,128)(2,1)S(1)} %collective-permute-done.18.refs_3_) | copy-start | bytes 331780
  229.9 29.9 %copy-start.23 = (bf16[4,72,192]{2,1,0:T(8,128)(2,1)}, bf16[4,72,192]{2,1,0:T(8,128)(2,1)S(1)}, u32[]{:S(2)}) copy-start(bf16[4,72,192]{2,1,0:T(8,128)(2,1)S(1)} %collective-permute-done.17.refs_2_) | copy-start | bytes 331780
  238.9 13.8 %all-to-all-start.5 = ((bf16[32,4,1152]{2,1,0:T(4,128)(2,1)}), bf16[32,4,1152]{2,1,0:T(4,128)(2,1)S(1)}, u32[]{:S(2)}, u32[]{:S(2)}) async-start(bf16[32,4,1152]{2,1,0:T(4,128)(2,1)} %caption.1), calls=%async_computation.5 | async-start | bytes 589824 | tf_op jit(solution)/shard_map/all_to_all | solution.py:41
  242.8 16.9 %copy-start.24 = (bf16[4,72,192]{2,1,0:T(8,128)(2,1)}, bf16[4,72,192]{2,1,0:T(8,128)(2,1)S(1)}, u32[]{:S(2)}) copy-start(bf16[4,72,192]{2,1,0:T(8,128)(2,1)S(1)} %collective-permute-done.16.refs_1_) | copy-start | bytes 331780
  253.9 16.9 %all-to-all-start.6 = ((bf16[32,72,128]{2,1,0:T(8,128)(2,1)}), bf16[32,72,128]{2,1,0:T(8,128)(2,1)S(1)}, u32[]{:S(2)}, u32[]{:S(2)}) async-start(bf16[32,72,128]{2,1,0:T(8,128)(2,1)} %text_kv.1), calls=%async_computation.6 | async-start | bytes 1179648 | tf_op jit(solution)/shard_map/all_to_all | solution.py:41
  (15 other events, 27.3 us)
Sparse Core Ops, SparseCore 0:
  110.6 75.8 all-gather.1

commit v2 on v1

--- a/solution.py
+++ b/solution.py
@@ -130,7 +130,14 @@
     return jnp.broadcast_to(row, (128, row.shape[1])).T[:, :1]
 
 
-def gate_up_kernel(at_ref, in_ref, gain_ref, gate_ref, up_ref, out_ref, weight, rows32):
+def gate_up_kernel(
+    at_ref, in_ref, gain_ref, gate_ref, up_ref, side_ref, other_ref, out_ref, pair_ref, weight, rows32
+):
+    own, other = side_ref[...].astype(F32), other_ref[...].astype(F32)
+    first = at_ref[2] == 0
+    pair_ref[...] = jnp.concatenate(
+        [jnp.where(first, own, other), jnp.where(first, other, own)], axis=0
+    ).astype(BF16)
     prompts, _, both = out_ref.shape
     plane, group, feats = in_ref.shape
     tokens = plane * group // prompts
@@ -252,14 +259,6 @@
         out_ref[:, k * W : (k + 1) * W] = ref[...]
 
 
-def pair_kernel(at_ref, own_ref, other_ref, out_ref):
-    own, other = own_ref[...].astype(F32), other_ref[...].astype(F32)
-    first = at_ref[2] == 0
-    out_ref[...] = jnp.concatenate(
-        [jnp.where(first, own, other), jnp.where(first, other, own)], axis=0
-    ).astype(BF16)
-
-
 def qkv_kernel(at_ref, *refs):
     tokens, weights = refs[:4], refs[4:8]
     fulls = refs[8:12]
@@ -456,7 +455,7 @@
         + [third(0), third(1), whole(img.shape), whole(gate.shape)],
         out_specs=[whole((rows, W))] * 2,
         scratch_shapes=[pltpu.VMEM((W, rows), F32)],
-        compiler_params=grant(56),
+        compiler_params=grant(24),
         cost_estimate=pl.CostEstimate(
             flops=4 * rows * W * W, bytes_accessed=8 << 20, transcendentals=0
         ),
@@ -473,7 +472,7 @@
         in_specs=[SMEM, whole(cq.shape), whole(after.shape), whole(kv.shape), third(2)],
         out_specs=whole((rows, W)),
         scratch_shapes=[pltpu.VMEM((W, rows), F32)],
-        compiler_params=grant(56),
+        compiler_params=grant(16),
         cost_estimate=pl.CostEstimate(
             flops=4 * rows * W * W, bytes_accessed=5 << 20, transcendentals=rows * LT * HEADS
         ),
@@ -549,28 +548,29 @@
         "embed_sum",
         shape(picked.shape),
         (picked,),
-        after=(tie(*token_blocks[1:], *weight_blocks[1:]),),
-    )
-    gate_up, tick = call(
+        after=(tie(*token_blocks[1:], *weight_blocks[1:3]),),
+    )
+    side = call(side_kernel, "side_weights", shape((w_out.shape[0], 3 * W)), (w_out, w_cq, w_co))
+    gate_up, pair, tick = call(
         gate_up_kernel,
         "text_gate_up",
-        [shape((prompts, tokens + 2 * share, 2 * units))],
-        (at, exchange(embedded, PLANE), ff_gain.reshape(1, feats), wi_gate.T, wi_up.T),
+        [shape((prompts, tokens + 2 * share, 2 * units)), shape((HEAD, 3 * W))],
+        (
+            at,
+            exchange(embedded, PLANE),
+            ff_gain.reshape(1, feats),
+            wi_gate.T,
+            wi_up.T,
+            side,
+            crossed(side, "tp", 1),
+        ),
         scratch=[pltpu.VMEM((feats, 2 * units), BF16), pltpu.VMEM((tokens, feats), F32)],
-        in_specs=[SMEM] + [VMEM] * 4,
+        in_specs=[SMEM] + [VMEM] * 6,
         flops=4 * prompts * tokens * feats * units,
         moved=4 << 20,
         after=(tie(*fulls[1:], *others),),
         tick=True,
-    )
-    side = call(side_kernel, "side_weights", shape((w_out.shape[0], 3 * W)), (w_out, w_cq, w_co))
-    pair = call(
-        pair_kernel,
-        "side_pair",
-        shape((HEAD, 3 * W)),
-        (at, side, crossed(side, "tp", 1)),
-        in_specs=[SMEM, VMEM, VMEM],
-        after=(tick,),
+        mib=20,
     )
     side = lax.all_gather(pair, SEQ, axis=0, tiled=True)
     *found, attended = call(
@@ -605,28 +605,24 @@
         exps=tokens * units,
         after=(attended,),
     )
-    cap_part, tick = call(
+    cap_part = call(
         cap_kernel,
         "caption_partial",
-        [shape((plane, share, W + 128))],
+        shape((plane, share, W + 128)),
         (exchange(down, PLANE), final_gain.reshape(1, width), cap_weight),
         scratch=[pltpu.VMEM((tokens, width), F32), pltpu.VMEM((tokens, W + 128), F32)],
-        tick=True,
-    )
-    *grouped, tick = call(
+    )
+    grouped = call(
         regroup_kernel,
         "regroup",
         [shape((4, HEAD, rows))] * 4,
         tuple(found),
-        after=(tick,),
-        tick=True,
     )
     caption = call(
         caption_kernel,
         "caption",
         shape((plane, share, W)),
         (exchange(cap_part, PLANE), cap_bias.reshape(1, W)),
-        after=(tick,),
     )
     parts = [grouped[0]] + [shifted(grouped[d], "x", d) for d in range(1, 4)]
     after_self, cross_query = project(at, parts, side, pixels, modulate[2:3])

time: 286 us -> 284 us (level)
  starting transfers between devices: 68.6 us -> 62.4 us
  waiting for transfers between devices: 92.8 us -> 97.5 us
  Pallas kernels: 95.2 us -> 90.8 us
  local copies, waits for them, and re-layouts: 10.7 us -> 14.5 us
    ppermute x14, waiting for transfers between devices: 35.2 us -> 63.7 us  [crossed(): return lax.ppermute(value, axis, [(i, i ^ mask) for i in range(size)])]
    all_to_all x7, waiting for transfers between devices: 37.5 us -> 25.3 us  [exchange(): return lax.all_to_all(blocks, axes, 0, 0, tiled=True)]
    ppermute x6, waiting for transfers between devices: 20.1 us -> 8.48 us  [shifted(): lax.ppermute(value, axis, [(i, (i + shift) % size) for i in range(size)])]
    ppermute x6, starting transfers between devices: 15.5 us -> 10 us  [shifted(): lax.ppermute(value, axis, [(i, (i + shift) % size) for i in range(size)])]
    unnamed x71 -> x69, local copies, waits for them, and re-layouts: 8.74 us -> 13.2 us
    pallas_call x1, Pallas kernels: 5.23 us -> 2.12 us  [project(): pl.pallas_call(project_kernel, grid=(1,), out_shape=[shape((rows, W))] *...]
    pallas_call x12 -> x11, Pallas kernels: 82.9 us -> 83.9 us  [call(): pl.pallas_call(body, out_shape=outs if many else outs[0], in_specs=(in_sp...]
  transfers between devices with their start and end apart: 28 -> 28, of which waited for: 15 -> 14; matrix products, arithmetic and copies ran while one was open for 2% -> 1% of each run, Pallas kernels for 30% -> 29%
where the time goes in v2:
time: 284 us; the launch traced here: 283 us
  waiting for transfers between devices  97.5 us (34%)
  Pallas kernels  90.8 us (32%)
  starting transfers between devices  62.4 us (22%)
  local copies, waits for them, and re-layouts  14.5 us (5%)
  between operations  14.4 us (5%)
    pallas_call x11, Pallas kernels, call(): pl.pallas_call(body, out_shape=outs if many else outs[0], in_specs=(in_sp...  83.9 us
    ppermute x14, waiting for transfers between devices, crossed(): return lax.ppermute(value, axis, [(i, i ^ mask) for i in range(size)])  63.7 us
    all_to_all x7, starting transfers between devices, exchange(): return lax.all_to_all(blocks, axes, 0, 0, tiled=True)  38.8 us
    all_to_all x7, waiting for transfers between devices, exchange(): return lax.all_to_all(blocks, axes, 0, 0, tiled=True)  25.3 us
    ppermute x14, starting transfers between devices, crossed(): return lax.ppermute(value, axis, [(i, i ^ mask) for i in range(size)])  13.5 us
    unnamed x69, local copies, waits for them, and re-layouts  13.2 us
    ppermute x6, starting transfers between devices, shifted(): lax.ppermute(value, axis, [(i, (i + shift) % size) for i in range(size)])  10 us
    ppermute x6, waiting for transfers between devices, shifted(): lax.ppermute(value, axis, [(i, (i + shift) % size) for i in range(size)])  8.48 us
  transfers between devices with their start and end apart: 28, of which 14 were waited for; matrix products, arithmetic and copies ran while one was open for 1% of the time, Pallas kernels for 29%

profile of v2, /device:TPU:32, one launch (start us, length us, event | category | flops | bytes accessed | tf_op | source)
XLA Modules:
  0.0 283.4 jit_solution(12924579259999872929)
XLA Ops:
  6.5 0.8 subtract_bitcast_fusion
  7.8 2.3 fusion.2
  10.1 7.5 %all-to-all-start = ((bf16[32,32,512]{2,1,0:T(8,128)(2,1)}), bf16[32,32,512]{2,1,0:T(8,128)(2,1)S(1)}, u32[]{:S(2)}, u32[]{:S(2)}) async-start(bf16[32,32,512]{2,1,0:T(8,128)(2,1)} %bitcast.37), calls=%async_computation | async-start | bytes 2097152 | tf_op jit(solution)/shard_map/all_to_all | solution.py:41
  17.6 1.1 modulate.1
  18.7 3.3 %collective-permute-start.4 = (bf16[216,1152]{1,0:T(8,128)(2,1)S(1)}, bf16[216,1152]{1,0:T(8,128)(2,1)}, u32[]{:S(2)}, u32[]{:S(2)}) collective-permute-start(bf16[216,1152]{1,0:T(8,128)(2,1)S(1)} %get-tuple-element.26.refs_5_), channel_id=1, source_target_pairs={{0,16},{16,0},{1,17},{17,1},{2,18},{18,2},{3,19},{19,3},{4,20},{20... | collective-permute-start | bytes 1493000 | tf_op jit(solution)/shard_map/ppermute | solution.py:51
  22.0 1.5 collective-permute-start
  23.5 2.7 collective-permute-start.1
  26.2 1.4 collective-permute-start.2
  27.7 16.5 %collective-permute-done.4.refs_7_ = bf16[216,1152]{1,0:T(8,128)(2,1)} collective-permute-done((bf16[216,1152]{1,0:T(8,128)(2,1)S(1)}, bf16[216,1152]{1,0:T(8,128)(2,1)}, u32[]{:S(2)}, u32[]{:S(2)}) %collective-permute-start.4) | collective-permute-done | bytes 497696 | tf_op jit(solution)/shard_map/ppermute | solution.py:51
  44.8 7.4 %collective-permute-done.1.refs_3_ = bf16[192,1152]{1,0:T(8,128)(2,1)} collective-permute-done((bf16[192,1152]{1,0:T(8,128)(2,1)}, bf16[192,1152]{1,0:T(8,128)(2,1)}, u32[]{:S(2)}, u32[]{:S(2)}) %collective-permute-start.1) | collective-permute-done | bytes 442400 | tf_op jit(solution)/shard_map/ppermute | solution.py:46
  52.9 1.2 embed_sum.1
  54.2 5.4 %all-to-all-start.1 = ((bf16[32,32,512]{2,1,0:T(8,128)(2,1)}), bf16[32,32,512]{2,1,0:T(8,128)(2,1)S(1)}, u32[]{:S(2)}, u32[]{:S(2)}) async-start(bf16[32,32,512]{2,1,0:T(8,128)(2,1)} %embed_sum.1), calls=%async_computation.1 | async-start | bytes 2097152 | tf_op jit(solution)/shard_map/all_to_all | solution.py:41
  59.7 5.7 %query_key_value.1 = (bf16[240,768]{1,0:T(8,128)(2,1)}, bf16[240,768]{1,0:T(8,128)(2,1)}, bf16[240,768]{1,0:T(8,128)(2,1)}, bf16[240,768]{1,0:T(8,128)(2,1)}) custom-call(s32[5]{0:T(128)} %stack.23.refs_0_.at_ref, bf16[192,1152]{1,0:T(8,128)(2,1)} %get-tuple-element.25.refs_1_, bf16[192,1152]{1,0:T(8,128)(2,1)} %copy-done.31, ...), custom_call_target="tpu_custom_call" | custom-call | flops 1528823808 | bytes 8388608 | tf_op jit(solution)/shard_map/query_key_value/pallas_call | solution.py:93
  65.5 1.8 collective-permute-start.6
  67.3 2.7 collective-permute-start.7
  70.2 11.9 %collective-permute-done.6.refs_2_ = bf16[240,768]{1,0:T(8,128)(2,1)S(1)} collective-permute-done((bf16[240,768]{1,0:T(8,128)(2,1)}, bf16[240,768]{1,0:T(8,128)(2,1)S(1)}, u32[]{:S(2)}, u32[]{:S(2)}) %collective-permute-start.6) | collective-permute-done | bytes 368672 | tf_op jit(solution)/shard_map/ppermute | solution.py:51
  82.1 9.0 %collective-permute-done.7.refs_3_ = bf16[240,768]{1,0:T(8,128)(2,1)S(1)} collective-permute-done((bf16[240,768]{1,0:T(8,128)(2,1)}, bf16[240,768]{1,0:T(8,128)(2,1)S(1)}, u32[]{:S(2)}, u32[]{:S(2)}) %collective-permute-start.7) | collective-permute-done | bytes 368672 | tf_op jit(solution)/shard_map/ppermute | solution.py:51
  94.4 6.7 %collective-permute-done.13.refs_6_ = bf16[36,3456]{1,0:T(8,128)(2,1)S(1)} collective-permute-done((bf16[36,3456]{1,0:T(8,128)(2,1)S(1)}, bf16[36,3456]{1,0:T(8,128)(2,1)S(1)}, u32[]{:S(2)}, u32[]{:S(2)}) %collective-permute-start.13) | collective-permute-done | bytes 248864 | tf_op jit(solution)/shard_map/ppermute | solution.py:51
  101.1 1.0 copy-done.19
  102.1 2.8 text_gate_up.1
  104.9 1.1 copy-done.5
  106.0 8.6 %all-to-all-start.2 = ((bf16[8,136,640]{2,1,0:T(8,128)(2,1)}), bf16[8,136,640]{2,1,0:T(8,128)(2,1)S(1)}, u32[]{:S(2)}, u32[]{:S(2)}) async-start(bf16[8,136,640]{2,1,0:T(8,128)(2,1)} %copy-done.5), calls=%async_computation.2 | async-start | bytes 2785280 | tf_op jit(solution)/shard_map/all_to_all | solution.py:41
  114.6 67.0 %self_attention.1 = (bf16[4,72,192]{2,1,0:T(8,128)(2,1)}, bf16[4,72,192]{2,1,0:T(8,128)(2,1)}, bf16[4,72,192]{2,1,0:T(8,128)(2,1)}, bf16[4,72,192]{2,1,0:T(8,128)(2,1)}, f32[8,128]{1,0:T(8,128)}) custom-call(s32[5]{0:T(128)} %stack.23.refs_0_.at_ref, bf16[240,768]{1,0:T(8,128)(2,1)} %get-tuple-element.27.refs_1_, bf16[240,768]{1,0:T(8,128)(2,1)} %copy-done.24, ...), custom_call_target="tpu_custom_call" | custom-call | flops 9663676416 | bytes 8388608 | tf_op jit(solution)/shard_map/self_attention/pallas_call | solution.py:93
  181.6 1.7 copy-done.3
  184.0 2.0 text_down.1
  186.0 4.8 %all-to-all-start.3 = ((bf16[32,136,128]{2,1,0:T(8,128)(2,1)}), bf16[32,136,128]{2,1,0:T(8,128)(2,1)S(1)}, u32[]{:S(2)}, u32[]{:S(2)}) async-start(bf16[32,136,128]{2,1,0:T(8,128)(2,1)} %text_down.1), calls=%async_computation.3 | async-start | bytes 2228224 | tf_op jit(solution)/shard_map/all_to_all | solution.py:41
  190.8 1.9 collective-permute-start.14
  192.7 2.7 collective-permute-start.15
  195.7 13.6 %collective-permute-done.14.refs_1_ = bf16[4,72,192]{2,1,0:T(8,128)(2,1)S(1)} collective-permute-done((bf16[4,72,192]{2,1,0:T(8,128)(2,1)}, bf16[4,72,192]{2,1,0:T(8,128)(2,1)S(1)}, u32[]{:S(2)}, u32[]{:S(2)}) %collective-permute-start.14) | collective-permute-done | bytes 110624 | tf_op jit(solution)/shard_map/ppermute | solution.py:51
  209.3 4.2 %collective-permute-done.15.refs_2_ = bf16[4,72,192]{2,1,0:T(8,128)(2,1)S(1)} collective-permute-done((bf16[4,72,192]{2,1,0:T(8,128)(2,1)S(1)}, bf16[4,72,192]{2,1,0:T(8,128)(2,1)S(1)}, u32[]{:S(2)}, u32[]{:S(2)}) %collective-permute-start.15) | collective-permute-done | bytes 110624 | tf_op jit(solution)/shard_map/ppermute | solution.py:51
  213.5 0.8 regroup.1
  214.3 2.8 %collective-permute-start.19 = (bf16[4,72,192]{2,1,0:T(8,128)(2,1)}, bf16[4,72,192]{2,1,0:T(8,128)(2,1)S(1)}, u32[]{:S(2)}, u32[]{:S(2)}) collective-permute-start(bf16[4,72,192]{2,1,0:T(8,128)(2,1)} %get-tuple-element.39), channel_id=1, source_target_pairs={{0,12},{4,0},{8,4},{12,8},{1,13},{5,1},{9,5},{13,9},{2,14},{6,2},{... | collective-permute-start | bytes 331784 | tf_op jit(solution)/shard_map/ppermute | solution.py:46
  217.1 0.8 collective-permute-start.18
  218.7 1.1 caption_partial.1
  219.8 4.8 %all-to-all-start.4 = ((bf16[32,4,1280]{2,1,0:T(4,128)(2,1)}), bf16[32,4,1280]{2,1,0:T(4,128)(2,1)S(1)}, u32[]{:S(2)}, u32[]{:S(2)}) async-start(bf16[32,4,1280]{2,1,0:T(4,128)(2,1)} %caption_partial.1), calls=%async_computation.4 | async-start | bytes 655360 | tf_op jit(solution)/shard_map/all_to_all | solution.py:41
  224.6 1.0 collective-permute-done.18.refs_2_
  225.6 9.2 %all-to-all-done.4.refs_0_ = bf16[32,4,1280]{2,1,0:T(4,128)(2,1)S(1)} async-done(((bf16[32,4,1280]{2,1,0:T(4,128)(2,1)}), bf16[32,4,1280]{2,1,0:T(4,128)(2,1)S(1)}, u32[]{:S(2)}, u32[]{:S(2)}) %all-to-all-start.4) | async-done | bytes 327712 | tf_op jit(solution)/shard_map/all_to_all | solution.py:41
  234.8 0.9 caption.1
  235.8 3.9 %all-to-all-start.5 = ((bf16[32,4,1152]{2,1,0:T(4,128)(2,1)}), bf16[32,4,1152]{2,1,0:T(4,128)(2,1)S(1)}, u32[]{:S(2)}, u32[]{:S(2)}) async-start(bf16[32,4,1152]{2,1,0:T(4,128)(2,1)} %caption.1), calls=%async_computation.5 | async-start | bytes 589824 | tf_op jit(solution)/shard_map/all_to_all | solution.py:41
  239.7 9.9 %all-to-all-done.5.refs_0_ = bf16[32,4,1152]{2,1,0:T(4,128)(2,1)S(1)} async-done(((bf16[32,4,1152]{2,1,0:T(4,128)(2,1)}), bf16[32,4,1152]{2,1,0:T(4,128)(2,1)S(1)}, u32[]{:S(2)}, u32[]{:S(2)}) %all-to-all-start.5) | async-done | bytes 294944 | tf_op jit(solution)/shard_map/all_to_all | solution.py:41
  249.5 0.9 copy-done.8
  250.4 1.2 text_kv.1
  251.6 3.9 %all-to-all-start.6 = ((bf16[32,72,128]{2,1,0:T(8,128)(2,1)}), bf16[32,72,128]{2,1,0:T(8,128)(2,1)S(1)}, u32[]{:S(2)}, u32[]{:S(2)}) async-start(bf16[32,72,128]{2,1,0:T(8,128)(2,1)} %text_kv.1), calls=%async_computation.6 | async-start | bytes 1179648 | tf_op jit(solution)/shard_map/all_to_all | solution.py:41
  256.9 3.3 %copy-done.1 = bf16[1152,3456]{1,0:T(8,128)(2,1)S(1)} copy-done((bf16[1152,3456]{1,0:T(8,128)(2,1)S(1)}, bf16[1152,3456]{1,0:T(8,128)(2,1)}, u32[]{:S(2)}) %copy-start.1) | copy-done | bytes 7962648
  260.1 2.1 project_out_and_query.1
  262.2 6.2 %all-to-all-done.6.kv_ref = bf16[32,72,128]{2,1,0:T(8,128)(2,1)S(1)} async-done(((bf16[32,72,128]{2,1,0:T(8,128)(2,1)}), bf16[32,72,128]{2,1,0:T(8,128)(2,1)S(1)}, u32[]{:S(2)}, u32[]{:S(2)}) %all-to-all-start.6) | async-done | bytes 589856 | tf_op jit(solution)/shard_map/all_to_all | solution.py:41
  268.5 3.3 %copy-done.2 = bf16[1152,3456]{1,0:T(8,128)(2,1)S(1)} copy-done((bf16[1152,3456]{1,0:T(8,128)(2,1)S(1)}, bf16[1152,3456]{1,0:T(8,128)(2,1)}, u32[]{:S(2)}) %copy-start.2) | copy-done | bytes 7962648
  271.7 4.8 %cross_attention.1 = bf16[192,1152]{1,0:T(8,128)(2,1)} custom-call(s32[1]{0:T(128)S(6)} %copy.21.len_ref, bf16[192,1152]{1,0:T(8,128)(2,1)S(1)} %get-tuple-element.41.cq_ref, bf16[192,1152]{1,0:T(8,128)(2,1)S(1)} %get-tuple-element.42.after_ref, bf16[32,72,128]{2,1,0:T(8,128)(2,1)S(1)} %all-to-all-done.6.kv_ref, bf16[1152,3456]{1,0:T(8,128)(2,1)S(1)} %copy-done.2), custom_call_target="tpu_custom_call" | custom-call | flops 1019215872 | bytes 5242880 | tf_op jit(solution)/shard_map/cross_attention/pallas_call | solution.py:468
  (102 shorter events, 7.8 us)
Async XLA Ops:
  10.1 7.5 %copy-start.22 = (f32[1,3,1152]{2,0,1:T(1,128)S(1)}, f32[1,3,1152]{2,0,1:T(1,128)}, u32[]{:S(2)}) copy-start(f32[1,3,1152]{2,0,1:T(1,128)} %param.28) | copy-start | bytes 41476
  10.1 7.5 %copy-start.4 = (bf16[1,192,1152]{2,1,0:T(8,128)(2,1)S(1)}, bf16[1,192,1152]{2,1,0:T(8,128)(2,1)}, u32[]{:S(2)}) copy-start(bf16[1,192,1152]{2,1,0:T(8,128)(2,1)} %param.27) | copy-start | bytes 1327108
  10.1 7.5 %copy-start.6 = (bf16[1152,216]{0,1:T(8,128)(2,1)S(1)}, bf16[1152,216]{0,1:T(8,128)(2,1)}, u32[]{:S(2)}) copy-start(bf16[1152,216]{0,1:T(8,128)(2,1)} %param.29) | copy-start | bytes 1492996
  10.1 42.9 %all-to-all-start = ((bf16[32,32,512]{2,1,0:T(8,128)(2,1)}), bf16[32,32,512]{2,1,0:T(8,128)(2,1)S(1)}, u32[]{:S(2)}, u32[]{:S(2)}) async-start(bf16[32,32,512]{2,1,0:T(8,128)(2,1)} %bitcast.37), calls=%async_computation | async-start | bytes 2097152 | tf_op jit(solution)/shard_map/all_to_all | solution.py:41
  18.7 35.5 %copy-start.17 = (bf16[216,1152]{1,0:T(8,128)(2,1)}, bf16[216,1152]{1,0:T(8,128)(2,1)S(1)}, u32[]{:S(2)}) copy-start(bf16[216,1152]{1,0:T(8,128)(2,1)S(1)} %get-tuple-element.26.refs_5_) | copy-start | bytes 1492996
  18.7 25.5 %collective-permute-start.4 = (bf16[216,1152]{1,0:T(8,128)(2,1)S(1)}, bf16[216,1152]{1,0:T(8,128)(2,1)}, u32[]{:S(2)}, u32[]{:S(2)}) collective-permute-start(bf16[216,1152]{1,0:T(8,128)(2,1)S(1)} %get-tuple-element.26.refs_5_), channel_id=1, source_target_pairs={{0,16},{16,0},{1,17},{17,1},{2,18},{18,2},{3,19},{19,3},{4,20},{20... | collective-permute-start | bytes 1493000 | tf_op jit(solution)/shard_map/ppermute | solution.py:51
  22.0 30.2 %collective-permute-start.3 = (bf16[216,1152]{1,0:T(8,128)(2,1)S(1)}, bf16[216,1152]{1,0:T(8,128)(2,1)}, u32[]{:S(2)}, u32[]{:S(2)}) collective-permute-start(bf16[216,1152]{1,0:T(8,128)(2,1)S(1)} %get-tuple-element.26.refs_5_), channel_id=1, source_target_pairs={{0,2},{2,0},{1,3},{3,1},{4,6},{6,4},{5,7},{7,5},{8,10},{10,8},{9,1... | collective-permute-start | bytes 1493000 | tf_op jit(solution)/shard_map/ppermute | solution.py:51
  22.0 22.8 %collective-permute-start = (bf16[192,1152]{1,0:T(8,128)(2,1)}, bf16[192,1152]{1,0:T(8,128)(2,1)S(1)}, u32[]{:S(2)}, u32[]{:S(2)}) collective-permute-start(bf16[192,1152]{1,0:T(8,128)(2,1)} %get-tuple-element.25.refs_1_), channel_id=1, source_target_pairs={{0,4},{4,8},{8,12},{12,0},{1,5},{5,9},{9,13},{13,1},{2,6},{6,10},{... | collective-permute-start | bytes 1327112 | tf_op jit(solution)/shard_map/ppermute | solution.py:46
  23.5 28.7 %collective-permute-start.1 = (bf16[192,1152]{1,0:T(8,128)(2,1)}, bf16[192,1152]{1,0:T(8,128)(2,1)}, u32[]{:S(2)}, u32[]{:S(2)}) collective-permute-start(bf16[192,1152]{1,0:T(8,128)(2,1)} %get-tuple-element.25.refs_1_), channel_id=1, source_target_pairs={{0,8},{4,12},{8,0},{12,4},{1,9},{5,13},{9,1},{13,5},{2,10},{6,14},... | collective-permute-start | bytes 1327112 | tf_op jit(solution)/shard_map/ppermute | solution.py:46
  26.2 26.0 %collective-permute-start.2 = (bf16[192,1152]{1,0:T(8,128)(2,1)}, bf16[192,1152]{1,0:T(8,128)(2,1)}, u32[]{:S(2)}, u32[]{:S(2)}) collective-permute-start(bf16[192,1152]{1,0:T(8,128)(2,1)} %get-tuple-element.25.refs_1_), channel_id=1, source_target_pairs={{0,12},{4,0},{8,4},{12,8},{1,13},{5,1},{9,5},{13,9},{2,14},{6,2},{... | collective-permute-start | bytes 1327112 | tf_op jit(solution)/shard_map/ppermute | solution.py:46
  44.2 15.5 %collective-permute-start.5 = (bf16[216,1152]{1,0:T(8,128)(2,1)}, bf16[216,1152]{1,0:T(8,128)(2,1)}, u32[]{:S(2)}, u32[]{:S(2)}) collective-permute-start(bf16[216,1152]{1,0:T(8,128)(2,1)} %collective-permute-done.4.refs_7_), channel_id=1, source_target_pairs={{0,2},{2,0},{1,3},{3,1},{4,6},{6,4},{5,7},{7,5},{8,10},{10,8},{9,1... | collective-permute-start | bytes 1493000 | tf_op jit(solution)/shard_map/ppermute | solution.py:51
  44.8 9.4 %copy-start.31 = (bf16[192,1152]{1,0:T(8,128)(2,1)}, bf16[192,1152]{1,0:T(8,128)(2,1)S(1)}, u32[]{:S(2)}) copy-start(bf16[192,1152]{1,0:T(8,128)(2,1)S(1)} %collective-permute-done.refs_2_) | copy-start | bytes 1327108
  54.2 46.9 %all-to-all-start.1 = ((bf16[32,32,512]{2,1,0:T(8,128)(2,1)}), bf16[32,32,512]{2,1,0:T(8,128)(2,1)S(1)}, u32[]{:S(2)}, u32[]{:S(2)}) async-start(bf16[32,32,512]{2,1,0:T(8,128)(2,1)} %embed_sum.1), calls=%async_computation.1 | async-start | bytes 2097152 | tf_op jit(solution)/shard_map/all_to_all | solution.py:41
  59.6 32.3 %copy-start.10 = (bf16[36,1152]{1,0:T(8,128)(2,1)S(1)}, bf16[36,1152]{1,0:T(8,128)(2,1)}, u32[]{:S(2)}) copy-start(bf16[36,1152]{1,0:T(8,128)(2,1)} %refs_0_.1) | copy-start | bytes 248836
  59.6 32.3 %copy-start.11 = (bf16[36,1152]{1,0:T(8,128)(2,1)S(1)}, bf16[36,1152]{1,0:T(8,128)(2,1)}, u32[]{:S(2)}) copy-start(bf16[36,1152]{1,0:T(8,128)(2,1)} %refs_1_.2) | copy-start | bytes 248836
  59.6 32.3 %copy-start.12 = (bf16[36,1152]{1,0:T(8,128)(2,1)S(1)}, bf16[36,1152]{1,0:T(8,128)(2,1)}, u32[]{:S(2)}) copy-start(bf16[36,1152]{1,0:T(8,128)(2,1)} %refs_2_.2) | copy-start | bytes 248836
  59.6 41.4 %copy-start.14 = (s32[5]{0:T(128)S(1)}, s32[5]{0:T(128)}, u32[]{:S(2)}) copy-start(s32[5]{0:T(128)} %stack.23.refs_0_.at_ref) | copy-start | bytes 64
  59.7 41.4 %copy-start.18 = (bf16[512,320]{0,1:T(8,128)(2,1)S(1)}, bf16[512,320]{0,1:T(8,128)(2,1)}, u32[]{:S(2)}) copy-start(bf16[512,320]{0,1:T(8,128)(2,1)} %param.21) | copy-start | bytes 983044
  59.7 41.4 %copy-start.20 = (f32[512]{0:T(512)S(1)}, f32[512]{0:T(512)}, u32[]{:S(2)}) copy-start(f32[512]{0:T(512)} %param.20) | copy-start | bytes 6148
  59.7 197.2 %all-gather.2.cloned.1.call-start = ((), (), s32[]{:S(2)}) async-start(), calls=%async_computation.7 | async-start | bytes 8460288 | tf_op jit(solution)/shard_map/all_gather | solution.py:575
  65.5 16.6 %collective-permute-start.6 = (bf16[240,768]{1,0:T(8,128)(2,1)}, bf16[240,768]{1,0:T(8,128)(2,1)S(1)}, u32[]{:S(2)}, u32[]{:S(2)}) collective-permute-start(bf16[240,768]{1,0:T(8,128)(2,1)} %get-tuple-element.28), channel_id=1, source_target_pairs={{0,1},{1,0},{16,17},{17,16},{2,3},{3,2},{18,19},{19,18},{4,5},{5,4... | collective-permute-start | bytes 1105928 | tf_op jit(solution)/shard_map/ppermute | solution.py:51
  67.3 23.9 %collective-permute-start.7 = (bf16[240,768]{1,0:T(8,128)(2,1)}, bf16[240,768]{1,0:T(8,128)(2,1)S(1)}, u32[]{:S(2)}, u32[]{:S(2)}) collective-permute-start(bf16[240,768]{1,0:T(8,128)(2,1)} %get-tuple-element.29), channel_id=1, source_target_pairs={{0,16},{1,17},{16,0},{17,1},{2,18},{3,19},{18,2},{19,3},{4,20},{5,... | collective-permute-start | bytes 1105928 | tf_op jit(solution)/shard_map/ppermute | solution.py:51
  69.9 22.0 %collective-permute-start.8 = (bf16[240,768]{1,0:T(8,128)(2,1)}, bf16[240,768]{1,0:T(8,128)(2,1)S(1)}, u32[]{:S(2)}, u32[]{:S(2)}) collective-permute-start(bf16[240,768]{1,0:T(8,128)(2,1)} %get-tuple-element.30), channel_id=1, source_target_pairs={{0,17},{1,16},{16,1},{17,0},{2,19},{3,18},{18,3},{19,2},{4,21},{5,... | collective-permute-start | bytes 1105928 | tf_op jit(solution)/shard_map/ppermute | solution.py:51
  70.2 22.5 %collective-permute-start.9 = (bf16[240,768]{1,0:T(8,128)(2,1)}, bf16[240,768]{1,0:T(8,128)(2,1)S(1)}, u32[]{:S(2)}, u32[]{:S(2)}) collective-permute-start(bf16[240,768]{1,0:T(8,128)(2,1)} %get-tuple-element.27.refs_1_), channel_id=1, source_target_pairs={{0,2},{2,0},{1,3},{3,1},{4,6},{6,4},{5,7},{7,5},{8,10},{10,8},{9,1... | collective-permute-start | bytes 1105928 | tf_op jit(solution)/shard_map/ppermute | solution.py:51
  82.1 11.5 %copy-start.24 = (bf16[240,768]{1,0:T(8,128)(2,1)}, bf16[240,768]{1,0:T(8,128)(2,1)S(1)}, u32[]{:S(2)}) copy-start(bf16[240,768]{1,0:T(8,128)(2,1)S(1)} %collective-permute-done.6.refs_2_) | copy-start | bytes 1105924
  82.1 10.5 %collective-permute-start.10 = (bf16[240,768]{1,0:T(8,128)(2,1)S(1)}, bf16[240,768]{1,0:T(8,128)(2,1)S(1)}, u32[]{:S(2)}, u32[]{:S(2)}) collective-permute-start(bf16[240,768]{1,0:T(8,128)(2,1)S(1)} %collective-permute-done.6.refs_2_), channel_id=1, source_target_pairs={{0,2},{2,0},{1,3},{3,1},{4,6},{6,4},{5,7},{7,5},{8,10},{10,8},{9,1... | collective-permute-start | bytes 1105928 | tf_op jit(solution)/shard_map/ppermute | solution.py:51
  91.1 1.7 collective-permute-start.11
  91.9 1.7 collective-permute-start.12
  92.0 9.1 %collective-permute-start.13 = (bf16[36,3456]{1,0:T(8,128)(2,1)S(1)}, bf16[36,3456]{1,0:T(8,128)(2,1)S(1)}, u32[]{:S(2)}, u32[]{:S(2)}) collective-permute-start(bf16[36,3456]{1,0:T(8,128)(2,1)S(1)} %side_weights.1.refs_5_), channel_id=1, source_target_pairs={{0,1},{1,0},{2,3},{3,2},{4,5},{5,4},{6,7},{7,6},{8,9},{9,8},{10,11... | collective-permute-start | bytes 746504 | tf_op jit(solution)/shard_map/ppermute | solution.py:51
  105.9 8.6 %copy-start.21 = (f32[8,128]{1,0:T(8,128)}, f32[8,128]{1,0:T(8,128)S(1)}, u32[]{:S(2)}) copy-start(f32[8,128]{1,0:T(8,128)S(1)} %get-tuple-element.31.refs_9_) | copy-start | bytes 12292
  106.0 75.6 %all-to-all-start.2 = ((bf16[8,136,640]{2,1,0:T(8,128)(2,1)}), bf16[8,136,640]{2,1,0:T(8,128)(2,1)S(1)}, u32[]{:S(2)}, u32[]{:S(2)}) async-start(bf16[8,136,640]{2,1,0:T(8,128)(2,1)} %copy-done.5), calls=%async_computation.2 | async-start | bytes 2785280 | tf_op jit(solution)/shard_map/all_to_all | solution.py:41
  186.0 6.7 %copy-start.33 = (bf16[4,72,192]{2,1,0:T(8,128)(2,1)S(1)}, bf16[4,72,192]{2,1,0:T(8,128)(2,1)}, u32[]{:S(2)}) copy-start(bf16[4,72,192]{2,1,0:T(8,128)(2,1)} %get-tuple-element.34) | copy-start | bytes 331780
  186.0 9.4 %copy-start.32 = (bf16[4,72,192]{2,1,0:T(8,128)(2,1)S(1)}, bf16[4,72,192]{2,1,0:T(8,128)(2,1)}, u32[]{:S(2)}) copy-start(bf16[4,72,192]{2,1,0:T(8,128)(2,1)} %get-tuple-element.35) | copy-start | bytes 331780
  186.0 27.5 %copy-start.9 = (bf16[4,72,192]{2,1,0:T(8,128)(2,1)S(1)}, bf16[4,72,192]{2,1,0:T(8,128)(2,1)}, u32[]{:S(2)}) copy-start(bf16[4,72,192]{2,1,0:T(8,128)(2,1)} %get-tuple-element.32.refs_0_) | copy-start | bytes 331780
  186.0 31.1 %copy-start.23 = (f32[1152]{0:T(1024)S(1)}, f32[1152]{0:T(1024)}, u32[]{:S(2)}) copy-start(f32[1152]{0:T(1024)} %param.26) | copy-start | bytes 13828
  186.0 32.7 %copy-start.7 = (bf16[128,1152]{1,0:T(8,128)(2,1)S(1)}, bf16[128,1152]{1,0:T(8,128)(2,1)}, u32[]{:S(2)}) copy-start(bf16[128,1152]{1,0:T(8,128)(2,1)} %refs_2_.3) | copy-start | bytes 884740
  186.0 32.7 %copy-start.16 = (f32[128]{0:T(128)S(1)}, f32[128]{0:T(128)}, u32[]{:S(2)}) copy-start(f32[128]{0:T(128)} %param.24) | copy-start | bytes 1540
  186.0 32.6 %all-to-all-start.3 = ((bf16[32,136,128]{2,1,0:T(8,128)(2,1)}), bf16[32,136,128]{2,1,0:T(8,128)(2,1)S(1)}, u32[]{:S(2)}, u32[]{:S(2)}) async-start(bf16[32,136,128]{2,1,0:T(8,128)(2,1)} %text_down.1), calls=%async_computation.3 | async-start | bytes 2228224 | tf_op jit(solution)/shard_map/all_to_all | solution.py:41
  190.8 18.5 %collective-permute-start.14 = (bf16[4,72,192]{2,1,0:T(8,128)(2,1)}, bf16[4,72,192]{2,1,0:T(8,128)(2,1)S(1)}, u32[]{:S(2)}, u32[]{:S(2)}) collective-permute-start(bf16[4,72,192]{2,1,0:T(8,128)(2,1)} %get-tuple-element.33), channel_id=1, source_target_pairs={{0,1},{1,0},{16,17},{17,16},{2,3},{3,2},{18,19},{19,18},{4,5},{5,4... | collective-permute-start | bytes 331784 | tf_op jit(solution)/shard_map/ppermute | solution.py:51
  192.7 20.8 %collective-permute-start.15 = (bf16[4,72,192]{2,1,0:T(8,128)(2,1)S(1)}, bf16[4,72,192]{2,1,0:T(8,128)(2,1)S(1)}, u32[]{:S(2)}, u32[]{:S(2)}) collective-permute-start(bf16[4,72,192]{2,1,0:T(8,128)(2,1)S(1)} %copy-done.33), channel_id=1, source_target_pairs={{0,16},{1,17},{16,0},{17,1},{2,18},{3,19},{18,2},{19,3},{4,20},{5,... | collective-permute-start | bytes 331784 | tf_op jit(solution)/shard_map/ppermute | solution.py:51
  195.4 18.1 %collective-permute-start.16 = (bf16[4,72,192]{2,1,0:T(8,128)(2,1)S(1)}, bf16[4,72,192]{2,1,0:T(8,128)(2,1)S(1)}, u32[]{:S(2)}, u32[]{:S(2)}) collective-permute-start(bf16[4,72,192]{2,1,0:T(8,128)(2,1)S(1)} %copy-done.32), channel_id=1, source_target_pairs={{0,17},{1,16},{16,1},{17,0},{2,19},{3,18},{18,3},{19,2},{4,21},{5,... | collective-permute-start | bytes 331784 | tf_op jit(solution)/shard_map/ppermute | solution.py:51
  214.3 10.3 %collective-permute-start.19 = (bf16[4,72,192]{2,1,0:T(8,128)(2,1)}, bf16[4,72,192]{2,1,0:T(8,128)(2,1)S(1)}, u32[]{:S(2)}, u32[]{:S(2)}) collective-permute-start(bf16[4,72,192]{2,1,0:T(8,128)(2,1)} %get-tuple-element.39), channel_id=1, source_target_pairs={{0,12},{4,0},{8,4},{12,8},{1,13},{5,1},{9,5},{13,9},{2,14},{6,2},{... | collective-permute-start | bytes 331784 | tf_op jit(solution)/shard_map/ppermute | solution.py:46
  217.1 8.5 %collective-permute-start.18 = (bf16[4,72,192]{2,1,0:T(8,128)(2,1)}, bf16[4,72,192]{2,1,0:T(8,128)(2,1)S(1)}, u32[]{:S(2)}, u32[]{:S(2)}) collective-permute-start(bf16[4,72,192]{2,1,0:T(8,128)(2,1)} %get-tuple-element.38), channel_id=1, source_target_pairs={{0,8},{4,12},{8,0},{12,4},{1,9},{5,13},{9,1},{13,5},{2,10},{6,14},... | collective-permute-start | bytes 331784 | tf_op jit(solution)/shard_map/ppermute | solution.py:46
  217.9 21.7 %collective-permute-start.17 = (bf16[4,72,192]{2,1,0:T(8,128)(2,1)}, bf16[4,72,192]{2,1,0:T(8,128)(2,1)S(1)}, u32[]{:S(2)}, u32[]{:S(2)}) collective-permute-start(bf16[4,72,192]{2,1,0:T(8,128)(2,1)} %get-tuple-element.37), channel_id=1, source_target_pairs={{0,4},{4,8},{8,12},{12,0},{1,5},{5,9},{9,13},{13,1},{2,6},{6,10},{... | collective-permute-start | bytes 331784 | tf_op jit(solution)/shard_map/ppermute | solution.py:46
  219.8 37.1 %copy-start.15 = (s32[5]{0:T(128)S(1)}, s32[5]{0:T(128)}, u32[]{:S(2)}) copy-start(s32[5]{0:T(128)} %stack.23.refs_0_.at_ref) | copy-start | bytes 64
  219.8 15.0 %all-to-all-start.4 = ((bf16[32,4,1280]{2,1,0:T(4,128)(2,1)}), bf16[32,4,1280]{2,1,0:T(4,128)(2,1)S(1)}, u32[]{:S(2)}, u32[]{:S(2)}) async-start(bf16[32,4,1280]{2,1,0:T(4,128)(2,1)} %caption_partial.1), calls=%async_computation.4 | async-start | bytes 655360 | tf_op jit(solution)/shard_map/all_to_all | solution.py:41
  235.8 13.8 %all-to-all-start.5 = ((bf16[32,4,1152]{2,1,0:T(4,128)(2,1)}), bf16[32,4,1152]{2,1,0:T(4,128)(2,1)S(1)}, u32[]{:S(2)}, u32[]{:S(2)}) async-start(bf16[32,4,1152]{2,1,0:T(4,128)(2,1)} %caption.1), calls=%async_computation.5 | async-start | bytes 589824 | tf_op jit(solution)/shard_map/all_to_all | solution.py:41
  251.6 16.9 %all-to-all-start.6 = ((bf16[32,72,128]{2,1,0:T(8,128)(2,1)}), bf16[32,72,128]{2,1,0:T(8,128)(2,1)S(1)}, u32[]{:S(2)}, u32[]{:S(2)}) async-start(bf16[32,72,128]{2,1,0:T(8,128)(2,1)} %text_kv.1), calls=%async_computation.6 | async-start | bytes 1179648 | tf_op jit(solution)/shard_map/all_to_all | solution.py:41
  (14 other events, 21.0 us)
Sparse Core Ops, SparseCore 0:
  106.1 75.8 all-gather.1

commit v3 on v2

--- a/solution.py
+++ b/solution.py
@@ -543,14 +543,15 @@
     fulls = [made[0]] + [crossed(made[m], ROW, m) for m in range(1, 4)]
     others = [crossed(full, "core", 1) for full in fulls]
 
+    side = call(side_kernel, "side_weights", shape((w_out.shape[0], 3 * W)), (w_out, w_cq, w_co))
+    other_side = crossed(side, "tp", 1)
     embedded = call(
         embed_kernel,
         "embed_sum",
         shape(picked.shape),
         (picked,),
-        after=(tie(*token_blocks[1:], *weight_blocks[1:3]),),
-    )
-    side = call(side_kernel, "side_weights", shape((w_out.shape[0], 3 * W)), (w_out, w_cq, w_co))
+        after=(tie(*token_blocks[1:], *weight_blocks[1:3], other_side),),
+    )
     gate_up, pair, tick = call(
         gate_up_kernel,
         "text_gate_up",
@@ -562,7 +563,7 @@
             wi_gate.T,
             wi_up.T,
             side,
-            crossed(side, "tp", 1),
+            other_side,
         ),
         scratch=[pltpu.VMEM((feats, 2 * units), BF16), pltpu.VMEM((tokens, feats), F32)],
         in_specs=[SMEM] + [VMEM] * 6,
@@ -612,17 +613,19 @@
         (exchange(down, PLANE), final_gain.reshape(1, width), cap_weight),
         scratch=[pltpu.VMEM((tokens, width), F32), pltpu.VMEM((tokens, W + 128), F32)],
     )
-    grouped = call(
+    *grouped, tick = call(
         regroup_kernel,
         "regroup",
         [shape((4, HEAD, rows))] * 4,
         tuple(found),
+        tick=True,
     )
     caption = call(
         caption_kernel,
         "caption",
         shape((plane, share, W)),
         (exchange(cap_part, PLANE), cap_bias.reshape(1, W)),
+        after=(tick,),
     )
     parts = [grouped[0]] + [shifted(grouped[d], "x", d) for d in range(1, 4)]
     after_self, cross_query = project(at, parts, side, pixels, modulate[2:3])
@@ -632,7 +635,6 @@
         shape((plane, w_ckv.shape[1], tokens)),
         (exchange(caption, PLANE), w_ckv.T),
         scratch=[pltpu.VMEM((tokens, W), F32)],
-        after=(tie(*(part[0] for part in parts[1:])),),
     )
     text_kv = exchange(kv_part, PLANE)
     result = cross(text_lengths, cross_query, after_self, text_kv, side)

time: 284 us -> 291 us (1.025)
  blocking collectives: 0 us -> 37.4 us
  waiting for transfers between devices: 97.5 us -> 74.8 us
  starting transfers between devices: 62.4 us -> 57 us
    all_to_all x0 -> x2, blocking collectives: none -> 37.4 us  [exchange(): return lax.all_to_all(blocks, axes, 0, 0, tiled=True)]
    all_to_all x7 -> x5, waiting for transfers between devices: 25.3 us -> 0.01 us  [exchange(): return lax.all_to_all(blocks, axes, 0, 0, tiled=True)]
    ppermute x6, waiting for transfers between devices: 8.48 us -> 19 us  [shifted(): lax.ppermute(value, axis, [(i, (i + shift) % size) for i in range(size)])]
    ppermute x14, waiting for transfers between devices: 63.7 us -> 55.8 us  [crossed(): return lax.ppermute(value, axis, [(i, i ^ mask) for i in range(size)])]
    all_to_all x7 -> x5, starting transfers between devices: 38.8 us -> 31.3 us  [exchange(): return lax.all_to_all(blocks, axes, 0, 0, tiled=True)]
  transfers between devices with their start and end apart: 28 -> 26, of which waited for: 14 -> 13; matrix products, arithmetic and copies ran while one was open for 1% -> 1% of each run, Pallas kernels for 29% -> 28%
where the time goes in v3:
time: 291 us; the launch traced here: 290 us
  Pallas kernels  88.5 us (30%)
  waiting for transfers between devices  74.8 us (26%)
  starting transfers between devices  57 us (20%)
  blocking collectives  37.4 us (13%)
  between operations  14.4 us (5%)
  local copies, waits for them, and re-layouts  13.7 us (5%)
    pallas_call x11, Pallas kernels, call(): pl.pallas_call(body, out_shape=outs if many else outs[0], in_specs=(in_sp...  81.5 us
    ppermute x14, waiting for transfers between devices, crossed(): return lax.ppermute(value, axis, [(i, i ^ mask) for i in range(size)])  55.8 us
    all_to_all x2, blocking collectives, exchange(): return lax.all_to_all(blocks, axes, 0, 0, tiled=True)  37.4 us
    all_to_all x5, starting transfers between devices, exchange(): return lax.all_to_all(blocks, axes, 0, 0, tiled=True)  31.3 us
    ppermute x6, waiting for transfers between devices, shifted(): lax.ppermute(value, axis, [(i, (i + shift) % size) for i in range(size)])  19 us
    ppermute x14, starting transfers between devices, crossed(): return lax.ppermute(value, axis, [(i, i ^ mask) for i in range(size)])  13.5 us
    unnamed x69, local copies, waits for them, and re-layouts  12.3 us
    ppermute x6, starting transfers between devices, shifted(): lax.ppermute(value, axis, [(i, (i + shift) % size) for i in range(size)])  12.3 us
  transfers between devices with their start and end apart: 26, of which 13 were waited for; matrix products, arithmetic and copies ran while one was open for 1% of the time, Pallas kernels for 28%

profile of v3, /device:TPU:32, one launch (start us, length us, event | category | flops | bytes accessed | tf_op | source)
XLA Modules:
  0.0 289.7 jit_solution(16206352980923962177)
XLA Ops:
  6.5 0.8 subtract_bitcast_fusion
  7.8 2.3 fusion.2
  10.1 7.5 %all-to-all-start = ((bf16[32,32,512]{2,1,0:T(8,128)(2,1)}), bf16[32,32,512]{2,1,0:T(8,128)(2,1)S(1)}, u32[]{:S(2)}, u32[]{:S(2)}) async-start(bf16[32,32,512]{2,1,0:T(8,128)(2,1)} %bitcast.31), calls=%async_computation | async-start | bytes 2097152 | tf_op jit(solution)/shard_map/all_to_all | solution.py:41
  17.6 1.3 modulate.1
  18.9 3.3 %collective-permute-start.4 = (bf16[216,1152]{1,0:T(8,128)(2,1)}, bf16[216,1152]{1,0:T(8,128)(2,1)}, u32[]{:S(2)}, u32[]{:S(2)}) collective-permute-start(bf16[216,1152]{1,0:T(8,128)(2,1)} %get-tuple-element.27.refs_5_), channel_id=1, source_target_pairs={{0,16},{16,0},{1,17},{17,1},{2,18},{18,2},{3,19},{19,3},{4,20},{20... | collective-permute-start | bytes 1493000 | tf_op jit(solution)/shard_map/ppermute | solution.py:51
  22.9 1.5 collective-permute-start
  24.4 2.7 collective-permute-start.1
  27.1 21.8 %collective-permute-done.13.refs_6_ = bf16[36,3456]{1,0:T(8,128)(2,1)S(1)} collective-permute-done((bf16[36,3456]{1,0:T(8,128)(2,1)S(1)}, bf16[36,3456]{1,0:T(8,128)(2,1)S(1)}, u32[]{:S(2)}, u32[]{:S(2)}) %collective-permute-start.13) | collective-permute-done | bytes 248864 | tf_op jit(solution)/shard_map/ppermute | solution.py:51
  48.9 2.1 collective-permute-start.2
  52.3 8.7 %collective-permute-done.2.refs_4_ = bf16[192,1152]{1,0:T(8,128)(2,1)} collective-permute-done((bf16[192,1152]{1,0:T(8,128)(2,1)}, bf16[192,1152]{1,0:T(8,128)(2,1)}, u32[]{:S(2)}, u32[]{:S(2)}) %collective-permute-start.2) | collective-permute-done | bytes 442400 | tf_op jit(solution)/shard_map/ppermute | solution.py:46
  61.7 1.2 embed_sum.1
  62.9 7.2 %all-to-all-start.1 = ((bf16[32,32,512]{2,1,0:T(8,128)(2,1)}), bf16[32,32,512]{2,1,0:T(8,128)(2,1)S(1)}, u32[]{:S(2)}, u32[]{:S(2)}) async-start(bf16[32,32,512]{2,1,0:T(8,128)(2,1)} %embed_sum.1), calls=%async_computation.1 | async-start | bytes 2097152 | tf_op jit(solution)/shard_map/all_to_all | solution.py:41
  70.3 5.7 %query_key_value.1 = (bf16[240,768]{1,0:T(8,128)(2,1)}, bf16[240,768]{1,0:T(8,128)(2,1)}, bf16[240,768]{1,0:T(8,128)(2,1)}, bf16[240,768]{1,0:T(8,128)(2,1)}) custom-call(s32[5]{0:T(128)} %stack.23.refs_0_.at_ref, bf16[192,1152]{1,0:T(8,128)(2,1)} %get-tuple-element.26.refs_1_, bf16[192,1152]{1,0:T(8,128)(2,1)} %copy-done.30, ...), custom_call_target="tpu_custom_call" | custom-call | flops 1528823808 | bytes 8388608 | tf_op jit(solution)/shard_map/query_key_value/pallas_call | solution.py:93
  75.9 1.8 collective-permute-start.6
  77.7 2.7 collective-permute-start.7
  80.6 12.0 %collective-permute-done.6.refs_2_ = bf16[240,768]{1,0:T(8,128)(2,1)S(1)} collective-permute-done((bf16[240,768]{1,0:T(8,128)(2,1)}, bf16[240,768]{1,0:T(8,128)(2,1)S(1)}, u32[]{:S(2)}, u32[]{:S(2)}) %collective-permute-start.6) | collective-permute-done | bytes 368672 | tf_op jit(solution)/shard_map/ppermute | solution.py:51
  92.7 9.0 %collective-permute-done.7.refs_3_ = bf16[240,768]{1,0:T(8,128)(2,1)S(1)} collective-permute-done((bf16[240,768]{1,0:T(8,128)(2,1)}, bf16[240,768]{1,0:T(8,128)(2,1)S(1)}, u32[]{:S(2)}, u32[]{:S(2)}) %collective-permute-start.7) | collective-permute-done | bytes 368672 | tf_op jit(solution)/shard_map/ppermute | solution.py:51
  101.7 0.7 collective-permute-done.8.refs_4_
  102.5 0.9 collective-permute-done.11.refs_7_
  103.4 0.7 collective-permute-done.12.refs_8_
  104.2 0.7 copy-done.29
  105.0 1.0 copy-done.18
  105.9 2.8 text_gate_up.1
  108.7 1.1 copy-done.5
  109.8 8.6 %all-to-all-start.2 = ((bf16[8,136,640]{2,1,0:T(8,128)(2,1)}), bf16[8,136,640]{2,1,0:T(8,128)(2,1)S(1)}, u32[]{:S(2)}, u32[]{:S(2)}) async-start(bf16[8,136,640]{2,1,0:T(8,128)(2,1)} %copy-done.5), calls=%async_computation.2 | async-start | bytes 2785280 | tf_op jit(solution)/shard_map/all_to_all | solution.py:41
  118.5 67.0 %self_attention.1 = (bf16[4,72,192]{2,1,0:T(8,128)(2,1)}, bf16[4,72,192]{2,1,0:T(8,128)(2,1)}, bf16[4,72,192]{2,1,0:T(8,128)(2,1)}, bf16[4,72,192]{2,1,0:T(8,128)(2,1)}, f32[8,128]{1,0:T(8,128)}) custom-call(s32[5]{0:T(128)} %stack.23.refs_0_.at_ref, bf16[240,768]{1,0:T(8,128)(2,1)} %get-tuple-element.28.refs_1_, bf16[240,768]{1,0:T(8,128)(2,1)} %copy-done.23, ...), custom_call_target="tpu_custom_call" | custom-call | flops 9663676416 | bytes 8388608 | tf_op jit(solution)/shard_map/self_attention/pallas_call | solution.py:93
  185.5 1.7 copy-done.3
  187.9 1.0 text_down.1
  189.0 23.8 %all_to_all.35.refs_0_ = bf16[32,136,128]{2,1,0:T(8,128)(2,1)S(1)} all-to-all(bf16[32,136,128]{2,1,0:T(8,128)(2,1)S(1)} %text_down.1), channel_id=1, replica_groups=mesh['grp'=8,'yhi'=2,'x'=4,'core'=2,'tp'=2] {'yhi','x','core','tp'}, dimensions={0} | all-to-all | bytes 2228224 | tf_op jit(solution)/shard_map/all_to_all | solution.py:41
  212.8 1.1 caption_partial.1
  213.9 4.1 %all-to-all-start.4 = ((bf16[32,4,1280]{2,1,0:T(4,128)(2,1)}), bf16[32,4,1280]{2,1,0:T(4,128)(2,1)S(1)}, u32[]{:S(2)}, u32[]{:S(2)}) async-start(bf16[32,4,1280]{2,1,0:T(4,128)(2,1)} %caption_partial.1), calls=%async_computation.4 | async-start | bytes 655360 | tf_op jit(solution)/shard_map/all_to_all | solution.py:41
  218.0 1.8 collective-permute-start.14
  219.8 2.8 collective-permute-start.15
  222.8 5.1 %collective-permute-done.14.refs_1_ = bf16[4,72,192]{2,1,0:T(8,128)(2,1)S(1)} collective-permute-done((bf16[4,72,192]{2,1,0:T(8,128)(2,1)S(1)}, bf16[4,72,192]{2,1,0:T(8,128)(2,1)S(1)}, u32[]{:S(2)}, u32[]{:S(2)}) %collective-permute-start.14) | collective-permute-done | bytes 110624 | tf_op jit(solution)/shard_map/ppermute | solution.py:51
  227.9 4.5 %collective-permute-done.15.refs_2_ = bf16[4,72,192]{2,1,0:T(8,128)(2,1)S(1)} collective-permute-done((bf16[4,72,192]{2,1,0:T(8,128)(2,1)S(1)}, bf16[4,72,192]{2,1,0:T(8,128)(2,1)S(1)}, u32[]{:S(2)}, u32[]{:S(2)}) %collective-permute-start.15) | collective-permute-done | bytes 110624 | tf_op jit(solution)/shard_map/ppermute | solution.py:51
  232.3 1.0 collective-permute-done.16.refs_3_
  233.6 13.7 %all_to_all.36.refs_0_ = bf16[32,4,1152]{2,1,0:T(4,128)(2,1)S(1)} all-to-all(bf16[32,4,1152]{2,1,0:T(4,128)(2,1)S(1)} %caption.1), channel_id=1, replica_groups=mesh['grp'=8,'yhi'=2,'x'=4,'core'=2,'tp'=2] {'yhi','x','core','tp'}, dimensions={0} | all-to-all | bytes 589824 | tf_op jit(solution)/shard_map/all_to_all | solution.py:41
  247.3 1.1 text_kv.1
  248.5 3.9 %all-to-all-start.6 = ((bf16[32,72,128]{2,1,0:T(8,128)(2,1)}), bf16[32,72,128]{2,1,0:T(8,128)(2,1)S(1)}, u32[]{:S(2)}, u32[]{:S(2)}) async-start(bf16[32,72,128]{2,1,0:T(8,128)(2,1)} %text_kv.1), calls=%async_computation.6 | async-start | bytes 1179648 | tf_op jit(solution)/shard_map/all_to_all | solution.py:41
  252.4 1.8 collective-permute-start.17
  254.1 2.7 collective-permute-start.18
  256.9 1.4 collective-permute-start.19
  259.6 6.5 %collective-permute-done.17.refs_1_ = bf16[4,72,192]{2,1,0:T(8,128)(2,1)S(1)} collective-permute-done((bf16[4,72,192]{2,1,0:T(8,128)(2,1)S(1)}, bf16[4,72,192]{2,1,0:T(8,128)(2,1)S(1)}, u32[]{:S(2)}, u32[]{:S(2)}) %collective-permute-start.17) | collective-permute-done | bytes 110624 | tf_op jit(solution)/shard_map/ppermute | solution.py:46
  266.1 3.2 %collective-permute-done.18.refs_2_ = bf16[4,72,192]{2,1,0:T(8,128)(2,1)S(1)} collective-permute-done((bf16[4,72,192]{2,1,0:T(8,128)(2,1)S(1)}, bf16[4,72,192]{2,1,0:T(8,128)(2,1)S(1)}, u32[]{:S(2)}, u32[]{:S(2)}) %collective-permute-start.18) | collective-permute-done | bytes 110624 | tf_op jit(solution)/shard_map/ppermute | solution.py:46
  269.3 3.3 %copy-done.1 = bf16[1152,3456]{1,0:T(8,128)(2,1)S(1)} copy-done((bf16[1152,3456]{1,0:T(8,128)(2,1)S(1)}, bf16[1152,3456]{1,0:T(8,128)(2,1)}, u32[]{:S(2)}) %copy-start.1) | copy-done | bytes 7962648
  272.6 2.1 project_out_and_query.1
  274.7 3.3 %copy-done.2 = bf16[1152,3456]{1,0:T(8,128)(2,1)S(1)} copy-done((bf16[1152,3456]{1,0:T(8,128)(2,1)S(1)}, bf16[1152,3456]{1,0:T(8,128)(2,1)}, u32[]{:S(2)}) %copy-start.2) | copy-done | bytes 7962648
  278.0 4.8 %cross_attention.1 = bf16[192,1152]{1,0:T(8,128)(2,1)} custom-call(s32[1]{0:T(128)S(6)} %copy.21.len_ref, bf16[192,1152]{1,0:T(8,128)(2,1)S(1)} %get-tuple-element.42.cq_ref, bf16[192,1152]{1,0:T(8,128)(2,1)S(1)} %get-tuple-element.43.after_ref, bf16[32,72,128]{2,1,0:T(8,128)(2,1)S(1)} %all-to-all-done.6.kv_ref, bf16[1152,3456]{1,0:T(8,128)(2,1)S(1)} %copy-done.2), custom_call_target="tpu_custom_call" | custom-call | flops 1019215872 | bytes 5242880 | tf_op jit(solution)/shard_map/cross_attention/pallas_call | solution.py:468
  (96 shorter events, 5.5 us)
Async XLA Ops:
  10.1 7.5 %copy-start.21 = (f32[1,3,1152]{2,0,1:T(1,128)S(1)}, f32[1,3,1152]{2,0,1:T(1,128)}, u32[]{:S(2)}) copy-start(f32[1,3,1152]{2,0,1:T(1,128)} %param.28) | copy-start | bytes 41476
  10.1 7.5 %copy-start.4 = (bf16[1,192,1152]{2,1,0:T(8,128)(2,1)S(1)}, bf16[1,192,1152]{2,1,0:T(8,128)(2,1)}, u32[]{:S(2)}) copy-start(bf16[1,192,1152]{2,1,0:T(8,128)(2,1)} %param.27) | copy-start | bytes 1327108
  10.1 7.5 %copy-start.6 = (bf16[1152,216]{0,1:T(8,128)(2,1)S(1)}, bf16[1152,216]{0,1:T(8,128)(2,1)}, u32[]{:S(2)}) copy-start(bf16[1152,216]{0,1:T(8,128)(2,1)} %param.29) | copy-start | bytes 1492996
  10.1 12.1 %copy-start.10 = (bf16[36,1152]{1,0:T(8,128)(2,1)S(1)}, bf16[36,1152]{1,0:T(8,128)(2,1)}, u32[]{:S(2)}) copy-start(bf16[36,1152]{1,0:T(8,128)(2,1)} %refs_0_.1) | copy-start | bytes 248836
  10.1 12.1 %copy-start.11 = (bf16[36,1152]{1,0:T(8,128)(2,1)S(1)}, bf16[36,1152]{1,0:T(8,128)(2,1)}, u32[]{:S(2)}) copy-start(bf16[36,1152]{1,0:T(8,128)(2,1)} %refs_1_.2) | copy-start | bytes 248836
  10.1 12.1 %copy-start.12 = (bf16[36,1152]{1,0:T(8,128)(2,1)S(1)}, bf16[36,1152]{1,0:T(8,128)(2,1)}, u32[]{:S(2)}) copy-start(bf16[36,1152]{1,0:T(8,128)(2,1)} %refs_2_.2) | copy-start | bytes 248836
  10.1 51.6 %all-to-all-start = ((bf16[32,32,512]{2,1,0:T(8,128)(2,1)}), bf16[32,32,512]{2,1,0:T(8,128)(2,1)S(1)}, u32[]{:S(2)}, u32[]{:S(2)}) async-start(bf16[32,32,512]{2,1,0:T(8,128)(2,1)} %bitcast.31), calls=%async_computation | async-start | bytes 2097152 | tf_op jit(solution)/shard_map/all_to_all | solution.py:41
  18.9 32.1 %collective-permute-start.4 = (bf16[216,1152]{1,0:T(8,128)(2,1)}, bf16[216,1152]{1,0:T(8,128)(2,1)}, u32[]{:S(2)}, u32[]{:S(2)}) collective-permute-start(bf16[216,1152]{1,0:T(8,128)(2,1)} %get-tuple-element.27.refs_5_), channel_id=1, source_target_pairs={{0,16},{16,0},{1,17},{17,1},{2,18},{18,2},{3,19},{19,3},{4,20},{20... | collective-permute-start | bytes 1493000 | tf_op jit(solution)/shard_map/ppermute | solution.py:51
  22.2 26.6 %collective-permute-start.13 = (bf16[36,3456]{1,0:T(8,128)(2,1)S(1)}, bf16[36,3456]{1,0:T(8,128)(2,1)S(1)}, u32[]{:S(2)}, u32[]{:S(2)}) collective-permute-start(bf16[36,3456]{1,0:T(8,128)(2,1)S(1)} %side_weights.1.refs_5_), channel_id=1, source_target_pairs={{0,1},{1,0},{2,3},{3,2},{4,5},{5,4},{6,7},{7,6},{8,9},{9,8},{10,11... | collective-permute-start | bytes 746504 | tf_op jit(solution)/shard_map/ppermute | solution.py:51
  22.9 38.1 %collective-permute-start.3 = (bf16[216,1152]{1,0:T(8,128)(2,1)}, bf16[216,1152]{1,0:T(8,128)(2,1)}, u32[]{:S(2)}, u32[]{:S(2)}) collective-permute-start(bf16[216,1152]{1,0:T(8,128)(2,1)} %get-tuple-element.27.refs_5_), channel_id=1, source_target_pairs={{0,2},{2,0},{1,3},{3,1},{4,6},{6,4},{5,7},{7,5},{8,10},{10,8},{9,1... | collective-permute-start | bytes 1493000 | tf_op jit(solution)/shard_map/ppermute | solution.py:51
  22.9 28.8 %collective-permute-start = (bf16[192,1152]{1,0:T(8,128)(2,1)}, bf16[192,1152]{1,0:T(8,128)(2,1)S(1)}, u32[]{:S(2)}, u32[]{:S(2)}) collective-permute-start(bf16[192,1152]{1,0:T(8,128)(2,1)} %get-tuple-element.26.refs_1_), channel_id=1, source_target_pairs={{0,4},{4,8},{8,12},{12,0},{1,5},{5,9},{9,13},{13,1},{2,6},{6,10},{... | collective-permute-start | bytes 1327112 | tf_op jit(solution)/shard_map/ppermute | solution.py:46
  24.4 27.9 %collective-permute-start.1 = (bf16[192,1152]{1,0:T(8,128)(2,1)}, bf16[192,1152]{1,0:T(8,128)(2,1)}, u32[]{:S(2)}, u32[]{:S(2)}) collective-permute-start(bf16[192,1152]{1,0:T(8,128)(2,1)} %get-tuple-element.26.refs_1_), channel_id=1, source_target_pairs={{0,8},{4,12},{8,0},{12,4},{1,9},{5,13},{9,1},{13,5},{2,10},{6,14},... | collective-permute-start | bytes 1327112 | tf_op jit(solution)/shard_map/ppermute | solution.py:46
  48.9 12.1 %collective-permute-start.2 = (bf16[192,1152]{1,0:T(8,128)(2,1)}, bf16[192,1152]{1,0:T(8,128)(2,1)}, u32[]{:S(2)}, u32[]{:S(2)}) collective-permute-start(bf16[192,1152]{1,0:T(8,128)(2,1)} %get-tuple-element.26.refs_1_), channel_id=1, source_target_pairs={{0,12},{4,0},{8,4},{12,8},{1,13},{5,1},{9,5},{13,9},{2,14},{6,2},{... | collective-permute-start | bytes 1327112 | tf_op jit(solution)/shard_map/ppermute | solution.py:46
  51.0 19.3 %collective-permute-start.5 = (bf16[216,1152]{1,0:T(8,128)(2,1)}, bf16[216,1152]{1,0:T(8,128)(2,1)}, u32[]{:S(2)}, u32[]{:S(2)}) collective-permute-start(bf16[216,1152]{1,0:T(8,128)(2,1)} %collective-permute-done.4.refs_7_), channel_id=1, source_target_pairs={{0,2},{2,0},{1,3},{3,1},{4,6},{6,4},{5,7},{7,5},{8,10},{10,8},{9,1... | collective-permute-start | bytes 1493000 | tf_op jit(solution)/shard_map/ppermute | solution.py:51
  51.7 11.3 %copy-start.30 = (bf16[192,1152]{1,0:T(8,128)(2,1)}, bf16[192,1152]{1,0:T(8,128)(2,1)S(1)}, u32[]{:S(2)}) copy-start(bf16[192,1152]{1,0:T(8,128)(2,1)S(1)} %collective-permute-done.refs_2_) | copy-start | bytes 1327108
  62.9 42.0 %all-to-all-start.1 = ((bf16[32,32,512]{2,1,0:T(8,128)(2,1)}), bf16[32,32,512]{2,1,0:T(8,128)(2,1)S(1)}, u32[]{:S(2)}, u32[]{:S(2)}) async-start(bf16[32,32,512]{2,1,0:T(8,128)(2,1)} %embed_sum.1), calls=%async_computation.1 | async-start | bytes 2097152 | tf_op jit(solution)/shard_map/all_to_all | solution.py:41
  70.2 34.8 %copy-start.14 = (s32[5]{0:T(128)S(1)}, s32[5]{0:T(128)}, u32[]{:S(2)}) copy-start(s32[5]{0:T(128)} %stack.23.refs_0_.at_ref) | copy-start | bytes 64
  70.2 34.8 %copy-start.17 = (bf16[512,320]{0,1:T(8,128)(2,1)S(1)}, bf16[512,320]{0,1:T(8,128)(2,1)}, u32[]{:S(2)}) copy-start(bf16[512,320]{0,1:T(8,128)(2,1)} %param.21) | copy-start | bytes 983044
  70.2 34.8 %copy-start.19 = (f32[512]{0:T(512)S(1)}, f32[512]{0:T(512)}, u32[]{:S(2)}) copy-start(f32[512]{0:T(512)} %param.20) | copy-start | bytes 6148
  70.2 199.1 %all-gather.2.cloned.1.call-start = ((), (), s32[]{:S(2)}) async-start(), calls=%async_computation.7 | async-start | bytes 8460288 | tf_op jit(solution)/shard_map/all_gather | solution.py:576
  75.9 16.7 %collective-permute-start.6 = (bf16[240,768]{1,0:T(8,128)(2,1)}, bf16[240,768]{1,0:T(8,128)(2,1)S(1)}, u32[]{:S(2)}, u32[]{:S(2)}) collective-permute-start(bf16[240,768]{1,0:T(8,128)(2,1)} %get-tuple-element.29), channel_id=1, source_target_pairs={{0,1},{1,0},{16,17},{17,16},{2,3},{3,2},{18,19},{19,18},{4,5},{5,4... | collective-permute-start | bytes 1105928 | tf_op jit(solution)/shard_map/ppermute | solution.py:51
  77.7 24.0 %collective-permute-start.7 = (bf16[240,768]{1,0:T(8,128)(2,1)}, bf16[240,768]{1,0:T(8,128)(2,1)S(1)}, u32[]{:S(2)}, u32[]{:S(2)}) collective-permute-start(bf16[240,768]{1,0:T(8,128)(2,1)} %get-tuple-element.30), channel_id=1, source_target_pairs={{0,16},{1,17},{16,0},{17,1},{2,18},{3,19},{18,2},{19,3},{4,20},{5,... | collective-permute-start | bytes 1105928 | tf_op jit(solution)/shard_map/ppermute | solution.py:51
  80.4 22.0 %collective-permute-start.8 = (bf16[240,768]{1,0:T(8,128)(2,1)}, bf16[240,768]{1,0:T(8,128)(2,1)S(1)}, u32[]{:S(2)}, u32[]{:S(2)}) collective-permute-start(bf16[240,768]{1,0:T(8,128)(2,1)} %get-tuple-element.31), channel_id=1, source_target_pairs={{0,17},{1,16},{16,1},{17,0},{2,19},{3,18},{18,3},{19,2},{4,21},{5,... | collective-permute-start | bytes 1105928 | tf_op jit(solution)/shard_map/ppermute | solution.py:51
  80.6 21.8 %collective-permute-start.9 = (bf16[240,768]{1,0:T(8,128)(2,1)}, bf16[240,768]{1,0:T(8,128)(2,1)S(1)}, u32[]{:S(2)}, u32[]{:S(2)}) collective-permute-start(bf16[240,768]{1,0:T(8,128)(2,1)} %get-tuple-element.28.refs_1_), channel_id=1, source_target_pairs={{0,2},{2,0},{1,3},{3,1},{4,6},{6,4},{5,7},{7,5},{8,10},{10,8},{9,1... | collective-permute-start | bytes 1105928 | tf_op jit(solution)/shard_map/ppermute | solution.py:51
  92.7 11.5 %copy-start.23 = (bf16[240,768]{1,0:T(8,128)(2,1)}, bf16[240,768]{1,0:T(8,128)(2,1)S(1)}, u32[]{:S(2)}) copy-start(bf16[240,768]{1,0:T(8,128)(2,1)S(1)} %collective-permute-done.6.refs_2_) | copy-start | bytes 1105924
  92.7 9.8 %collective-permute-start.10 = (bf16[240,768]{1,0:T(8,128)(2,1)S(1)}, bf16[240,768]{1,0:T(8,128)(2,1)S(1)}, u32[]{:S(2)}, u32[]{:S(2)}) collective-permute-start(bf16[240,768]{1,0:T(8,128)(2,1)S(1)} %collective-permute-done.6.refs_2_), channel_id=1, source_target_pairs={{0,2},{2,0},{1,3},{3,1},{4,6},{6,4},{5,7},{7,5},{8,10},{10,8},{9,1... | collective-permute-start | bytes 1105928 | tf_op jit(solution)/shard_map/ppermute | solution.py:51
  101.7 1.7 collective-permute-start.11
  102.4 1.7 collective-permute-start.12
  109.8 8.6 %copy-start.20 = (f32[8,128]{1,0:T(8,128)}, f32[8,128]{1,0:T(8,128)S(1)}, u32[]{:S(2)}) copy-start(f32[8,128]{1,0:T(8,128)S(1)} %get-tuple-element.32.refs_9_) | copy-start | bytes 12292
  109.8 75.6 %all-to-all-start.2 = ((bf16[8,136,640]{2,1,0:T(8,128)(2,1)}), bf16[8,136,640]{2,1,0:T(8,128)(2,1)S(1)}, u32[]{:S(2)}, u32[]{:S(2)}) async-start(bf16[8,136,640]{2,1,0:T(8,128)(2,1)} %copy-done.5), calls=%async_computation.2 | async-start | bytes 2785280 | tf_op jit(solution)/shard_map/all_to_all | solution.py:41
  188.9 23.9 %copy-start.7 = (bf16[128,1152]{1,0:T(8,128)(2,1)S(1)}, bf16[128,1152]{1,0:T(8,128)(2,1)}, u32[]{:S(2)}) copy-start(bf16[128,1152]{1,0:T(8,128)(2,1)} %refs_2_.3) | copy-start | bytes 884740
  188.9 23.9 %copy-start.16 = (f32[128]{0:T(128)S(1)}, f32[128]{0:T(128)}, u32[]{:S(2)}) copy-start(f32[128]{0:T(128)} %param.24) | copy-start | bytes 1540
  188.9 29.1 %copy-start.33 = (bf16[4,72,192]{2,1,0:T(8,128)(2,1)S(1)}, bf16[4,72,192]{2,1,0:T(8,128)(2,1)}, u32[]{:S(2)}) copy-start(bf16[4,72,192]{2,1,0:T(8,128)(2,1)} %get-tuple-element.34) | copy-start | bytes 331780
  188.9 30.8 %copy-start.32 = (bf16[4,72,192]{2,1,0:T(8,128)(2,1)S(1)}, bf16[4,72,192]{2,1,0:T(8,128)(2,1)}, u32[]{:S(2)}) copy-start(bf16[4,72,192]{2,1,0:T(8,128)(2,1)} %get-tuple-element.35) | copy-start | bytes 331780
  188.9 33.6 %copy-start.31 = (bf16[4,72,192]{2,1,0:T(8,128)(2,1)S(1)}, bf16[4,72,192]{2,1,0:T(8,128)(2,1)}, u32[]{:S(2)}) copy-start(bf16[4,72,192]{2,1,0:T(8,128)(2,1)} %get-tuple-element.36) | copy-start | bytes 331780
  188.9 33.8 %copy-start.22 = (f32[1152]{0:T(1024)S(1)}, f32[1152]{0:T(1024)}, u32[]{:S(2)}) copy-start(f32[1152]{0:T(1024)} %param.26) | copy-start | bytes 13828
  188.9 44.4 %copy-start.9 = (bf16[4,72,192]{2,1,0:T(8,128)(2,1)S(1)}, bf16[4,72,192]{2,1,0:T(8,128)(2,1)}, u32[]{:S(2)}) copy-start(bf16[4,72,192]{2,1,0:T(8,128)(2,1)} %get-tuple-element.33.refs_0_) | copy-start | bytes 331780
  212.7 34.6 %copy-start.8 = (bf16[1152,72]{0,1:T(8,128)(2,1)S(1)}, bf16[1152,72]{0,1:T(8,128)(2,1)}, u32[]{:S(2)}) copy-start(bf16[1152,72]{0,1:T(8,128)(2,1)} %param.32) | copy-start | bytes 497668
  213.9 19.5 %all-to-all-start.4 = ((bf16[32,4,1280]{2,1,0:T(4,128)(2,1)}), bf16[32,4,1280]{2,1,0:T(4,128)(2,1)S(1)}, u32[]{:S(2)}, u32[]{:S(2)}) async-start(bf16[32,4,1280]{2,1,0:T(4,128)(2,1)} %caption_partial.1), calls=%async_computation.4 | async-start | bytes 655360 | tf_op jit(solution)/shard_map/all_to_all | solution.py:41
  218.0 51.4 %copy-start.15 = (s32[5]{0:T(128)S(1)}, s32[5]{0:T(128)}, u32[]{:S(2)}) copy-start(s32[5]{0:T(128)} %stack.23.refs_0_.at_ref) | copy-start | bytes 64
  218.0 9.9 %collective-permute-start.14 = (bf16[4,72,192]{2,1,0:T(8,128)(2,1)S(1)}, bf16[4,72,192]{2,1,0:T(8,128)(2,1)S(1)}, u32[]{:S(2)}, u32[]{:S(2)}) collective-permute-start(bf16[4,72,192]{2,1,0:T(8,128)(2,1)S(1)} %copy-done.33), channel_id=1, source_target_pairs={{0,1},{1,0},{16,17},{17,16},{2,3},{3,2},{18,19},{19,18},{4,5},{5,4... | collective-permute-start | bytes 331784 | tf_op jit(solution)/shard_map/ppermute | solution.py:51
  219.8 12.6 %collective-permute-start.15 = (bf16[4,72,192]{2,1,0:T(8,128)(2,1)S(1)}, bf16[4,72,192]{2,1,0:T(8,128)(2,1)S(1)}, u32[]{:S(2)}, u32[]{:S(2)}) collective-permute-start(bf16[4,72,192]{2,1,0:T(8,128)(2,1)S(1)} %copy-done.32), channel_id=1, source_target_pairs={{0,16},{1,17},{16,0},{17,1},{2,18},{3,19},{18,2},{19,3},{4,20},{5,... | collective-permute-start | bytes 331784 | tf_op jit(solution)/shard_map/ppermute | solution.py:51
  222.5 10.8 %collective-permute-start.16 = (bf16[4,72,192]{2,1,0:T(8,128)(2,1)S(1)}, bf16[4,72,192]{2,1,0:T(8,128)(2,1)S(1)}, u32[]{:S(2)}, u32[]{:S(2)}) collective-permute-start(bf16[4,72,192]{2,1,0:T(8,128)(2,1)S(1)} %copy-done.31), channel_id=1, source_target_pairs={{0,17},{1,16},{16,1},{17,0},{2,19},{3,18},{18,3},{19,2},{4,21},{5,... | collective-permute-start | bytes 331784 | tf_op jit(solution)/shard_map/ppermute | solution.py:51
  248.5 26.3 %all-to-all-start.6 = ((bf16[32,72,128]{2,1,0:T(8,128)(2,1)}), bf16[32,72,128]{2,1,0:T(8,128)(2,1)S(1)}, u32[]{:S(2)}, u32[]{:S(2)}) async-start(bf16[32,72,128]{2,1,0:T(8,128)(2,1)} %text_kv.1), calls=%async_computation.6 | async-start | bytes 1179648 | tf_op jit(solution)/shard_map/all_to_all | solution.py:41
  252.4 13.7 %collective-permute-start.17 = (bf16[4,72,192]{2,1,0:T(8,128)(2,1)S(1)}, bf16[4,72,192]{2,1,0:T(8,128)(2,1)S(1)}, u32[]{:S(2)}, u32[]{:S(2)}) collective-permute-start(bf16[4,72,192]{2,1,0:T(8,128)(2,1)S(1)} %get-tuple-element.38), channel_id=1, source_target_pairs={{0,4},{4,8},{8,12},{12,0},{1,5},{5,9},{9,13},{13,1},{2,6},{6,10},{... | collective-permute-start | bytes 331784 | tf_op jit(solution)/shard_map/ppermute | solution.py:46
  254.1 15.2 %collective-permute-start.18 = (bf16[4,72,192]{2,1,0:T(8,128)(2,1)S(1)}, bf16[4,72,192]{2,1,0:T(8,128)(2,1)S(1)}, u32[]{:S(2)}, u32[]{:S(2)}) collective-permute-start(bf16[4,72,192]{2,1,0:T(8,128)(2,1)S(1)} %get-tuple-element.39), channel_id=1, source_target_pairs={{0,8},{4,12},{8,0},{12,4},{1,9},{5,13},{9,1},{13,5},{2,10},{6,14},... | collective-permute-start | bytes 331784 | tf_op jit(solution)/shard_map/ppermute | solution.py:46
  256.9 12.5 %collective-permute-start.19 = (bf16[4,72,192]{2,1,0:T(8,128)(2,1)S(1)}, bf16[4,72,192]{2,1,0:T(8,128)(2,1)S(1)}, u32[]{:S(2)}, u32[]{:S(2)}) collective-permute-start(bf16[4,72,192]{2,1,0:T(8,128)(2,1)S(1)} %get-tuple-element.40), channel_id=1, source_target_pairs={{0,12},{4,0},{8,4},{12,8},{1,13},{5,1},{9,5},{13,9},{2,14},{6,2},{... | collective-permute-start | bytes 331784 | tf_op jit(solution)/shard_map/ppermute | solution.py:46
  269.3 3.3 %copy-start.1 = (bf16[1152,3456]{1,0:T(8,128)(2,1)S(1)}, bf16[1152,3456]{1,0:T(8,128)(2,1)}, u32[]{:S(2)}) copy-start(bf16[1152,3456]{1,0:T(8,128)(2,1)} %all-gather.2.cloned.1.call-done.refs_4_.refs_5_.wco_ref) | copy-start | bytes 23887876
  (12 other events, 18.0 us)
Sparse Core Ops, SparseCore 0:
  110.0 76.5 all-gather.1
